TPU v7x, 32 devices: a whole 2x2x4 slice. The times are simulated.
32 devices in a mesh: dp: 4 (over y, x), shard: 8 (over z, core).
Axes of the slice: x: 2, y: 2, z: 4, core: 2. Of those that a mesh axis runs over, the one named last changes fastest.
Arguments:
- clip_maps: bfloat16 [128, 32, 2, 1024], P(('dp', 'shard')), may hold values from -6 to 6
- lengths: int32 [128], P(('dp', 'shard')), may hold values from 7 to 31, as said below
- labels: int32 [128, 527], P(('dp', 'shard')), may hold values 0 or 1
- conv1_weight: bfloat16 [9216, 2048], P('shard'), may hold values from -0.0625 to 0.0625
- norm1_gain: float32 [2048], replicated, may hold values from 0.5 to 1.5
- norm1_shift: float32 [2048], replicated, may hold values from -0.5 to 0.5
- conv2_weight: bfloat16 [18432, 2048], P('shard'), may hold values from -0.046875 to 0.046875
- norm2_gain: float32 [2048], replicated, may hold values from 0.5 to 1.5
- norm2_shift: float32 [2048], replicated, may hold values from -0.5 to 0.5
- fc1_weight: bfloat16 [2048, 2048], P('shard'), may hold values from -0.125 to 0.125
- fc1_bias: float32 [2048], replicated, may hold values from -0.5 to 0.5
- fc2_weight: bfloat16 [2048, 527], P('shard'), may hold values from -0.125 to 0.125
- fc2_bias: float32 [527], replicated, may hold values from -1.5 to 0.5
Outputs:
- logits: float32 [128, 527], P(('dp', 'shard'))
- input_grad: float32 [128, 32, 2, 1024], P(('dp', 'shard'))
- conv1_grad: float32 [9216, 2048], P('shard')
- norm1_gain_grad: float32 [2048], replicated
- norm1_shift_grad: float32 [2048], replicated
- conv2_grad: float32 [18432, 2048], P('shard')
- norm2_gain_grad: float32 [2048], replicated
- norm2_shift_grad: float32 [2048], replicated
- fc1_grad: float32 [2048, 2048], P('shard')
- fc1_bias_grad: float32 [2048], replicated
- fc2_grad: float32 [2048, 527], P('shard')
- fc2_bias_grad: float32 [527], replicated
Inputs may be any that keep to these rules, and one draw needn't show every extreme that they name: `lengths`: every clip has 7, 15 or 31 valid frames; both 7 and 31 occur in every draw.
All inputs are finite; a program needn't handle non-finite values. No bound on the sum of `labels` on one device may be relied on, other than what follows from the above.
Results may differ from a plain program's by a relative error of at most 0.018.
Values may be sent and summed in bfloat16 or wider, within the bound.
No kernel may reach another device: no remote copies, remote signals or barrier semaphores. Data moves between devices by JAX's collectives and lax.ppermute only.
A program may use at most 576 MiB of HBM per device.

v0:
```python
import jax
import jax.numpy as jnp
from jax import lax
from jax.sharding import PartitionSpec as P

epsilon = 1e-05


def patch_rows(grid_in):
    clip_count, frame_count, mel_count, chan_count = grid_in.shape
    padded = jnp.pad(grid_in, ((0, 0), (1, 1), (1, 1), (0, 0)))
    tap_list = [
        padded[:, shift_t : shift_t + frame_count, shift_m : shift_m + mel_count, :]
        for shift_t in range(3)
        for shift_m in range(3)
    ]
    stacked = jnp.stack(tap_list, axis=3)
    return stacked.reshape(clip_count * frame_count * mel_count, 9 * chan_count)


def fold_rows(grad_rows, clip_count, frame_count, mel_count):
    chan_count = grad_rows.shape[1] // 9
    tap_terms = grad_rows.reshape(clip_count, frame_count, mel_count, 9, chan_count)
    summed = jnp.zeros((clip_count, frame_count + 2, mel_count + 2, chan_count), jnp.float32)
    for tap_index in range(9):
        shift_t = tap_index // 3
        shift_m = tap_index % 3
        summed = summed + jnp.pad(
            tap_terms[:, :, :, tap_index, :],
            ((0, 0), (shift_t, 2 - shift_t), (shift_m, 2 - shift_m), (0, 0)),
        )
    return summed[:, 1 : frame_count + 1, 1 : mel_count + 1, :]


def normalize(values_in, sum_first, sum_square, pixel_count, gain, shift):
    mean_value = sum_first / pixel_count
    inv_std = lax.rsqrt(sum_square / pixel_count - mean_value * mean_value + epsilon)
    normed = (values_in - mean_value) * inv_std
    return (normed, inv_std, normed * gain + shift)


def silu_slope(values_in):
    sigma = jax.nn.sigmoid(values_in)
    return sigma + values_in * sigma * (1.0 - sigma)


def transpose_dot(left, right):
    return lax.dot_general(
        left, right, (((0,), (0,)), ((), ())), preferred_element_type=jnp.float32
    )


def make_valid(clip_lengths, frame_count, mel_count):
    clip_count = clip_lengths.shape[0]
    frame_ids = lax.broadcasted_iota(jnp.int32, (clip_count, frame_count), 1)
    valid_two = (frame_ids < clip_lengths[:, None]).astype(jnp.float32)
    pixel_valid = jnp.broadcast_to(
        valid_two[:, :, None], (clip_count, frame_count, mel_count)
    ).reshape(-1, 1)
    return (valid_two[:, :, None, None], pixel_valid)


def pool_map(act_grid):
    clip_count, frame_count, mel_count, chans = act_grid.shape
    pooled = jnp.mean(
        act_grid.reshape(clip_count, frame_count // 2, 2, mel_count // 2, 2, chans), axis=(2, 4)
    )
    return jnp.mean(pooled, axis=2)


def pooled_slope(d_pooled, pre_two, pixel_valid, mel_count):
    clip_count, half_frames, chans = d_pooled.shape
    d_frames = jnp.repeat(d_pooled, 2, axis=1)[:, :, None, :] / (2.0 * mel_count)
    d_act_two = jnp.broadcast_to(d_frames, (clip_count, 2 * half_frames, mel_count, chans)).reshape(
        -1, chans
    )
    return d_act_two * pixel_valid * silu_slope(pre_two)


def tag_head(
    pooled, clip_lengths, labels, full_fc1, full_fc2, back_fc1, back_fc2, fc1_bias, fc2_bias
):
    clip_count, half_frames, chans = pooled.shape
    half_ids = lax.broadcasted_iota(jnp.int32, (clip_count, half_frames), 1)
    half_len = clip_lengths // 2
    pooled_valid = (half_ids < half_len[:, None]).astype(jnp.float32)[:, :, None]
    half_float = half_len.astype(jnp.float32)[:, None]
    largest = jnp.max(jnp.where(pooled_valid > 0, pooled, -1e30), axis=1, keepdims=True)
    exp_terms = jnp.exp(pooled - largest) * pooled_valid
    exp_sum = jnp.sum(exp_terms, axis=1)
    log_sum = largest[:, 0, :] + jnp.log(exp_sum)
    mean_time = jnp.sum(pooled * pooled_valid, axis=1) / half_float
    embedding = (log_sum + mean_time).astype(jnp.bfloat16)
    hidden = jnp.dot(embedding, full_fc1, preferred_element_type=jnp.float32) + fc1_bias
    gated_low = jax.nn.silu(hidden).astype(jnp.bfloat16)
    class_logits = jnp.dot(gated_low, full_fc2, preferred_element_type=jnp.float32) + fc2_bias
    d_logits = (jax.nn.sigmoid(class_logits) - labels.astype(jnp.float32)).astype(jnp.bfloat16)
    fc2_term = transpose_dot(gated_low, d_logits)
    fc2_bias_term = jnp.sum(d_logits.astype(jnp.float32), axis=0)
    d_gated = jnp.dot(d_logits, back_fc2.T, preferred_element_type=jnp.float32)
    d_hidden = (d_gated * silu_slope(hidden)).astype(jnp.bfloat16)
    fc1_term = transpose_dot(embedding, d_hidden)
    fc1_bias_term = jnp.sum(d_hidden.astype(jnp.float32), axis=0)
    d_embed = jnp.dot(d_hidden, back_fc1.T, preferred_element_type=jnp.float32)
    soft_weights = exp_terms / exp_sum[:, None, :]
    d_pooled = d_embed[:, None, :] * (soft_weights + pooled_valid / half_float[:, :, None])
    return (class_logits, d_pooled, fc1_term, fc2_term, fc1_bias_term, fc2_bias_term)


def on_device(
    clip_maps,
    lengths,
    labels,
    conv1_weight,
    norm1_gain,
    norm1_shift,
    conv2_weight,
    norm2_gain,
    norm2_shift,
    fc1_weight,
    fc1_bias,
    fc2_weight,
    fc2_bias,
):
    clip_count, frame_count, mel_count, chan_in = clip_maps.shape
    chan_mid = norm1_gain.shape[0]
    valid_four, pixel_valid = make_valid(lengths, frame_count, mel_count)
    masked = clip_maps * valid_four.astype(jnp.bfloat16)
    sent = (conv1_weight, conv2_weight, fc1_weight, fc2_weight)
    gathered = (
        lax.all_gather(sent[0], "shard", axis=0, tiled=True),
        lax.all_gather(sent[1], "shard", axis=0, tiled=True),
        lax.all_gather(sent[2], "shard", axis=0, tiled=True),
        lax.all_gather(sent[3], "shard", axis=0, tiled=True),
    )
    full_one, full_two, full_fc1, full_fc2 = gathered
    patch_one = patch_rows(masked)
    first_out = jnp.dot(patch_one, full_one, preferred_element_type=jnp.float32)
    sum_one, square_one, pixel_count = lax.psum(
        (
            jnp.sum(first_out * pixel_valid, axis=0),
            jnp.sum(first_out * first_out * pixel_valid, axis=0),
            jnp.sum(pixel_valid),
        ),
        ("dp", "shard"),
    )
    normed_one, inv_one, pre_one = normalize(
        first_out, sum_one, square_one, pixel_count, norm1_gain, norm1_shift
    )
    act_one = (jax.nn.silu(pre_one) * pixel_valid).astype(jnp.bfloat16)
    patch_two = patch_rows(act_one.reshape(clip_count, frame_count, mel_count, chan_mid))
    second_out = jnp.dot(patch_two, full_two, preferred_element_type=jnp.float32)
    sum_two, square_two = lax.psum(
        (
            jnp.sum(second_out * pixel_valid, axis=0),
            jnp.sum(second_out * second_out * pixel_valid, axis=0),
        ),
        ("dp", "shard"),
    )
    normed_two, inv_two, pre_two = normalize(
        second_out, sum_two, square_two, pixel_count, norm2_gain, norm2_shift
    )
    act_two = (jax.nn.silu(pre_two) * pixel_valid).reshape(
        clip_count, frame_count, mel_count, chan_mid
    )
    pooled_own = pool_map(act_two)
    back_weights = (
        lax.all_gather(sent[0], "shard", axis=0, tiled=True),
        lax.all_gather(sent[1], "shard", axis=0, tiled=True),
        lax.all_gather(sent[2], "shard", axis=0, tiled=True),
        lax.all_gather(sent[3], "shard", axis=0, tiled=True),
    )
    back_one, back_two, back_fc1, back_fc2 = back_weights
    class_logits, d_pooled, fc1_term, fc2_term, fc1_bias_term, fc2_bias_term = tag_head(
        pooled_own, lengths, labels, full_fc1, full_fc2, back_fc1, back_fc2, fc1_bias, fc2_bias
    )
    dz_two = pooled_slope(d_pooled, pre_two, pixel_valid, mel_count)
    shift_two_grad, gain_two_grad, fc1_bias_grad, fc2_bias_grad = lax.psum(
        (
            jnp.sum(dz_two, axis=0),
            jnp.sum(dz_two * normed_two, axis=0),
            fc1_bias_term,
            fc2_bias_term,
        ),
        ("dp", "shard"),
    )
    d_second = (
        norm2_gain
        * inv_two
        * (dz_two - (shift_two_grad + normed_two * gain_two_grad) / pixel_count)
        * pixel_valid
    ).astype(jnp.bfloat16)
    conv2_part = lax.psum_scatter(
        transpose_dot(patch_two, d_second), "shard", scatter_dimension=0, tiled=True
    )
    d_patch_two = jnp.dot(d_second, back_two.T, preferred_element_type=jnp.float32)
    d_act_one = fold_rows(d_patch_two, clip_count, frame_count, mel_count).reshape(-1, chan_mid)
    dz_one = d_act_one * pixel_valid * silu_slope(pre_one)
    shift_one_grad, gain_one_grad = lax.psum(
        (jnp.sum(dz_one, axis=0), jnp.sum(dz_one * normed_one, axis=0)), ("dp", "shard")
    )
    d_first = (
        norm1_gain
        * inv_one
        * (dz_one - (shift_one_grad + normed_one * gain_one_grad) / pixel_count)
        * pixel_valid
    ).astype(jnp.bfloat16)
    conv1_term = transpose_dot(patch_one, d_first)
    d_patch_one = jnp.dot(d_first, back_one.T, preferred_element_type=jnp.float32)
    input_grad = fold_rows(d_patch_one, clip_count, frame_count, mel_count) * valid_four
    conv1_part, fc1_part, fc2_part = (
        lax.psum_scatter(conv1_term, "shard", scatter_dimension=0, tiled=True),
        lax.psum_scatter(fc1_term, "shard", scatter_dimension=0, tiled=True),
        lax.psum_scatter(fc2_term, "shard", scatter_dimension=0, tiled=True),
    )
    conv1_grad, conv2_grad, fc1_grad, fc2_grad = (
        lax.psum(conv1_part.astype(jnp.bfloat16), "dp").astype(jnp.float32),
        lax.psum(conv2_part.astype(jnp.bfloat16), "dp").astype(jnp.float32),
        lax.psum(fc1_part.astype(jnp.bfloat16), "dp").astype(jnp.float32),
        lax.psum(fc2_part.astype(jnp.bfloat16), "dp").astype(jnp.float32),
    )
    return (
        class_logits,
        input_grad,
        conv1_grad,
        gain_one_grad,
        shift_one_grad,
        conv2_grad,
        gain_two_grad,
        shift_two_grad,
        fc1_grad,
        fc1_bias_grad,
        fc2_grad,
        fc2_bias_grad,
    )


def solution(mesh):
    in_specs = (
        P(("dp", "shard"), None, None, None),
        P(("dp", "shard")),
        P(("dp", "shard"), None),
        P("shard", None),
        P(),
        P(),
        P("shard", None),
        P(),
        P(),
        P("shard", None),
        P(),
        P("shard", None),
        P(),
    )
    out_specs = (
        P(("dp", "shard"), None),
        P(("dp", "shard"), None, None, None),
        P("shard", None),
        P(),
        P(),
        P("shard", None),
        P(),
        P(),
        P("shard", None),
        P(),
        P("shard", None),
        P(),
    )
    return jax.shard_map(
        on_device, mesh=mesh, in_specs=in_specs, out_specs=out_specs, check_vma=False
    )
```

profile of v0, /device:TPU:16, one launch (start us, length us, event | category | flops | bytes accessed | tf_op | source)
XLA Modules:
  0.0 3853.7 jit_solution(11554010571493035099)
XLA Ops:
  24.1 8.5 copy.68
  32.6 7.3 copy.112
  40.0 294.2 %all-gather.5.cloned.1.call-done = bf16[9216,2048]{1,0:T(8,128)(2,1)} async-done(((bf16[1152,2048]{1,0:T(8,128)(2,1)}), bf16[9216,2048]{1,0:T(8,128)(2,1)}) %all-gather.5.cloned.1.call-update) | async-done | bytes 37748752 | tf_op jit(solution)/shard_map/all_gather | solution.py:131
  334.2 22.1 multiply_reduce_fusion.4
  356.3 68.0 %all-reduce.23 = (f32[2048]{0:T(1024)S(1)}, f32[]{:T(128)}, f32[2048]{0:T(1024)S(1)}) all-reduce(f32[2048]{0:T(1024)S(1)} %get-tuple-element.15, f32[]{:T(128)} %broadcast_reduce_fusion, f32[2048]{0:T(1024)S(1)} %get-tuple-element.14), channel_id=1, replica_groups=mesh['dp'=4,'shard'=8] {'dp','shard'}, use_global_device_ids=true, to_apply=%region_1.2 | all-reduce | flops 4097 | bytes 32776 | tf_op jit(solution)/shard_map/psum | solution.py:139
  434.9 21.8 copy.77
  456.8 8.4 copy.113
  465.1 504.6 %all-gather.7.cloned.1.call-done = bf16[18432,2048]{1,0:T(8,128)(2,1)} async-done(((bf16[2304,2048]{1,0:T(8,128)(2,1)}), bf16[18432,2048]{1,0:T(8,128)(2,1)}) %all-gather.7.cloned.1.call-update) | async-done | bytes 75497488 | tf_op jit(solution)/shard_map/all_gather | solution.py:132
  969.8 32.8 multiply_reduce_fusion.2
  1002.6 43.1 %all-reduce.22 = (f32[2048]{0:T(1024)S(1)}, f32[2048]{0:T(1024)S(1)}) all-reduce(f32[2048]{0:T(1024)S(1)} %get-tuple-element.13, f32[2048]{0:T(1024)S(1)} %get-tuple-element.12), channel_id=1, replica_groups=mesh['dp'=4,'shard'=8] {'dp','shard'}, use_global_device_ids=true, to_apply=%region_7.8 | all-reduce | flops 4096 | bytes 32768 | tf_op jit(solution)/shard_map/psum | solution.py:153
  1049.0 3.4 reshape_reshape.3
  1052.5 3.3 reduce_sum.135
  1056.4 4.6 convolution_add_fusion
  1060.9 22.9 all-gather.11.cloned.1.call-done
  1083.8 2.9 convert_reduce_fusion.1
  1086.7 2.8 fusion.48
  1091.6 8.4 fusion.60
  1100.3 5.7 fusion.55
  1109.7 2.5 broadcast_in_dim.18
  1112.2 3.6 reshape.212
  1115.8 4.1 fusion.50
  1120.0 40.7 %all-reduce.21 = (f32[2048]{0:T(1024)S(1)}, f32[2048]{0:T(1024)S(1)}) all-reduce(f32[2048]{0:T(1024)S(1)} %get-tuple-element.19, f32[2048]{0:T(1024)S(1)} %get-tuple-element.18), channel_id=1, replica_groups=mesh['dp'=4,'shard'=8] {'dp','shard'}, use_global_device_ids=true, to_apply=%region_17.18 | all-reduce | flops 4096 | bytes 32768 | tf_op jit(solution)/shard_map/psum | solution.py:178
  1160.7 2.8 multiply_convert_fusion.1
  1163.5 36.6 fusion.56
  1200.1 21.1 reshape.213
  1221.2 52.9 %fusion.53 = (f32[4,32,2,1,2048]{4,3,2,1,0:T(1,128)}, f32[4,32,2,1,2048]{4,3,2,1,0:T(1,128)S(1)}, f32[4,32,2,1,2048]{4,3,2,1,0:T(1,128)S(1)}, f32[4,32,2,1,2048]...) fusion(f32[4,32,2,9,2048]{4,3,2,1,0:T(8,128)} %reshape.213), kind=kLoop, calls=%fused_computation.146 | loop fusion | bytes 37748736 | tf_op jit(solution)/shard_map/slice | solution.py:29
  1280.7 3.2 pad_add_fusion
  1283.9 2.4 copy_bitcast_fusion
  1286.3 2.4 copy_bitcast_fusion.2
  1288.6 7.8 pad_add_fusion.2
  1296.5 3.8 reshape.214
  1300.3 4.1 fusion.49
  1304.4 41.6 %all-reduce.20 = (f32[2048]{0:T(1024)S(1)}, f32[2048]{0:T(1024)S(1)}, f32[2048]{0:T(1024)}, f32[527]{0:T(1024)}) all-reduce(f32[2048]{0:T(1024)S(1)} %get-tuple-element.17, f32[2048]{0:T(1024)S(1)} %get-tuple-element.16, f32[2048]{0:T(1024)S(1)} %get-tuple-element.74, ...), channel_id=1, replica_groups=mesh['dp'=4,'shard'=8] {'dp','shard'}, use_global_device_ids=true, to_apply=%region_21.22 | all-reduce | flops 6671 | bytes 53368 | tf_op jit(solution)/shard_map/psum | solution.py:199
  1346.0 2.8 multiply_convert_fusion
  1348.9 28.5 fusion.58
  1378.5 54.0 %fusion.59 = f32[18432,2048]{1,0:T(8,128)} fusion(bf16[256,18432]{1,0:T(8,128)(2,1)} %bitcast.154, bf16[256,2048]{1,0:T(8,128)(2,1)S(1)} %copy-done.8), kind=kOutput, calls=%fused_computation.152 | convolution fusion | flops 19327352832 | bytes 161480704 | tf_op jit(solution)/shard_map/dot_general | solution.py:48
  1434.5 2.8 convert_element_type.148
  1437.2 657.2 %reduce-scatter.5.cloned.1.call-done = f32[1152,2048]{1,0:T(8,128)} async-done(((f32[9216,2048]{1,0:T(8,128)}), f32[1152,2048]{1,0:T(8,128)}) %reduce-scatter.5.cloned.1.call-update) | async-done | bytes 9437200 | tf_op jit(solution)/shard_map/reduce_scatter | solution.py:212
  2094.4 6.5 convert_element_type.144
  2101.0 1420.9 %reduce-scatter.7.cloned.1.call-done = f32[2304,2048]{1,0:T(8,128)} async-done(((f32[18432,2048]{1,0:T(8,128)}), f32[2304,2048]{1,0:T(8,128)}) %reduce-scatter.7.cloned.1.call-update) | async-done | bytes 18874384 | tf_op jit(solution)/shard_map/reduce_scatter | solution.py:193
  3521.9 11.7 convert_element_type.146
  3533.6 20.3 fusion.57
  3553.9 12.8 reshape.215
  3566.8 27.5 fusion.54
  3600.5 4.3 fusion.20
  3604.8 219.2 %all-reduce.27.cloned.1.call-done = (bf16[1152,2048]{1,0:T(8,128)(2,1)}, bf16[2304,2048]{1,0:T(8,128)(2,1)}, bf16[256,2048]{1,0:T(8,128)(2,1)}, bf16[256,527]{0,1:T(8,128)(2,1)}) async-done(((bf16[1152,2048]{1,0:T(8,128)(2,1)}, bf16[2304,2048]{1,0:T(8,128)(2,1)}, bf16[256,2048]{1,0:T(8,128)(2,1)}, bf16[256,527]{0,1:T(8,128)(2,1)}), (bf16[1152,2048]{1,0:T(8,128)(2,1)}, bf16[2304,2048]{1,0:T(8,128)(2,1)}, ...) | async-done | bytes 15474192 | tf_op jit(solution)/shard_map/psum | solution.py:217
  3824.0 7.3 convert_element_type.145
  3831.3 13.0 convert_element_type.147
  (145 shorter events, 55.8 us)
Async XLA Ops:
  7.2 327.0 %all-gather.5.cloned.1.call-start = ((), (), s32[]{:S(2)}) async-start(), calls=%async_computation.4 | async-start | bytes 42467328 | tf_op jit(solution)/shard_map/all_gather | solution.py:131
  7.9 2.1 copy-start.32
  7.9 3.1 copy-start.9
  7.9 961.8 %all-gather.7.cloned.1.call-start = ((), (), s32[]{:S(2)}) async-start(), calls=%async_computation.5 | async-start | bytes 84934656 | tf_op jit(solution)/shard_map/all_gather | solution.py:132
  8.7 1047.7 %all-gather.9.cloned.1.call-start = ((), (), s32[]{:S(2)}) async-start(), calls=%async_computation.6 | async-start | bytes 9437184 | tf_op jit(solution)/shard_map/all_gather | solution.py:133
  9.4 1074.4 %all-gather.11.cloned.1.call-start = ((), (), s32[]{:S(2)}) async-start(), calls=%async_computation.7 | async-start | bytes 2433024 | tf_op jit(solution)/shard_map/all_gather | solution.py:134
  10.0 1422.7 %reduce-scatter.11.cloned.1.call-start = ((), (), s32[]{:S(2)}) async-start(), calls=%async_computation.11 | async-start | bytes 4866048 | tf_op jit(solution)/shard_map/reduce_scatter | solution.py:214
  10.1 0.7 copy-start.23
  334.2 90.1 %copy-start.17 = (f32[2048]{0:T(1024)S(1)}, f32[2048]{0:T(1024)}, u32[]{:S(2)}) copy-start(f32[2048]{0:T(1024)} %param.17) | copy-start | bytes 24580
  334.2 92.6 %copy-start.20 = (f32[2048]{0:T(1024)S(1)}, f32[2048]{0:T(1024)}, u32[]{:S(2)}) copy-start(f32[2048]{0:T(1024)} %param.18) | copy-start | bytes 24580
  356.3 72.7 %copy-start = (f32[256,2048]{1,0:T(8,128)}, f32[256,2048]{1,0:T(8,128)S(1)}, u32[]{:S(2)}) copy-start(f32[256,2048]{1,0:T(8,128)S(1)} %get-tuple-element.71) | copy-start | bytes 6291460
  425.5 0.7 copy-start.12
  426.2 0.6 copy-start.14
  432.6 1.2 copy-start.6
  969.8 76.0 %copy-start.16 = (f32[2048]{0:T(1024)S(1)}, f32[2048]{0:T(1024)}, u32[]{:S(2)}) copy-start(f32[2048]{0:T(1024)} %param.20) | copy-start | bytes 24580
  969.8 77.2 %copy-start.19 = (f32[2048]{0:T(1024)S(1)}, f32[2048]{0:T(1024)}, u32[]{:S(2)}) copy-start(f32[2048]{0:T(1024)} %param.21) | copy-start | bytes 24580
  1052.5 3.9 copy-start.26
  1056.3 27.5 copy-start.25
  1056.3 27.5 copy-start.31
  1089.5 344.9 %reduce-scatter.9.cloned.1.call-start = ((), (), s32[]{:S(2)}) async-start(), calls=%async_computation.10 | async-start | bytes 18874368 | tf_op jit(solution)/shard_map/reduce_scatter | solution.py:213
  1100.0 994.4 %reduce-scatter.5.cloned.1.call-start = ((), (), s32[]{:S(2)}) async-start(), calls=%async_computation.8 | async-start | bytes 84934656 | tf_op jit(solution)/shard_map/reduce_scatter | solution.py:212
  1160.7 2.8 copy-start.27
  1160.7 2.8 copy-start.28
  1163.5 36.6 copy-start.7
  1274.0 1.6 copy-start.4
  1274.0 2.2 copy-start.5
  1276.3 2.2 copy-start.2
  1276.3 2.2 copy-start.3
  1296.4 3.8 copy-start.1
  1296.4 3.8 copy-start.13
  1296.4 3.8 copy-start.15
  1296.4 3.8 copy-start.18
  1296.4 3.8 copy-start.21
  1300.3 45.7 %copy-start.22 = (f32[2048]{0:T(1024)S(1)}, f32[2048]{0:T(1024)}, u32[]{:S(2)}) copy-start(f32[2048]{0:T(1024)} %get-tuple-element.37) | copy-start | bytes 24580
  1346.0 2.8 copy-start.29
  1346.0 2.8 copy-start.30
  1377.3 1.2 copy-start.8
  1377.3 2144.6 %reduce-scatter.7.cloned.1.call-start = ((), (), s32[]{:S(2)}) async-start(), calls=%async_computation.9 | async-start | bytes 169869312 | tf_op jit(solution)/shard_map/reduce_scatter | solution.py:193
  1432.6 2391.4 %all-reduce.27.cloned.1.call-start = ((), (), s32[]{:S(2)}) async-start(), calls=%async_computation.12 | async-start | bytes 30949376 | tf_op jit(solution)/shard_map/psum | solution.py:217
  3599.2 1.3 copy-start.24
  3831.3 13.0 copy-start.10
  3844.3 1.6 copy-start.11
Sparse Core Ops, SparseCore 0:
  9.7 324.4 all-gather.4
  335.9 633.8 all-gather.6
  971.4 81.5 all-gather.8
  1054.4 29.4 all-gather.10
  1089.6 49.7 reduce-scatter.10
  1141.7 166.6 reduce-scatter.8
  1377.5 716.9 reduce-scatter.4
  2096.8 1425.0 reduce-scatter.6
  3533.7 290.1 all-reduce.26
where the time goes:
time: 3870 us; the launch traced here: 3850 us
  waiting for transfers between devices  3120 us (81%)
  matrix products  221 us (6%)
  local copies, waits for them, and re-layouts  214 us (6%)
  blocking collectives  193 us (5%)
  other arithmetic  88.7 us (2%)
    reduce_scatter x1, waiting for transfers between devices, on_device(): lax.psum_scatter(transpose_dot(patch_two, d_second), 'shard', scatter_dim...  1420 us
    reduce_scatter x1, waiting for transfers between devices, on_device(): lax.psum_scatter(conv1_term, 'shard', scatter_dimension=0, tiled=True)  657 us
    all_gather x1, waiting for transfers between devices, on_device(): lax.all_gather(sent[1], 'shard', axis=0, tiled=True)  505 us
    all_gather x1, waiting for transfers between devices, on_device(): lax.all_gather(sent[0], 'shard', axis=0, tiled=True)  294 us
    psum x1, waiting for transfers between devices, on_device(): lax.psum(conv1_part.astype(jnp.bfloat16), 'dp').astype(jnp.float32)  219 us
    dot_general x4, matrix products, transpose_dot(): lax.dot_general(left, right, (((0,), (0,)), ((), ())), preferred_element_...  93.6 us
    slice x2, local copies, waits for them, and re-layouts, fold_rows(): tap_terms[:, :, :, tap_index, :]  80.3 us
  transfers between devices with their start and end apart: 9, of which 6 were waited for; matrix products, arithmetic and copies ran while one was open for 12% of the time, Pallas kernels for 0%

commit v1 on v0

--- a/solution.py
+++ b/solution.py
@@ -4,6 +4,348 @@
 from jax.sharding import PartitionSpec as P
 
 epsilon = 1e-05
+row_chunks = 4
+bf16 = jnp.bfloat16
+f32 = jnp.float32
+
+
+def roll_to(stacked, start, axis):
+    size = stacked.shape[axis]
+    doubled = jnp.concatenate([stacked, stacked], axis=axis)
+    return lax.dynamic_slice_in_dim(doubled, start, size, axis=axis)
+
+
+def receive_from(value, axis, size, step):
+    if step % size == 0:
+        return value
+    return lax.ppermute(value, axis, [(i, (i - step) % size) for i in range(size)])
+
+
+def send_to(value, axis, size, step):
+    return lax.ppermute(value, axis, [(i, (i + step) % size) for i in range(size)])
+
+
+def gather_relative(value, axis, size):
+    return [receive_from(value, axis, size, step) for step in range(size)]
+
+
+def scatter_sum(terms, axis, size):
+    total = terms[0].astype(f32)
+    for step in range(1, size):
+        total = total + send_to(terms[step].astype(bf16), axis, size, step).astype(f32)
+    return total
+
+
+def exchange(chunks, axis, size, me):
+    parts = []
+    for step in range(size):
+        chunk = lax.dynamic_index_in_dim(chunks, (me - step + size) % size, 0, keepdims=False)
+        parts.append(receive_from(chunk, axis, size, step))
+    return roll_to(jnp.stack(parts), (size - me) % size, 0)
+
+
+def shifted(rows):
+    zero = jnp.zeros((1, rows.shape[1]), rows.dtype)
+    return jnp.concatenate(
+        [
+            jnp.concatenate([zero, rows[:-1]], axis=0),
+            rows,
+            jnp.concatenate([rows[1:], zero], axis=0),
+        ],
+        axis=1,
+    )
+
+
+def mel_taps(taps):
+    grid = taps.reshape((3, 3) + taps.shape[1:])
+    first = jnp.stack([grid[:, 1], grid[:, 0]], axis=2)
+    second = jnp.stack([grid[:, 2], grid[:, 1]], axis=2)
+    return jnp.stack([first, second], axis=1)
+
+
+def fold_mel_taps(wide):
+    grid = jnp.stack(
+        [
+            wide[:, 0, :, 1],
+            wide[:, 0, :, 0] + wide[:, 1, :, 1],
+            wide[:, 1, :, 0],
+        ],
+        axis=1,
+    )
+    return grid.reshape((9,) + grid.shape[2:])
+
+
+def dot(left, right):
+    return jnp.dot(left, right, preferred_element_type=f32)
+
+
+def transpose_dot(left, right):
+    return lax.dot_general(left, right, (((0,), (0,)), ((), ())), preferred_element_type=f32)
+
+
+def dot_transpose(left, right):
+    return lax.dot_general(left, right, (((1,), (1,)), ((), ())), preferred_element_type=f32)
+
+
+def silu_slope(values_in):
+    sigma = jax.nn.sigmoid(values_in)
+    return sigma + values_in * sigma * (1.0 - sigma)
+
+
+def both_mels(sums):
+    half = sums.shape[0] // 2
+    total = sums[:half] + sums[half:]
+    return total, jnp.concatenate([total, total])
+
+
+def norm_of(values_in, valid, pixel_count):
+    _, sum_first = both_mels(jnp.sum(values_in * valid, axis=0))
+    _, sum_square = both_mels(jnp.sum(values_in * values_in * valid, axis=0))
+    mean_value = sum_first / pixel_count
+    inv_std = lax.rsqrt(sum_square / pixel_count - mean_value * mean_value + epsilon)
+    return (values_in - mean_value) * inv_std, inv_std
+
+
+def make_device(dp, shard):
+    everyone = ("dp", "shard")
+
+    def in_order(gathered):
+        split = gathered.reshape((dp, shard) + gathered.shape[1:])
+        return jnp.swapaxes(split, 0, 1)
+
+    def weight_in(weight, d, s):
+        rows, columns = weight.shape
+        part = rows // (9 * dp)
+        own = lax.dynamic_index_in_dim(weight.reshape(9, dp, part, columns), d, 1, keepdims=False)
+        chunks = own.reshape(9, part, shard, columns // shard)
+        chunks = jnp.moveaxis(chunks, 2, 0)
+        return exchange(chunks, "shard", shard, s).reshape(9, shard, part, columns // shard)
+
+    def weight_out(grad, d, s):
+        _, _, part, columns = grad.shape
+        chunks = grad.astype(bf16).reshape(shard, 9, part, columns)
+        parts = exchange(chunks, "shard", shard, s)
+        own = jnp.moveaxis(parts, 0, 2).reshape(9, part, shard * columns)
+        groups = roll_to(jnp.stack(gather_relative(own, "dp", dp)), (dp - d) % dp, 0)
+        return jnp.moveaxis(groups, 0, 1).reshape(9 * dp * part, shard * columns).astype(f32)
+
+    def on_device(
+        clip_maps,
+        lengths,
+        labels,
+        conv1_weight,
+        norm1_gain,
+        norm1_shift,
+        conv2_weight,
+        norm2_gain,
+        norm2_shift,
+        fc1_weight,
+        fc1_bias,
+        fc2_weight,
+        fc2_bias,
+    ):
+        d, s = lax.axis_index("dp"), lax.axis_index("shard")
+        clip_count, frames, mels, chan_in = clip_maps.shape
+        chan_mid = norm1_gain.shape[0]
+        clips = clip_count * dp * shard
+        rows = clips * frames
+        lane = chan_mid // (dp * shard)
+        lane_in = chan_in // (dp * shard)
+        wide = mels * lane
+
+        all_lengths = in_order(lax.all_gather(lengths, everyone)).reshape(clips)
+        all_labels = in_order(lax.all_gather(labels, everyone)).reshape(clips, labels.shape[1])
+        frame_ids = lax.broadcasted_iota(jnp.int32, (clips, frames), 1)
+        valid = (frame_ids < all_lengths[:, None]).astype(f32).reshape(rows, 1)
+        pixel_count = (jnp.sum(all_lengths) * mels).astype(f32)
+
+        own_frames = lax.broadcasted_iota(jnp.int32, (clip_count, frames), 1)
+        own_valid = (own_frames < lengths[:, None])[:, :, None, None]
+
+        masked = clip_maps * own_valid.astype(bf16)
+        split = masked.reshape(clip_count, frames, mels, shard, dp, lane_in)
+        chunks = jnp.moveaxis(split, 4, 0).reshape(dp, clip_count * frames, mels * shard * lane_in)
+        group = exchange(chunks, "dp", dp, d).reshape(dp * clip_count * frames, mels * shard * lane_in)
+        maps_in = roll_to(
+            jnp.stack(gather_relative(group, "shard", shard)), (shard - s) % shard, 0
+        ).reshape(rows, mels * shard * lane_in)
+
+        taps_one = weight_in(conv1_weight, d, s).reshape(9, shard * lane_in, dp, lane)
+        taps_one = roll_to(taps_one, d, 2)
+        wide_one = mel_taps(taps_one)
+        wide_one = jnp.moveaxis(wide_one, 3, 4).reshape(3 * mels * shard * lane_in, dp * wide)
+
+        taps_two = weight_in(conv2_weight, d, s)
+        taps_two = roll_to(roll_to(taps_two, s, 1).reshape(9, shard * lane, dp, lane), d, 2)
+        wide_two = mel_taps(taps_two).reshape(3, mels, shard, lane, mels, dp, lane)
+        wide_two = wide_two.transpose(0, 2, 1, 3, 5, 4, 6).reshape(3 * shard * wide, dp * wide)
+
+        full_fc1 = lax.all_gather(fc1_weight, "shard", axis=0, tiled=True)
+        full_fc2 = lax.all_gather(fc2_weight, "shard", axis=0, tiled=True)
+
+        own_start = (s * dp + d) * lane
+
+        def own_channels(vector):
+            own = lax.dynamic_slice_in_dim(vector, own_start, lane)
+            return jnp.concatenate([own] * mels)
+
+        gain_one, shift_one = own_channels(norm1_gain), own_channels(norm1_shift)
+        gain_two, shift_two = own_channels(norm2_gain), own_channels(norm2_shift)
+
+        step = rows // row_chunks
+        cuts = [slice(i * step, (i + 1) * step) for i in range(row_chunks)]
+
+        def scatter_dp(out):
+            return scatter_sum(
+                [out[:, k * wide : (k + 1) * wide] for k in range(dp)], "dp", dp
+            )
+
+        first_out = jnp.concatenate(
+            [scatter_dp(dot(shifted(maps_in[cut]), wide_one)) for cut in cuts], axis=0
+        )
+        normed_one, inv_one = norm_of(first_out, valid, pixel_count)
+        pre_one = normed_one * gain_one + shift_one
+        act_one = (jax.nn.silu(pre_one) * valid).astype(bf16)
+
+        second_parts, act_parts = [], []
+        for cut in cuts:
+            act_part = jnp.concatenate(gather_relative(act_one[cut], "shard", shard), axis=1)
+            act_parts.append(act_part)
+            second_parts.append(scatter_dp(dot(shifted(act_part), wide_two)))
+        second_out = jnp.concatenate(second_parts, axis=0)
+        normed_two, inv_two = norm_of(second_out, valid, pixel_count)
+        pre_two = normed_two * gain_two + shift_two
+        act_two = jax.nn.silu(pre_two) * valid
+
+        halves = frames // 2
+        pooled = jnp.sum(act_two.reshape(clips, halves, 2, wide), axis=2)
+        pooled = (pooled[:, :, :lane] + pooled[:, :, lane:]) / (2.0 * mels)
+        half_len = all_lengths // 2
+        half_ids = lax.broadcasted_iota(jnp.int32, (clips, halves), 1)
+        pooled_valid = (half_ids < half_len[:, None]).astype(f32)[:, :, None]
+        half_float = half_len.astype(f32)[:, None]
+        largest = jnp.max(jnp.where(pooled_valid > 0, pooled, -1e30), axis=1, keepdims=True)
+        exp_terms = jnp.exp(pooled - largest) * pooled_valid
+        exp_sum = jnp.sum(exp_terms, axis=1)
+        log_sum = largest[:, 0, :] + jnp.log(exp_sum)
+        mean_time = jnp.sum(pooled * pooled_valid, axis=1) / half_float
+        own_embedding = (log_sum + mean_time).astype(bf16)
+        embedding = in_order(lax.all_gather(own_embedding, everyone))
+        embedding = jnp.moveaxis(embedding, 2, 0).reshape(clips, chan_mid)
+        hidden = dot(embedding, full_fc1) + fc1_bias
+        gated = jax.nn.silu(hidden).astype(bf16)
+        logits = dot(gated, full_fc2) + fc2_bias
+        d_logits = (jax.nn.sigmoid(logits) - all_labels.astype(f32)).astype(bf16)
+        d_gated = dot_transpose(d_logits, full_fc2)
+        d_hidden = (d_gated * silu_slope(hidden)).astype(bf16)
+        own_fc1 = lax.dynamic_slice_in_dim(fc1_weight, d * lane, lane, axis=0)
+        d_embed = dot_transpose(d_hidden, own_fc1)
+        soft = exp_terms / exp_sum[:, None, :]
+        d_pooled = d_embed[:, None, :] * (soft + pooled_valid / half_float[:, :, None])
+
+        fc_rows = shard_rows = fc1_weight.shape[0]
+        fc1_grad = transpose_dot(
+            lax.dynamic_slice_in_dim(embedding, s * fc_rows, fc_rows, axis=1), d_hidden
+        )
+        fc2_rows = fc2_weight.shape[0]
+        fc2_grad = transpose_dot(
+            lax.dynamic_slice_in_dim(gated, s * fc2_rows, fc2_rows, axis=1), d_logits
+        )
+        fc1_bias_grad = jnp.sum(d_hidden.astype(f32), axis=0)
+        fc2_bias_grad = jnp.sum(d_logits.astype(f32), axis=0)
+        own_logits = lax.dynamic_slice_in_dim(logits, (s * dp + d) * clip_count, clip_count, axis=0)
+
+        d_frames = jnp.concatenate([d_pooled, d_pooled], axis=2) / (2.0 * mels)
+        d_frames = jnp.broadcast_to(d_frames[:, :, None, :], (clips, halves, 2, wide))
+        dz_two = d_frames.reshape(rows, wide) * valid * silu_slope(pre_two)
+        shift_two_grad, shift_two_lanes = both_mels(jnp.sum(dz_two, axis=0))
+        gain_two_grad, gain_two_lanes = both_mels(jnp.sum(dz_two * normed_two, axis=0))
+        d_second = (
+            gain_two
+            * inv_two
+            * (dz_two - (shift_two_lanes + normed_two * gain_two_lanes) / pixel_count)
+            * valid
+        ).astype(bf16)
+
+        back_two = wide_two.reshape(3, shard * wide, dp * wide)[::-1]
+        back_two = jnp.swapaxes(back_two, 1, 2).reshape(3 * dp * wide, shard * wide)
+        d_act_parts, d_second_parts = [], []
+        for cut in cuts:
+            part = jnp.concatenate(gather_relative(d_second[cut], "dp", dp), axis=1)
+            d_second_parts.append(part)
+            out = dot(shifted(part), back_two)
+            d_act_parts.append(
+                scatter_sum(
+                    [out[:, k * wide : (k + 1) * wide] for k in range(shard)], "shard", shard
+                )
+            )
+        d_act_one = jnp.concatenate(d_act_parts, axis=0)
+        act_all = jnp.concatenate(act_parts, axis=0)
+        grad_two = transpose_dot(shifted(act_all), jnp.concatenate(d_second_parts, axis=0))
+        grad_two = grad_two.reshape(3, shard, mels, lane, dp, mels, lane)
+        grad_two = grad_two.transpose(0, 2, 1, 3, 5, 4, 6).reshape(
+            3, mels, shard * lane, mels, dp * lane
+        )
+        grad_two = fold_mel_taps(grad_two).reshape(9, shard, lane, dp, lane)
+        grad_two = roll_to(roll_to(grad_two, (shard - s) % shard, 1), (dp - d) % dp, 3)
+        conv2_grad = weight_out(grad_two.reshape(9, shard, lane, dp * lane), d, s)
+
+        dz_one = d_act_one * valid * silu_slope(pre_one)
+        shift_one_grad, shift_one_lanes = both_mels(jnp.sum(dz_one, axis=0))
+        gain_one_grad, gain_one_lanes = both_mels(jnp.sum(dz_one * normed_one, axis=0))
+        d_first = (
+            gain_one
+            * inv_one
+            * (dz_one - (shift_one_lanes + normed_one * gain_one_lanes) / pixel_count)
+            * valid
+        ).astype(bf16)
+
+        back_one = wide_one.reshape(3, mels * shard * lane_in, dp * wide)[::-1]
+        back_one = jnp.swapaxes(back_one, 1, 2).reshape(3 * dp * wide, mels * shard * lane_in)
+        d_first_all = jnp.concatenate(
+            [jnp.concatenate(gather_relative(d_first[cut], "dp", dp), axis=1) for cut in cuts], axis=0
+        )
+        d_in = dot(shifted(d_first_all), back_one).astype(bf16)
+        d_in = d_in.reshape(shard, rows // shard, mels * shard * lane_in)
+        d_in = scatter_sum(
+            [
+                lax.dynamic_index_in_dim(d_in, (s + k) % shard, 0, keepdims=False)
+                for k in range(shard)
+            ],
+            "shard",
+            shard,
+        ).astype(bf16)
+        d_in = exchange(d_in.reshape(dp, rows // (shard * dp), mels * shard * lane_in), "dp", dp, d)
+        d_in = d_in.reshape(dp, clip_count, frames, mels, shard, lane_in)
+        input_grad = jnp.moveaxis(d_in, 0, 4).reshape(clip_maps.shape).astype(f32)
+        input_grad = input_grad * own_valid.astype(f32)
+
+        grad_one = transpose_dot(shifted(maps_in), d_first_all)
+        grad_one = grad_one.reshape(3, mels, shard * lane_in, dp, mels, lane)
+        grad_one = jnp.moveaxis(grad_one, 4, 3).reshape(3, mels, shard * lane_in, mels, dp * lane)
+        grad_one = fold_mel_taps(grad_one).reshape(9, shard, lane_in, dp, lane)
+        grad_one = roll_to(grad_one, (dp - d) % dp, 3)
+        conv1_grad = weight_out(grad_one.reshape(9, shard, lane_in, dp * lane), d, s)
+
+        norm_grads = jnp.stack([gain_one_grad, shift_one_grad, gain_two_grad, shift_two_grad])
+        norm_grads = in_order(lax.all_gather(norm_grads, everyone))
+        norm_grads = jnp.moveaxis(norm_grads, 2, 0).reshape(4, chan_mid)
+        return (
+            own_logits,
+            input_grad,
+            conv1_grad,
+            norm_grads[0],
+            norm_grads[1],
+            conv2_grad,
+            norm_grads[2],
+            norm_grads[3],
+            fc1_grad,
+            fc1_bias_grad,
+            fc2_grad,
+            fc2_bias_grad,
+        )
+
+    return on_device
 
 
 def patch_rows(grid_in):
@@ -37,17 +379,6 @@
     inv_std = lax.rsqrt(sum_square / pixel_count - mean_value * mean_value + epsilon)
     normed = (values_in - mean_value) * inv_std
     return (normed, inv_std, normed * gain + shift)
-
-
-def silu_slope(values_in):
-    sigma = jax.nn.sigmoid(values_in)
-    return sigma + values_in * sigma * (1.0 - sigma)
-
-
-def transpose_dot(left, right):
-    return lax.dot_general(
-        left, right, (((0,), (0,)), ((), ())), preferred_element_type=jnp.float32
-    )
 
 
 def make_valid(clip_lengths, frame_count, mel_count):
@@ -236,10 +567,11 @@
 
 
 def solution(mesh):
+    both = ("dp", "shard")
     in_specs = (
-        P(("dp", "shard"), None, None, None),
-        P(("dp", "shard")),
-        P(("dp", "shard"), None),
+        P(both, None, None, None),
+        P(both),
+        P(both, None),
         P("shard", None),
         P(),
         P(),
@@ -252,19 +584,21 @@
         P(),
     )
     out_specs = (
-        P(("dp", "shard"), None),
-        P(("dp", "shard"), None, None, None),
-        P("shard", None),
-        P(),
-        P(),
-        P("shard", None),
-        P(),
-        P(),
-        P("shard", None),
-        P(),
-        P("shard", None),
-        P(),
-    )
+        P(both, None),
+        P(both, None, None, None),
+        P("shard", None),
+        P(),
+        P(),
+        P("shard", None),
+        P(),
+        P(),
+        P("shard", None),
+        P(),
+        P("shard", None),
+        P(),
+    )
+    dp, shard = mesh.shape["dp"], mesh.shape["shard"]
+    step = make_device(dp, shard) if shard <= 8 else on_device
     return jax.shard_map(
-        on_device, mesh=mesh, in_specs=in_specs, out_specs=out_specs, check_vma=False
-    )
+        step, mesh=mesh, in_specs=in_specs, out_specs=out_specs, check_vma=False
+    )

time: 3870 us -> 1820 us (0.47)
  waiting for transfers between devices: 3120 us -> 470 us
  starting transfers between devices: 0.57 us -> 382 us
  local copies, waits for them, and re-layouts: 214 us -> 458 us
  matrix products: 221 us -> 166 us
  other arithmetic: 88.7 us -> 139 us
    reduce_scatter x4 -> x0, waiting for transfers between devices: 2080 us -> none  [the longest x1 1420 us: on_device(): lax.psum_scatter(transpose_dot(patch_two, d_second), 'shard', scatter_dim...]
    all_gather x4 -> x2, waiting for transfers between devices: 822 us -> 0.01 us  [the longest x1 0.01 us: on_device(): full_fc1 = lax.all_gather(fc1_weight, 'shard', axis=0, tiled=True)]
    ppermute x0 -> x158, waiting for transfers between devices: none -> 469 us  [the longest x99 353 us: receive_from(): lax.ppermute(value, axis, [(i, (i - step) % size) for i in range(size)])]
    ppermute x0 -> x158, starting transfers between devices: none -> 382 us  [the longest x99 201 us: receive_from(): lax.ppermute(value, axis, [(i, (i - step) % size) for i in range(size)])]
    psum x1 -> x0, waiting for transfers between devices: 219 us -> none  [on_device(): lax.psum(conv1_part.astype(jnp.bfloat16), 'dp').astype(jnp.float32)]
    psum x4 -> x0, blocking collectives: 193 us -> none  [the longest x1 68 us: on_device(): lax.psum((jnp.sum(first_out * pixel_valid, axis=0), jnp.sum(first_out * f...]
    unnamed x93 -> x456, local copies, waits for them, and re-layouts: 37 us -> 166 us
    all_gather x0 -> x3, blocking collectives: none -> 129 us  [the longest x1 53.3 us: on_device(): norm_grads = in_order(lax.all_gather(norm_grads, everyone))]
  transfers between devices with their start and end apart: 9 -> 160, of which waited for: 6 -> 62; matrix products, arithmetic and copies ran while one was open for 12% -> 27% of each run, Pallas kernels for 0% -> 0%
where the time goes in v1:
time: 1820 us; the launch traced here: 1810 us
  waiting for transfers between devices  470 us (26%)
  local copies, waits for them, and re-layouts  458 us (25%)
  starting transfers between devices  382 us (21%)
  blocking collectives  174 us (10%)
  matrix products  166 us (9%)
  other arithmetic  139 us (8%)
  between operations  18.6 us (1%)
    ppermute x99, waiting for transfers between devices, receive_from(): lax.ppermute(value, axis, [(i, (i - step) % size) for i in range(size)])  353 us
    ppermute x99, starting transfers between devices, receive_from(): lax.ppermute(value, axis, [(i, (i - step) % size) for i in range(size)])  201 us
    ppermute x59, starting transfers between devices, send_to(): lax.ppermute(value, axis, [(i, (i + step) % size) for i in range(size)])  181 us
    unnamed x456, local copies, waits for them, and re-layouts  166 us
    ppermute x59, waiting for transfers between devices, send_to(): lax.ppermute(value, axis, [(i, (i + step) % size) for i in range(size)])  116 us
    dot_general x15, matrix products, dot(): return jnp.dot(left, right, preferred_element_type=f32)  97.9 us
    dot_general x4, matrix products, transpose_dot(): lax.dot_general(left, right, (((0,), (0,)), ((), ())), preferred_element_...  64.9 us
    all_gather x1, blocking collectives, on_device(): norm_grads = in_order(lax.all_gather(norm_grads, everyone))  53.3 us
  transfers between devices with their start and end apart: 160, of which 62 were waited for; matrix products, arithmetic and copies ran while one was open for 27% of the time, Pallas kernels for 0%

profile of v1, /device:TPU:16, one launch (start us, length us, event | category | flops | bytes accessed | tf_op | source)
XLA Modules:
  0.0 1807.6 jit_solution(3254151121308517082)
XLA Ops:
  28.7 45.7 %all-reduce.30 = s32[128]{0:T(128)S(1)} all-reduce(s32[128]{0:T(128)S(1)} %dynamic-update-slice), channel_id=2, replica_groups=mesh['dp'=4,'shard'=8] {'dp','shard'}, use_global_device_ids=true, to_apply=%add.30 | all-reduce | flops 128 | bytes 1024
  78.8 6.8 constant_dynamic-slice_fusion.5
  88.7 40.3 %all-gather.3 = s32[32,4,527]{2,1,0:T(4,128)S(1)} all-gather(s32[1,4,527]{2,1,0:T(4,128)S(1)} %bitcast.519), channel_id=3, replica_groups=mesh['dp'=4,'shard'=8] {'dp','shard'}, dimensions={0}, use_global_device_ids=true | all-gather | bytes 278256 | tf_op jit(solution)/shard_map/all_gather | solution.py:157
  214.5 14.8 collective-permute-done.38
  239.2 31.3 %collective-permute-done.41 = bf16[9,64,256]{2,1,0:T(8,128)(2,1)S(1)} collective-permute-done((bf16[9,64,256]{2,1,0:T(8,128)(2,1)S(1)}, bf16[9,64,256]{2,1,0:T(8,128)(2,1)S(1)}, u32[]{:S(2)}, u32[]{:S(2)}) %collective-permute-start.41) | collective-permute-done | bytes 294944 | tf_op jit(solution)/shard_map/ppermute | solution.py:21
  309.5 17.7 copy.247
  327.2 14.3 reshape_reshape.16
  343.6 14.3 reshape.800
  374.7 6.9 collective-permute-done.9
  472.3 24.6 %collective-permute-done.31 = bf16[1024,128]{1,0:T(8,128)(2,1)S(1)} collective-permute-done((bf16[1024,128]{1,0:T(8,128)(2,1)S(1)}, bf16[1024,128]{1,0:T(8,128)(2,1)S(1)}, u32[]{:S(2)}, u32[]{:S(2)}) %collective-permute-start.31) | collective-permute-done | bytes 262176 | tf_op jit(solution)/shard_map/ppermute | solution.py:21
  522.9 21.2 %collective-permute-done.67 = bf16[1024,128]{1,0:T(8,128)(2,1)S(1)} collective-permute-done((bf16[1024,128]{1,0:T(8,128)(2,1)S(1)}, bf16[1024,128]{1,0:T(8,128)(2,1)S(1)}, u32[]{:S(2)}, u32[]{:S(2)}) %collective-permute-start.67) | collective-permute-done | bytes 262176 | tf_op jit(solution)/shard_map/ppermute | solution.py:21
  555.7 16.0 collective-permute-done.71
  572.2 16.9 collective-permute-done.57
  600.8 15.9 collective-permute-done.61
  617.2 16.9 collective-permute-done.47
  665.7 7.7 fusion.313
  681.0 6.7 fusion.275
  727.4 34.9 %all_gather.30 = bf16[32,128,64]{1,2,0:T(8,128)(2,1)S(1)} all-gather(bf16[1,128,64]{1,2,0:T(8,128)(2,1)S(1)} %copy.250), channel_id=1, replica_groups=mesh['dp'=4,'shard'=8] {'dp','shard'}, dimensions={0}, use_global_device_ids=true | all-gather | bytes 540672 | tf_op jit(solution)/shard_map/all_gather | solution.py:233
  836.0 16.0 fusion.363
  852.0 43.2 %fusion.3 = f32[3072,512]{1,0:T(8,128)} fusion(bf16[4095,1024]{1,0:T(8,128)(2,1)} %get-tuple-element.120, bf16[4095,1024]{1,0:T(8,128)(2,1)} %get-tuple-element.119, bf16[1024,1024]{1,0:T(8,128)(2,1)} %copy-done.6, bf16[1024,1024]{1,0:T(8,128)(2,1)S(1)} %copy-done.5, bf16[1024,1024]{1,0:T(8,128)(2,1)S(1)} %constant_dynamic-update-slice_fusion.56, ...), kind=kOutput, calls=%fused_computation.5 | convolution fusion | flops 13086228480 | bytes 35647488 | tf_op jit(solution)/shard_map/dot_general | solution.py:83
  895.2 14.1 reshape.813
  909.3 19.1 %copy.269 = f32[3,8,2,64,4,2,64]{3,1,6,4,5,2,0:T(8,128)} copy(f32[3,8,2,64,4,2,64]{6,5,4,3,2,1,0:T(2,128)} %reshape.813) | data formatting | bytes 12582912 | tf_op jit(solution)/shard_map/reshape | solution.py:285
  928.4 11.5 reshape.814
  949.1 8.1 fusion.69
  961.7 9.1 copy.274
  970.8 6.8 convert_element_type.481
  1028.0 12.8 collective-permute-start.90
  1053.4 8.0 collective-permute-done.85
  1072.7 15.2 collective-permute-start.101
  1088.0 10.1 collective-permute-done.94
  1108.5 15.2 collective-permute-start.99
  1123.8 7.3 collective-permute-start.110
  1136.5 12.1 collective-permute-done.105
  1154.3 24.9 %collective-permute-start.148 = (bf16[9,64,256]{2,1,0:T(8,128)(2,1)}, bf16[9,64,256]{2,1,0:T(8,128)(2,1)S(1)}, u32[]{:S(2)}, u32[]{:S(2)}) collective-permute-start(bf16[9,64,256]{2,1,0:T(8,128)(2,1)} %get-tuple-element.149), channel_id=1, source_target_pairs={{0,7},{1,0},{2,1},{3,2},{4,3},{5,4},{6,5},{7,6},{8,15},{9,8},{10,9... | collective-permute-start | bytes 884744 | tf_op jit(solution)/shard_map/ppermute | solution.py:21
  1197.8 53.3 %all-gather.4 = f32[32,4,64]{2,1,0:T(4,128)S(1)} all-gather(f32[1,4,64]{2,1,0:T(4,128)S(1)} %maximum_bitcast_fusion.4), channel_id=4, replica_groups=mesh['dp'=4,'shard'=8] {'dp','shard'}, dimensions={0}, use_global_device_ids=true | all-gather | bytes 33792 | tf_op jit(solution)/shard_map/all_gather | solution.py:331
  1305.5 9.3 collective-permute-done.123
  1321.4 22.6 %maximum_maximum_fusion = bf16[4096,512]{1,0:T(8,128)(2,1)} fusion(bf16[1024,128]{1,0:T(8,128)(2,1)S(1)} %collective-permute-done.127, bf16[1024,128]{1,0:T(8,128)(2,1)S(1)} %collective-permute-done.126, bf16[1024,128]{1,0:T(8,128)(2,1)S(1)} %collective-permute-done.125, bf16[1024,128]{1,0:T(8,128)(2,1)S(1)} %copy-done.74, ...), kind=kLoop, calls=%fused_computation.101 | loop fusion | flops 67108864 | bytes 8388608 | tf_op jit(solution)/shard_map/concatenate | solution.py:305
  1344.1 17.3 fusion.65
  1391.2 47.0 %fusion.80 = bf16[4096,512]{1,0:T(8,128)(2,1)S(1)} fusion(bf16[1536,512]{1,0:T(8,128)(2,1)S(1)} %bitcast.502, bf16[4095,512]{1,0:T(8,128)(2,1)} %get-tuple-element.139, bf16[4095,512]{1,0:T(8,128)(2,1)} %get-tuple-element.138, bf16[1024,128]{1,0:T(8,128)(2,1)} %copy-done.96, bf16[1024,128]{1,0:T(8,128)(2,1)} %copy-done.95, ...), kind=kOutput, calls=%fused_computation.91 | convolution fusion | flops 6696206336 | bytes 18348032 | tf_op jit(solution)/shard_map/dot_general | solution.py:79
  1451.3 10.9 collective-permute-done.128
  1462.2 55.4 %collective-permute-start.134 = (bf16[512,512]{1,0:T(8,128)(2,1)}, bf16[512,512]{1,0:T(8,128)(2,1)}, u32[]{:S(2)}, u32[]{:S(2)}) collective-permute-start(bf16[512,512]{1,0:T(8,128)(2,1)} %get-tuple-element.132), channel_id=1, source_target_pairs={{0,7},{1,0},{2,1},{3,2},{4,3},{5,4},{6,5},{7,6},{8,15},{9,8},{10,9... | collective-permute-start | bytes 1572872 | tf_op jit(solution)/shard_map/ppermute | solution.py:25
  1528.4 10.1 collective-permute-done.134
  1542.3 60.2 %collective-permute-done.135 = bf16[128,512]{1,0:T(8,128)(2,1)S(1)} collective-permute-done((bf16[128,512]{1,0:T(8,128)(2,1)S(1)}, bf16[128,512]{1,0:T(8,128)(2,1)S(1)}, u32[]{:S(2)}, u32[]{:S(2)}) %collective-permute-start.135) | collective-permute-done | bytes 131104 | tf_op jit(solution)/shard_map/ppermute | solution.py:21
  1608.0 73.9 %collective-permute-start.137 = (bf16[128,512]{1,0:T(8,128)(2,1)S(1)}, bf16[128,512]{1,0:T(8,128)(2,1)S(1)}, u32[]{:S(2)}, u32[]{:S(2)}) collective-permute-start(bf16[128,512]{1,0:T(8,128)(2,1)S(1)} %get-tuple-element.283), channel_id=1, source_target_pairs={{0,8},{8,16},{16,24},{24,0},{1,9},{9,17},{17,25},{25,1},{2,10},{10... | collective-permute-start | bytes 393224 | tf_op jit(solution)/shard_map/ppermute | solution.py:21
  1692.6 6.9 copy.258
  1739.9 25.4 %collective-permute-done.157 = bf16[9,64,2048]{2,1,0:T(8,128)(2,1)S(1)} collective-permute-done((bf16[9,64,2048]{2,1,0:T(8,128)(2,1)S(1)}, bf16[9,64,2048]{2,1,0:T(8,128)(2,1)S(1)}, u32[]{:S(2)}, u32[]{:S(2)}) %collective-permute-start.157) | collective-permute-done | bytes 2359328 | tf_op jit(solution)/shard_map/ppermute | solution.py:21
  1774.9 12.5 convert_bitcast_fusion
  1787.4 13.0 copy.277
  (971 shorter events, 784.7 us)
Async XLA Ops:
  7.2 756.0 %all-gather.8.cloned.1.call-start = ((), (), s32[]{:S(2)}) async-start(), calls=%async_computation | async-start | bytes 9437184 | tf_op jit(solution)/shard_map/all_gather | solution.py:183
  7.9 761.3 %all-gather.10.cloned.1.call-start = ((), (), s32[]{:S(2)}) async-start(), calls=%async_computation.1 | async-start | bytes 2433024 | tf_op jit(solution)/shard_map/all_gather | solution.py:184
  17.8 139.0 %collective-permute-start = (bf16[128,512]{1,0:T(8,128)(2,1)}, bf16[128,512]{1,0:T(8,128)(2,1)}, u32[]{:S(2)}, u32[]{:S(2)}) collective-permute-start(bf16[128,512]{1,0:T(8,128)(2,1)} %get-tuple-element.290), channel_id=1, source_target_pairs={{0,24},{8,0},{16,8},{24,16},{1,25},{9,1},{17,9},{25,17},{2,26},{10... | collective-permute-start | bytes 393224 | tf_op jit(solution)/shard_map/ppermute | solution.py:21
  20.3 143.6 %collective-permute-start.1 = (bf16[128,512]{1,0:T(8,128)(2,1)}, bf16[128,512]{1,0:T(8,128)(2,1)}, u32[]{:S(2)}, u32[]{:S(2)}) collective-permute-start(bf16[128,512]{1,0:T(8,128)(2,1)} %get-tuple-element.289), channel_id=1, source_target_pairs={{0,16},{8,24},{16,0},{24,8},{1,17},{9,25},{17,1},{25,9},{2,18},{10... | collective-permute-start | bytes 393224 | tf_op jit(solution)/shard_map/ppermute | solution.py:21
  20.8 144.8 %collective-permute-start.2 = (bf16[128,512]{1,0:T(8,128)(2,1)}, bf16[128,512]{1,0:T(8,128)(2,1)}, u32[]{:S(2)}, u32[]{:S(2)}) collective-permute-start(bf16[128,512]{1,0:T(8,128)(2,1)} %get-tuple-element.287), channel_id=1, source_target_pairs={{0,8},{8,16},{16,24},{24,0},{1,9},{9,17},{17,25},{25,1},{2,10},{10... | collective-permute-start | bytes 393224 | tf_op jit(solution)/shard_map/ppermute | solution.py:21
  27.2 150.4 %collective-permute-start.10 = (bf16[9,32,256]{2,1,0:T(8,128)(2,1)}, bf16[9,32,256]{2,1,0:T(8,128)(2,1)}, u32[]{:S(2)}, u32[]{:S(2)}) collective-permute-start(bf16[9,32,256]{2,1,0:T(8,128)(2,1)} %bitcast.455), channel_id=1, source_target_pairs={{0,7},{1,0},{2,1},{3,2},{4,3},{5,4},{6,5},{7,6},{8,15},{9,8},{10,9... | collective-permute-start | bytes 442376 | tf_op jit(solution)/shard_map/ppermute | solution.py:21
  27.9 150.7 %collective-permute-start.11 = (bf16[9,32,256]{2,1,0:T(8,128)(2,1)}, bf16[9,32,256]{2,1,0:T(8,128)(2,1)}, u32[]{:S(2)}, u32[]{:S(2)}) collective-permute-start(bf16[9,32,256]{2,1,0:T(8,128)(2,1)} %bitcast.454), channel_id=1, source_target_pairs={{0,6},{1,7},{2,0},{3,1},{4,2},{5,3},{6,4},{7,5},{8,14},{9,15},{10,... | collective-permute-start | bytes 442376 | tf_op jit(solution)/shard_map/ppermute | solution.py:21
  183.5 45.9 %collective-permute-start.38 = (bf16[9,64,256]{2,1,0:T(8,128)(2,1)}, bf16[9,64,256]{2,1,0:T(8,128)(2,1)}, u32[]{:S(2)}, u32[]{:S(2)}) collective-permute-start(bf16[9,64,256]{2,1,0:T(8,128)(2,1)} %bitcast.446), channel_id=1, source_target_pairs={{0,5},{1,6},{2,7},{3,0},{4,1},{5,2},{6,3},{7,4},{8,13},{9,14},{10,... | collective-permute-start | bytes 884744 | tf_op jit(solution)/shard_map/ppermute | solution.py:21
  184.9 50.9 %collective-permute-start.39 = (bf16[9,64,256]{2,1,0:T(8,128)(2,1)}, bf16[9,64,256]{2,1,0:T(8,128)(2,1)}, u32[]{:S(2)}, u32[]{:S(2)}) collective-permute-start(bf16[9,64,256]{2,1,0:T(8,128)(2,1)} %bitcast.445), channel_id=1, source_target_pairs={{0,4},{1,5},{2,6},{3,7},{4,0},{5,1},{6,2},{7,3},{8,12},{9,13},{10,... | collective-permute-start | bytes 884744 | tf_op jit(solution)/shard_map/ppermute | solution.py:21
  187.6 49.8 %collective-permute-start.40 = (bf16[9,64,256]{2,1,0:T(8,128)(2,1)}, bf16[9,64,256]{2,1,0:T(8,128)(2,1)}, u32[]{:S(2)}, u32[]{:S(2)}) collective-permute-start(bf16[9,64,256]{2,1,0:T(8,128)(2,1)} %bitcast.444), channel_id=1, source_target_pairs={{0,3},{1,4},{2,5},{3,6},{4,7},{5,0},{6,1},{7,2},{8,11},{9,12},{10,... | collective-permute-start | bytes 884744 | tf_op jit(solution)/shard_map/ppermute | solution.py:21
  209.9 60.6 %collective-permute-start.41 = (bf16[9,64,256]{2,1,0:T(8,128)(2,1)S(1)}, bf16[9,64,256]{2,1,0:T(8,128)(2,1)S(1)}, u32[]{:S(2)}, u32[]{:S(2)}) collective-permute-start(bf16[9,64,256]{2,1,0:T(8,128)(2,1)S(1)} %bitcast.509), channel_id=1, source_target_pairs={{0,2},{1,3},{2,4},{3,5},{4,6},{5,7},{6,0},{7,1},{8,10},{9,11},{10,... | collective-permute-start | bytes 884744 | tf_op jit(solution)/shard_map/ppermute | solution.py:21
  212.8 58.4 %collective-permute-start.42 = (bf16[9,64,256]{2,1,0:T(8,128)(2,1)S(1)}, bf16[9,64,256]{2,1,0:T(8,128)(2,1)S(1)}, u32[]{:S(2)}, u32[]{:S(2)}) collective-permute-start(bf16[9,64,256]{2,1,0:T(8,128)(2,1)S(1)} %bitcast.508), channel_id=1, source_target_pairs={{0,1},{1,2},{2,3},{3,4},{4,5},{5,6},{6,7},{7,0},{8,9},{9,10},{10,1... | collective-permute-start | bytes 884744 | tf_op jit(solution)/shard_map/ppermute | solution.py:21
  229.4 131.5 %collective-permute-start.3 = (bf16[512,512]{1,0:T(8,128)(2,1)}, bf16[512,512]{1,0:T(8,128)(2,1)}, u32[]{:S(2)}, u32[]{:S(2)}) collective-permute-start(bf16[512,512]{1,0:T(8,128)(2,1)} %bitcast.9), channel_id=1, source_target_pairs={{0,7},{1,0},{2,1},{3,2},{4,3},{5,4},{6,5},{7,6},{8,15},{9,8},{10,9... | collective-permute-start | bytes 1572872 | tf_op jit(solution)/shard_map/ppermute | solution.py:21
  235.8 128.1 %collective-permute-start.4 = (bf16[512,512]{1,0:T(8,128)(2,1)}, bf16[512,512]{1,0:T(8,128)(2,1)}, u32[]{:S(2)}, u32[]{:S(2)}) collective-permute-start(bf16[512,512]{1,0:T(8,128)(2,1)} %bitcast.9), channel_id=1, source_target_pairs={{0,6},{1,7},{2,0},{3,1},{4,2},{5,3},{6,4},{7,5},{8,14},{9,15},{10,... | collective-permute-start | bytes 1572872 | tf_op jit(solution)/shard_map/ppermute | solution.py:21
  237.5 130.4 %collective-permute-start.5 = (bf16[512,512]{1,0:T(8,128)(2,1)}, bf16[512,512]{1,0:T(8,128)(2,1)}, u32[]{:S(2)}, u32[]{:S(2)}) collective-permute-start(bf16[512,512]{1,0:T(8,128)(2,1)} %bitcast.9), channel_id=1, source_target_pairs={{0,5},{1,6},{2,7},{3,0},{4,1},{5,2},{6,3},{7,4},{8,13},{9,14},{10,... | collective-permute-start | bytes 1572872 | tf_op jit(solution)/shard_map/ppermute | solution.py:21
  270.5 99.3 %collective-permute-start.6 = (bf16[512,512]{1,0:T(8,128)(2,1)}, bf16[512,512]{1,0:T(8,128)(2,1)}, u32[]{:S(2)}, u32[]{:S(2)}) collective-permute-start(bf16[512,512]{1,0:T(8,128)(2,1)} %bitcast.9), channel_id=1, source_target_pairs={{0,4},{1,5},{2,6},{3,7},{4,0},{5,1},{6,2},{7,3},{8,12},{9,13},{10,... | collective-permute-start | bytes 1572872 | tf_op jit(solution)/shard_map/ppermute | solution.py:21
  271.2 100.4 %collective-permute-start.7 = (bf16[512,512]{1,0:T(8,128)(2,1)}, bf16[512,512]{1,0:T(8,128)(2,1)}, u32[]{:S(2)}, u32[]{:S(2)}) collective-permute-start(bf16[512,512]{1,0:T(8,128)(2,1)} %bitcast.9), channel_id=1, source_target_pairs={{0,3},{1,4},{2,5},{3,6},{4,7},{5,0},{6,1},{7,2},{8,11},{9,12},{10,... | collective-permute-start | bytes 1572872 | tf_op jit(solution)/shard_map/ppermute | solution.py:21
  509.5 45.9 %collective-permute-start.69 = (bf16[1024,128]{1,0:T(8,128)(2,1)S(1)}, bf16[1024,128]{1,0:T(8,128)(2,1)S(1)}, u32[]{:S(2)}, u32[]{:S(2)}) collective-permute-start(bf16[1024,128]{1,0:T(8,128)(2,1)S(1)} %get-tuple-element.246), channel_id=1, source_target_pairs={{0,4},{1,5},{2,6},{3,7},{4,0},{5,1},{6,2},{7,3},{8,12},{9,13},{10,... | collective-permute-start | bytes 786440 | tf_op jit(solution)/shard_map/ppermute | solution.py:21
  512.4 43.1 %collective-permute-start.70 = (bf16[1024,128]{1,0:T(8,128)(2,1)S(1)}, bf16[1024,128]{1,0:T(8,128)(2,1)S(1)}, u32[]{:S(2)}, u32[]{:S(2)}) collective-permute-start(bf16[1024,128]{1,0:T(8,128)(2,1)S(1)} %get-tuple-element.246), channel_id=1, source_target_pairs={{0,3},{1,4},{2,5},{3,6},{4,7},{5,0},{6,1},{7,2},{8,11},{9,12},{10,... | collective-permute-start | bytes 786440 | tf_op jit(solution)/shard_map/ppermute | solution.py:21
  520.2 51.5 %collective-permute-start.71 = (bf16[1024,128]{1,0:T(8,128)(2,1)S(1)}, bf16[1024,128]{1,0:T(8,128)(2,1)S(1)}, u32[]{:S(2)}, u32[]{:S(2)}) collective-permute-start(bf16[1024,128]{1,0:T(8,128)(2,1)S(1)} %get-tuple-element.246), channel_id=1, source_target_pairs={{0,2},{1,3},{2,4},{3,5},{4,6},{5,7},{6,0},{7,1},{8,10},{9,11},{10,... | collective-permute-start | bytes 786440 | tf_op jit(solution)/shard_map/ppermute | solution.py:21
  572.0 44.7 %collective-permute-start.61 = (bf16[1024,128]{1,0:T(8,128)(2,1)S(1)}, bf16[1024,128]{1,0:T(8,128)(2,1)S(1)}, u32[]{:S(2)}, u32[]{:S(2)}) collective-permute-start(bf16[1024,128]{1,0:T(8,128)(2,1)S(1)} %get-tuple-element.247), channel_id=1, source_target_pairs={{0,2},{1,3},{2,4},{3,5},{4,6},{5,7},{6,0},{7,1},{8,10},{9,11},{10,... | collective-permute-start | bytes 786440 | tf_op jit(solution)/shard_map/ppermute | solution.py:21
  639.7 52.8 %collective-permute-start.43 = (bf16[1024,128]{1,0:T(8,128)(2,1)}, bf16[1024,128]{1,0:T(8,128)(2,1)}, u32[]{:S(2)}, u32[]{:S(2)}) collective-permute-start(bf16[1024,128]{1,0:T(8,128)(2,1)} %get-tuple-element.239), channel_id=1, source_target_pairs={{0,8},{8,16},{16,24},{24,0},{1,9},{9,17},{17,25},{25,1},{2,10},{10... | collective-permute-start | bytes 786440 | tf_op jit(solution)/shard_map/ppermute | solution.py:25
  645.1 50.3 %collective-permute-start.44 = (bf16[1024,128]{1,0:T(8,128)(2,1)}, bf16[1024,128]{1,0:T(8,128)(2,1)}, u32[]{:S(2)}, u32[]{:S(2)}) collective-permute-start(bf16[1024,128]{1,0:T(8,128)(2,1)} %get-tuple-element.241), channel_id=1, source_target_pairs={{0,16},{8,24},{16,0},{24,8},{1,17},{9,25},{17,1},{25,9},{2,18},{10... | collective-permute-start | bytes 786440 | tf_op jit(solution)/shard_map/ppermute | solution.py:25
  646.7 48.7 %collective-permute-start.45 = (bf16[1024,128]{1,0:T(8,128)(2,1)}, bf16[1024,128]{1,0:T(8,128)(2,1)}, u32[]{:S(2)}, u32[]{:S(2)}) collective-permute-start(bf16[1024,128]{1,0:T(8,128)(2,1)} %get-tuple-element.240), channel_id=1, source_target_pairs={{0,24},{8,0},{16,8},{24,16},{1,25},{9,1},{17,9},{25,17},{2,26},{10... | collective-permute-start | bytes 786440 | tf_op jit(solution)/shard_map/ppermute | solution.py:25
  1106.4 42.1 %collective-permute-start.105 = (bf16[1024,128]{1,0:T(8,128)(2,1)S(1)}, bf16[1024,128]{1,0:T(8,128)(2,1)S(1)}, u32[]{:S(2)}, u32[]{:S(2)}) collective-permute-start(bf16[1024,128]{1,0:T(8,128)(2,1)S(1)} %get-tuple-element.178), channel_id=1, source_target_pairs={{0,7},{1,0},{2,1},{3,2},{4,3},{5,4},{6,5},{7,6},{8,15},{9,8},{10,9... | collective-permute-start | bytes 786440 | tf_op jit(solution)/shard_map/ppermute | solution.py:25
  1108.5 43.3 %collective-permute-start.99 = (bf16[1024,128]{1,0:T(8,128)(2,1)S(1)}, bf16[1024,128]{1,0:T(8,128)(2,1)S(1)}, u32[]{:S(2)}, u32[]{:S(2)}) collective-permute-start(bf16[1024,128]{1,0:T(8,128)(2,1)S(1)} %get-tuple-element.177), channel_id=1, source_target_pairs={{0,1},{1,2},{2,3},{3,4},{4,5},{5,6},{6,7},{7,0},{8,9},{9,10},{10,1... | collective-permute-start | bytes 786440 | tf_op jit(solution)/shard_map/ppermute | solution.py:25
  1154.3 102.3 %collective-permute-start.148 = (bf16[9,64,256]{2,1,0:T(8,128)(2,1)}, bf16[9,64,256]{2,1,0:T(8,128)(2,1)S(1)}, u32[]{:S(2)}, u32[]{:S(2)}) collective-permute-start(bf16[9,64,256]{2,1,0:T(8,128)(2,1)} %get-tuple-element.149), channel_id=1, source_target_pairs={{0,7},{1,0},{2,1},{3,2},{4,3},{5,4},{6,5},{7,6},{8,15},{9,8},{10,9... | collective-permute-start | bytes 884744 | tf_op jit(solution)/shard_map/ppermute | solution.py:21
  1179.2 80.8 %collective-permute-start.149 = (bf16[9,64,256]{2,1,0:T(8,128)(2,1)}, bf16[9,64,256]{2,1,0:T(8,128)(2,1)S(1)}, u32[]{:S(2)}, u32[]{:S(2)}) collective-permute-start(bf16[9,64,256]{2,1,0:T(8,128)(2,1)} %get-tuple-element.148), channel_id=1, source_target_pairs={{0,6},{1,7},{2,0},{3,1},{4,2},{5,3},{6,4},{7,5},{8,14},{9,15},{10,... | collective-permute-start | bytes 884744 | tf_op jit(solution)/shard_map/ppermute | solution.py:21
  1185.2 75.5 %collective-permute-start.150 = (bf16[9,64,256]{2,1,0:T(8,128)(2,1)}, bf16[9,64,256]{2,1,0:T(8,128)(2,1)S(1)}, u32[]{:S(2)}, u32[]{:S(2)}) collective-permute-start(bf16[9,64,256]{2,1,0:T(8,128)(2,1)} %get-tuple-element.147), channel_id=1, source_target_pairs={{0,5},{1,6},{2,7},{3,0},{4,1},{5,2},{6,3},{7,4},{8,13},{9,14},{10,... | collective-permute-start | bytes 884744 | tf_op jit(solution)/shard_map/ppermute | solution.py:21
  1188.8 75.0 %collective-permute-start.151 = (bf16[9,64,256]{2,1,0:T(8,128)(2,1)}, bf16[9,64,256]{2,1,0:T(8,128)(2,1)S(1)}, u32[]{:S(2)}, u32[]{:S(2)}) collective-permute-start(bf16[9,64,256]{2,1,0:T(8,128)(2,1)} %get-tuple-element.146), channel_id=1, source_target_pairs={{0,4},{1,5},{2,6},{3,7},{4,0},{5,1},{6,2},{7,3},{8,12},{9,13},{10,... | collective-permute-start | bytes 884744 | tf_op jit(solution)/shard_map/ppermute | solution.py:21
  1189.6 76.1 %collective-permute-start.152 = (bf16[9,64,256]{2,1,0:T(8,128)(2,1)}, bf16[9,64,256]{2,1,0:T(8,128)(2,1)}, u32[]{:S(2)}, u32[]{:S(2)}) collective-permute-start(bf16[9,64,256]{2,1,0:T(8,128)(2,1)} %get-tuple-element.145), channel_id=1, source_target_pairs={{0,3},{1,4},{2,5},{3,6},{4,7},{5,0},{6,1},{7,2},{8,11},{9,12},{10,... | collective-permute-start | bytes 884744 | tf_op jit(solution)/shard_map/ppermute | solution.py:21
  1384.7 56.4 %collective-permute-start.138 = (bf16[9,32,256]{2,1,0:T(8,128)(2,1)S(1)}, bf16[9,32,256]{2,1,0:T(8,128)(2,1)S(1)}, u32[]{:S(2)}, u32[]{:S(2)}) collective-permute-start(bf16[9,32,256]{2,1,0:T(8,128)(2,1)S(1)} %get-tuple-element.207), channel_id=1, source_target_pairs={{0,7},{1,0},{2,1},{3,2},{4,3},{5,4},{6,5},{7,6},{8,15},{9,8},{10,9... | collective-permute-start | bytes 442376 | tf_op jit(solution)/shard_map/ppermute | solution.py:21
  1384.7 58.2 %collective-permute-start.139 = (bf16[9,32,256]{2,1,0:T(8,128)(2,1)S(1)}, bf16[9,32,256]{2,1,0:T(8,128)(2,1)S(1)}, u32[]{:S(2)}, u32[]{:S(2)}) collective-permute-start(bf16[9,32,256]{2,1,0:T(8,128)(2,1)S(1)} %get-tuple-element.206), channel_id=1, source_target_pairs={{0,6},{1,7},{2,0},{3,1},{4,2},{5,3},{6,4},{7,5},{8,14},{9,15},{10,... | collective-permute-start | bytes 442376 | tf_op jit(solution)/shard_map/ppermute | solution.py:21
  1386.5 56.5 %collective-permute-start.140 = (bf16[9,32,256]{2,1,0:T(8,128)(2,1)S(1)}, bf16[9,32,256]{2,1,0:T(8,128)(2,1)S(1)}, u32[]{:S(2)}, u32[]{:S(2)}) collective-permute-start(bf16[9,32,256]{2,1,0:T(8,128)(2,1)S(1)} %get-tuple-element.205), channel_id=1, source_target_pairs={{0,5},{1,6},{2,7},{3,0},{4,1},{5,2},{6,3},{7,4},{8,13},{9,14},{10,... | collective-permute-start | bytes 442376 | tf_op jit(solution)/shard_map/ppermute | solution.py:21
  1389.5 54.6 %collective-permute-start.141 = (bf16[9,32,256]{2,1,0:T(8,128)(2,1)S(1)}, bf16[9,32,256]{2,1,0:T(8,128)(2,1)S(1)}, u32[]{:S(2)}, u32[]{:S(2)}) collective-permute-start(bf16[9,32,256]{2,1,0:T(8,128)(2,1)S(1)} %get-tuple-element.204), channel_id=1, source_target_pairs={{0,4},{1,5},{2,6},{3,7},{4,0},{5,1},{6,2},{7,3},{8,12},{9,13},{10,... | collective-permute-start | bytes 442376 | tf_op jit(solution)/shard_map/ppermute | solution.py:21
  1389.7 54.7 %collective-permute-start.142 = (bf16[9,32,256]{2,1,0:T(8,128)(2,1)S(1)}, bf16[9,32,256]{2,1,0:T(8,128)(2,1)S(1)}, u32[]{:S(2)}, u32[]{:S(2)}) collective-permute-start(bf16[9,32,256]{2,1,0:T(8,128)(2,1)S(1)} %get-tuple-element.203), channel_id=1, source_target_pairs={{0,3},{1,4},{2,5},{3,6},{4,7},{5,0},{6,1},{7,2},{8,11},{9,12},{10,... | collective-permute-start | bytes 442376 | tf_op jit(solution)/shard_map/ppermute | solution.py:21
  1444.5 75.9 %collective-permute-start.130 = (bf16[512,512]{1,0:T(8,128)(2,1)}, bf16[512,512]{1,0:T(8,128)(2,1)}, u32[]{:S(2)}, u32[]{:S(2)}) collective-permute-start(bf16[512,512]{1,0:T(8,128)(2,1)} %get-tuple-element.136), channel_id=1, source_target_pairs={{0,3},{1,4},{2,5},{3,6},{4,7},{5,0},{6,1},{7,2},{8,11},{9,12},{10,... | collective-permute-start | bytes 1572872 | tf_op jit(solution)/shard_map/ppermute | solution.py:25
  1447.5 72.9 %collective-permute-start.131 = (bf16[512,512]{1,0:T(8,128)(2,1)}, bf16[512,512]{1,0:T(8,128)(2,1)}, u32[]{:S(2)}, u32[]{:S(2)}) collective-permute-start(bf16[512,512]{1,0:T(8,128)(2,1)} %get-tuple-element.135), channel_id=1, source_target_pairs={{0,4},{1,5},{2,6},{3,7},{4,0},{5,1},{6,2},{7,3},{8,12},{9,13},{10,... | collective-permute-start | bytes 1572872 | tf_op jit(solution)/shard_map/ppermute | solution.py:25
  1451.0 70.5 %collective-permute-start.132 = (bf16[512,512]{1,0:T(8,128)(2,1)}, bf16[512,512]{1,0:T(8,128)(2,1)}, u32[]{:S(2)}, u32[]{:S(2)}) collective-permute-start(bf16[512,512]{1,0:T(8,128)(2,1)} %get-tuple-element.134), channel_id=1, source_target_pairs={{0,5},{1,6},{2,7},{3,0},{4,1},{5,2},{6,3},{7,4},{8,13},{9,14},{10,... | collective-permute-start | bytes 1572872 | tf_op jit(solution)/shard_map/ppermute | solution.py:25
  1462.2 65.1 %collective-permute-start.133 = (bf16[512,512]{1,0:T(8,128)(2,1)}, bf16[512,512]{1,0:T(8,128)(2,1)}, u32[]{:S(2)}, u32[]{:S(2)}) collective-permute-start(bf16[512,512]{1,0:T(8,128)(2,1)} %get-tuple-element.133), channel_id=1, source_target_pairs={{0,6},{1,7},{2,0},{3,1},{4,2},{5,3},{6,4},{7,5},{8,14},{9,15},{10,... | collective-permute-start | bytes 1572872 | tf_op jit(solution)/shard_map/ppermute | solution.py:25
  1462.2 76.2 %collective-permute-start.134 = (bf16[512,512]{1,0:T(8,128)(2,1)}, bf16[512,512]{1,0:T(8,128)(2,1)}, u32[]{:S(2)}, u32[]{:S(2)}) collective-permute-start(bf16[512,512]{1,0:T(8,128)(2,1)} %get-tuple-element.132), channel_id=1, source_target_pairs={{0,7},{1,0},{2,1},{3,2},{4,3},{5,4},{6,5},{7,6},{8,15},{9,8},{10,9... | collective-permute-start | bytes 1572872 | tf_op jit(solution)/shard_map/ppermute | solution.py:25
  1520.4 214.6 %collective-permute-start.155 = (bf16[9,64,2048]{2,1,0:T(8,128)(2,1)}, bf16[9,64,2048]{2,1,0:T(8,128)(2,1)S(1)}, u32[]{:S(2)}, u32[]{:S(2)}) collective-permute-start(bf16[9,64,2048]{2,1,0:T(8,128)(2,1)} %bitcast.498), channel_id=1, source_target_pairs={{0,24},{8,0},{16,8},{24,16},{1,25},{9,1},{17,9},{25,17},{2,26},{10... | collective-permute-start | bytes 7077896 | tf_op jit(solution)/shard_map/ppermute | solution.py:21
  1520.4 216.1 %collective-permute-start.156 = (bf16[9,64,2048]{2,1,0:T(8,128)(2,1)}, bf16[9,64,2048]{2,1,0:T(8,128)(2,1)}, u32[]{:S(2)}, u32[]{:S(2)}) collective-permute-start(bf16[9,64,2048]{2,1,0:T(8,128)(2,1)} %bitcast.499), channel_id=1, source_target_pairs={{0,16},{8,24},{16,0},{24,8},{1,17},{9,25},{17,1},{25,9},{2,18},{10... | collective-permute-start | bytes 7077896 | tf_op jit(solution)/shard_map/ppermute | solution.py:21
  1521.5 187.4 %collective-permute-start.145 = (bf16[9,32,2048]{2,1,0:T(8,128)(2,1)}, bf16[9,32,2048]{2,1,0:T(8,128)(2,1)}, u32[]{:S(2)}, u32[]{:S(2)}) collective-permute-start(bf16[9,32,2048]{2,1,0:T(8,128)(2,1)} %bitcast.168), channel_id=1, source_target_pairs={{0,24},{8,0},{16,8},{24,16},{1,25},{9,1},{17,9},{25,17},{2,26},{10... | collective-permute-start | bytes 3538952 | tf_op jit(solution)/shard_map/ppermute | solution.py:21
  1527.3 185.5 %collective-permute-start.146 = (bf16[9,32,2048]{2,1,0:T(8,128)(2,1)}, bf16[9,32,2048]{2,1,0:T(8,128)(2,1)}, u32[]{:S(2)}, u32[]{:S(2)}) collective-permute-start(bf16[9,32,2048]{2,1,0:T(8,128)(2,1)} %bitcast.168), channel_id=1, source_target_pairs={{0,16},{8,24},{16,0},{24,8},{1,17},{9,25},{17,1},{25,9},{2,18},{10... | collective-permute-start | bytes 3538952 | tf_op jit(solution)/shard_map/ppermute | solution.py:21
  1541.2 61.3 %collective-permute-start.135 = (bf16[128,512]{1,0:T(8,128)(2,1)S(1)}, bf16[128,512]{1,0:T(8,128)(2,1)S(1)}, u32[]{:S(2)}, u32[]{:S(2)}) collective-permute-start(bf16[128,512]{1,0:T(8,128)(2,1)S(1)} %get-tuple-element.286), channel_id=1, source_target_pairs={{0,24},{8,0},{16,8},{24,16},{1,25},{9,1},{17,9},{25,17},{2,26},{10... | collective-permute-start | bytes 393224 | tf_op jit(solution)/shard_map/ppermute | solution.py:21
  1608.0 78.1 %collective-permute-start.137 = (bf16[128,512]{1,0:T(8,128)(2,1)S(1)}, bf16[128,512]{1,0:T(8,128)(2,1)S(1)}, u32[]{:S(2)}, u32[]{:S(2)}) collective-permute-start(bf16[128,512]{1,0:T(8,128)(2,1)S(1)} %get-tuple-element.283), channel_id=1, source_target_pairs={{0,8},{8,16},{16,24},{24,0},{1,9},{9,17},{17,25},{25,1},{2,10},{10... | collective-permute-start | bytes 393224 | tf_op jit(solution)/shard_map/ppermute | solution.py:21
  1708.9 56.3 %collective-permute-start.157 = (bf16[9,64,2048]{2,1,0:T(8,128)(2,1)S(1)}, bf16[9,64,2048]{2,1,0:T(8,128)(2,1)S(1)}, u32[]{:S(2)}, u32[]{:S(2)}) collective-permute-start(bf16[9,64,2048]{2,1,0:T(8,128)(2,1)S(1)} %bitcast.500), channel_id=1, source_target_pairs={{0,8},{8,16},{16,24},{24,0},{1,9},{9,17},{17,25},{25,1},{2,10},{10... | collective-permute-start | bytes 7077896 | tf_op jit(solution)/shard_map/ppermute | solution.py:21
  (242 other events, 5889.3 us)
Sparse Core Ops, SparseCore 0:
  9.6 87.7 all-gather.7
  99.0 30.4 all-gather.9

commit v2 on v0

--- a/solution.py
+++ b/solution.py
@@ -1,9 +1,585 @@
+import functools
+import math
 import jax
 import jax.numpy as jnp
 from jax import lax
+from jax.experimental import pallas as pl
+from jax.experimental.pallas import tpu as pltpu
 from jax.sharding import PartitionSpec as P
-
+bf16 = jnp.bfloat16
+f32 = jnp.float32
 epsilon = 1e-05
+big_vmem = 56 * 1024 * 1024
+VM = pl.BlockSpec(memory_space=pltpu.VMEM)
+SM = pl.BlockSpec(memory_space=pltpu.SMEM)
+HB = pl.BlockSpec(memory_space=pl.ANY)
+
+def params():
+    return pltpu.CompilerParams(vmem_limit_bytes=big_vmem)
+
+def cost(flops, moved):
+    return pl.CostEstimate(flops=int(flops), bytes_accessed=int(moved), transcendentals=0)
+
+
+def split_kernel(shard, place, weight, *refs):
+    outs, (own, sem) = refs[:shard], refs[shard:]
+    copy = pltpu.make_async_copy(weight.at[:, place[0]], own, sem)
+    copy.start()
+    copy.wait()
+    for step in range(shard):
+        column = lax.rem(place[1] - step + shard, shard)
+        width = outs[step].shape[2]
+        outs[step][...] = own[:, :, pl.ds(pl.multiple_of(column * width, width), width)]
+
+
+def split_weight(weight, place, dp, shard):
+    rows, columns = weight.shape
+    part = rows // (9 * dp)
+    chunk = jax.ShapeDtypeStruct((9, part, columns // shard), bf16)
+    return pl.pallas_call(
+        functools.partial(split_kernel, shard),
+        out_shape=[chunk] * shard,
+        in_specs=[SM, HB],
+        out_specs=[VM] * shard,
+        scratch_shapes=[pltpu.VMEM((9, part, columns), bf16), pltpu.SemaphoreType.DMA(())],
+        compiler_params=params(),
+        cost_estimate=cost(0, 4 * rows * columns // dp),
+        name="split_weight",
+    )(place, weight.reshape(9, dp, part, columns))
+
+
+def expand_kernel(shard, by_mel, table, *refs):
+    pieces, (spread, out, held) = refs[:shard], refs[shard:]
+    for step in range(shard):
+        held[pl.ds(9 * step, 9)] = pieces[step][...]
+    part = held.shape[1]
+
+    def one(position, carry):
+        for a in range(3):
+            taps = [held[table[(3 * a + b) * shard + position]] for b in range(3)]
+            for m in range(2):
+                pair = jnp.concatenate([taps[m + 1], taps[m]], axis=1)
+                wide = jnp.dot(pair, spread[...], preferred_element_type=f32).astype(bf16)
+                if by_mel:
+                    out[a, m, position] = wide
+                else:
+                    out[a, position, pl.ds(m * part, part)] = wide
+        return carry
+
+    lax.fori_loop(0, shard, one, 0)
+
+
+def expand_weight(pieces, table, spread, by_mel):
+    shard = len(pieces)
+    _, part, columns = pieces[0].shape
+    shape = (3, 2, shard, part, 2 * columns) if by_mel else (3, shard, 2 * part, 2 * columns)
+    wide = pl.pallas_call(
+        functools.partial(expand_kernel, shard, by_mel),
+        out_shape=jax.ShapeDtypeStruct(shape, bf16),
+        in_specs=[SM] + [VM] * (shard + 1),
+        out_specs=VM,
+        scratch_shapes=[pltpu.VMEM((9 * shard, part, columns), bf16)],
+        compiler_params=params(),
+        cost_estimate=cost(2 * 6 * shard * part * 4 * columns * columns, 30 * shard * part * columns),
+        name="expand_weight",
+    )(table, *pieces, spread)
+    return wide.reshape(3, 2 * shard * part, 2 * columns)
+
+
+def conv_kernel(count, back, split, tile, *refs):
+    rows_in, taps, outs, (first, last) = refs[:count], refs[count], refs[count + 1 : -2], refs[-2:]
+    height = first.shape[0] - 8
+    width = first.shape[1]
+    first[0:8] = jnp.zeros((8, width), f32)
+    last[height:] = jnp.zeros((8, width), f32)
+    late, early = (2, 0) if back else (0, 2)
+    contract = (((1,), (1,)), ((), ())) if back else (((1,), (0,)), ((), ()))
+
+    def block(ref, at):
+        value = ref[at] if len(ref.shape) == 2 else jnp.concatenate(
+            [ref[i, at] for i in range(ref.shape[0])], axis=1)
+        return value
+
+    def one(i, carry):
+        at = pl.ds(pl.multiple_of(i * tile, tile), tile)
+        rows = jnp.concatenate([block(ref, at) for ref in rows_in], axis=1)
+        first[pl.ds(pl.multiple_of(i * tile + 8, 8), tile)] = lax.dot_general(
+            rows, taps[late], contract, preferred_element_type=f32)
+        last[at] = lax.dot_general(rows, taps[early], contract, preferred_element_type=f32)
+        return carry
+
+    lax.fori_loop(0, height // tile, one, 0)
+
+    def two(i, carry):
+        start = pl.multiple_of(i * tile, tile)
+        at = pl.ds(start, tile)
+        rows = jnp.concatenate([block(ref, at) for ref in rows_in], axis=1)
+        total = lax.dot_general(rows, taps[1], contract, preferred_element_type=f32)
+        before = first[pl.ds(start, tile + 8)]
+        after = last[pl.ds(start, tile + 8)]
+        total = total + before[7 : tile + 7] + after[1 : tile + 1]
+        total = total.astype(bf16)
+        column = 0
+        for out in outs:
+            if len(out.shape) == 2:
+                step = out.shape[1]
+                out[at] = total[:, column : column + step]
+                column += step
+            else:
+                step = out.shape[2]
+                for k in range(out.shape[0]):
+                    out[k, at] = total[:, column : column + step]
+                    column += step
+        return carry
+
+    lax.fori_loop(0, height // tile, two, 0)
+
+
+def convolve(rows_in, taps, out_shapes, back=False, tile=256, name="convolve"):
+    height = rows_in[0].shape[-2]
+    width = taps.shape[1] if back else taps.shape[2]
+    moved = 2 * (sum(r.size for r in rows_in) + taps.size + sum(math.prod(s) for s in out_shapes))
+    return pl.pallas_call(
+        functools.partial(conv_kernel, len(rows_in), back, None, tile),
+        out_shape=[jax.ShapeDtypeStruct(s, bf16) for s in out_shapes],
+        in_specs=[VM] * (len(rows_in) + 1),
+        out_specs=[VM] * len(out_shapes),
+        scratch_shapes=[pltpu.VMEM((height + 8, width), f32)] * 2,
+        compiler_params=params(),
+        cost_estimate=cost(2 * height * taps.size, moved),
+        name=name,
+    )(*rows_in, taps)
+
+
+def grad_kernel(chunks, x_count, g_count, part, by_mel, shard, tile, table, *refs):
+    n = chunks * x_count
+    x_refs, g_refs = refs[:n], refs[n : n + chunks * g_count]
+    spread, outs = refs[n + chunks * g_count], refs[n + chunks * g_count + 1 : -2]
+    total, moved = refs[-2:]
+    height = g_refs[0].shape[0]
+    half = spread.shape[0] // 2
+    total[...] = jnp.zeros_like(total)
+
+    def block(ref, at):
+        return ref[at] if len(ref.shape) == 2 else jnp.concatenate(
+            [ref[i, at] for i in range(ref.shape[0])], axis=1)
+
+    width = 2 * half
+    moved[0:8] = jnp.zeros((8, width), f32)
+    moved[height + 8 :] = jnp.zeros((8, width), f32)
+    for chunk in range(chunks):
+        xs = x_refs[chunk * x_count : (chunk + 1) * x_count]
+        gs = g_refs[chunk * g_count : (chunk + 1) * g_count]
+        column = 0
+        for g in gs:
+            moved[8 : height + 8, column : column + g.shape[1]] = g[...].astype(f32)
+            column += g.shape[1]
+
+        def one(i, carry, xs=xs):
+            start = pl.multiple_of(i * tile, tile)
+            at = pl.ds(start, tile)
+            rows = jnp.concatenate([block(ref, at) for ref in xs], axis=1)
+            around = moved[pl.ds(start, tile + 16)]
+            three = jnp.concatenate(
+                [around[9 - a : 9 - a + tile].astype(bf16) for a in range(3)], axis=1)
+            total[...] += lax.dot_general(
+                rows, three, (((0,), (0,)), ((), ())), preferred_element_type=f32)
+            return carry
+
+        lax.fori_loop(0, height // tile, one, 0)
+
+    def fold(position, carry):
+        for a in range(3):
+            if by_mel:
+                at = [pl.multiple_of((m * shard + position) * part, part) for m in range(2)]
+            else:
+                at = [pl.multiple_of((2 * position + m) * part, part) for m in range(2)]
+            rows = [total[pl.ds(start, part), a * width : (a + 1) * width].astype(bf16) for start in at]
+            top, bottom = [
+                lax.dot_general(r, spread[...], (((1,), (1,)), ((), ())), preferred_element_type=f32)
+                for r in rows
+            ]
+            taps = [top[:, half:], top[:, :half] + bottom[:, half:], bottom[:, :half]]
+            for b in range(3):
+                outs[0][table[(3 * a + b) * shard + position]] = taps[b].astype(bf16)
+        return carry
+
+    lax.fori_loop(0, shard, fold, 0)
+
+
+def weight_grad(x_chunks, g_chunks, table, spread, part, by_mel, shard, tile=256, name="weight_grad"):
+    chunks = len(x_chunks)
+    xs = [x for chunk in x_chunks for x in chunk]
+    gs = [g for chunk in g_chunks for g in chunk]
+    height = gs[0].shape[0]
+    wide = spread.shape[0]
+    deep = 2 * shard * part
+    flops = 2 * chunks * height * deep * wide * 3
+    return pl.pallas_call(
+        functools.partial(grad_kernel, chunks, len(x_chunks[0]), len(g_chunks[0]), part, by_mel, shard, tile),
+        out_shape=jax.ShapeDtypeStruct((9 * shard, part, wide // 2), bf16),
+        in_specs=[SM] + [VM] * (len(xs) + len(gs) + 1),
+        out_specs=VM,
+        scratch_shapes=[pltpu.VMEM((deep, 3 * wide), f32), pltpu.VMEM((height + 16, wide), f32)],
+        compiler_params=params(),
+        cost_estimate=cost(flops, sum(2 * v.size for v in xs + gs) + 9 * shard * part * wide),
+        name=name,
+    )(table, *xs, *gs, spread)
+
+
+def join_kernel(dp, shard, place, *refs):
+    parts, out = refs[:-1], refs[-1]
+    half = shard // 2
+    width = parts[0].shape[3]
+    for source in range(dp):
+        group = lax.bitwise_xor(place[0], source)
+        for step in range(shard):
+            column = lax.rem(place[1] + step, shard)
+            value = parts[2 * source + step // half][step % half, 0]
+            out[0, group, :, pl.ds(pl.multiple_of(column * width, width), width)] = value.astype(f32)
+
+
+def join_grad(parts, place, dp, shard):
+    half, _, part, width = parts[0].shape
+    block = pl.BlockSpec((half, 1, part, width), lambda i: (0, i, 0, 0))
+    out = pl.pallas_call(
+        functools.partial(join_kernel, dp, shard),
+        grid=(9,),
+        out_shape=jax.ShapeDtypeStruct((9, dp, part, shard * width), f32),
+        in_specs=[SM] + [block] * len(parts),
+        out_specs=pl.BlockSpec((1, dp, part, shard * width), lambda i: (i, 0, 0, 0)),
+        compiler_params=params(),
+        cost_estimate=cost(0, 6 * 9 * dp * part * shard * width),
+        name="join_grad",
+    )(place, *parts)
+    return out.reshape(9 * dp * part, shard * width)
+
+
+def roll_to(stacked, start, axis):
+    size = stacked.shape[axis]
+    doubled = jnp.concatenate([stacked, stacked], axis=axis)
+    return lax.dynamic_slice_in_dim(doubled, start, size, axis=axis)
+
+
+def pick(stacked, index):
+    return lax.dynamic_index_in_dim(stacked, index, 0, keepdims=False)
+
+
+def dot(left, right):
+    return jnp.dot(left, right, preferred_element_type=f32)
+
+
+def dot_transpose(left, right):
+    return lax.dot_general(left, right, (((1,), (1,)), ((), ())), preferred_element_type=f32)
+
+
+def both_mels(sums):
+    half = sums.shape[0] // 2
+    total = sums[:half] + sums[half:]
+    return total, jnp.concatenate([total, total])
+
+
+def norm_of(values_in, valid, pixel_count):
+    _, sum_first = both_mels(jnp.sum(values_in * valid, axis=0))
+    _, sum_square = both_mels(jnp.sum(values_in * values_in * valid, axis=0))
+    mean_value = sum_first / pixel_count
+    inv_std = lax.rsqrt(sum_square / pixel_count - mean_value * mean_value + epsilon)
+    return (values_in - mean_value) * inv_std, inv_std
+
+
+def make_device(dp, shard):
+    depth = shard // 2
+
+    def permute(value, axis, size, move):
+        return lax.ppermute(value, axis, [(i, move(i) % size) for i in range(size)])
+
+    def from_z(value, k):
+        return permute(value, "shard", shard, lambda i: i - 2 * k)
+
+    def to_z(value, k):
+        return permute(value, "shard", shard, lambda i: i + 2 * k)
+
+    def from_shard(value, k):
+        return permute(value, "shard", shard, lambda i: i - k)
+
+    def other_core(value):
+        return permute(value, "shard", shard, lambda i: i ^ 1)
+
+    def other_dp(value, r):
+        return permute(value, "dp", dp, lambda i: i ^ r)
+
+    def gather_dp(value, order):
+        one, two = other_dp(value, 1), other_dp(value, 2)
+        three = other_dp(one, 2) if order == 0 else other_dp(two, 1)
+        return [value, one, two, three]
+
+    def unswap(parts, d):
+        low = [jnp.where(d % 2 == 1, parts[r ^ 1], parts[r]) for r in range(dp)]
+        return [jnp.where(d // 2 == 1, low[r ^ 2], low[r]) for r in range(dp)]
+
+    def core_order(mine, theirs, c):
+        return [jnp.where(c == 0, mine, theirs), jnp.where(c == 0, theirs, mine)]
+
+    def gather_small(value, d, z, c):
+        line = jnp.stack([value] + [from_z(value, k) for k in range(1, depth)])
+        line = roll_to(line, (depth - z) % depth, 0)
+        pair = jnp.stack(core_order(line, other_core(line), c), axis=1)
+        return jnp.stack(unswap([pair] + [other_dp(pair, r) for r in range(1, dp)], d), axis=2)
+
+    def weight_in(weight, place):
+        pieces = split_weight(weight, place, dp, shard)
+        return [pieces[0]] + [from_shard(pieces[k], k) for k in range(1, shard)]
+
+    def weight_out(grad, place):
+        part, width = grad.shape[1:]
+        pieces = grad.reshape(shard, 9, part, width)
+        parts = [pieces[0]] + [from_shard(pieces[shard - k], k) for k in range(1, shard)]
+        half = shard // 2
+        low = gather_dp(jnp.stack(parts[:half]), 0)
+        high = gather_dp(jnp.stack(parts[half:]), 1)
+        return join_grad([h for pair in zip(low, high) for h in pair], place, dp, shard)
+
+    def on_device(
+        clip_maps,
+        lengths,
+        labels,
+        conv1_weight,
+        norm1_gain,
+        norm1_shift,
+        conv2_weight,
+        norm2_gain,
+        norm2_shift,
+        fc1_weight,
+        fc1_bias,
+        fc2_weight,
+        fc2_bias,
+    ):
+        d, s = lax.axis_index("dp"), lax.axis_index("shard")
+        z, c = s // 2, s % 2
+        place = jnp.stack([d, s]).astype(jnp.int32)
+        clip_count, frames, mels, chan_in = clip_maps.shape
+        chan_mid = norm1_gain.shape[0]
+        classes = labels.shape[1]
+        clips = clip_count * dp * shard
+        rows = clips * frames
+        step = rows // depth
+        own_rows = clip_count * frames
+        lane = chan_mid // (dp * shard)
+        lane_in = chan_in // (dp * shard)
+        wide = mels * lane
+        quarter = shard * lane_in
+        wide_in = mels * quarter
+
+        position = lax.broadcasted_iota(jnp.int32, (9, shard), 1)
+        tap = lax.broadcasted_iota(jnp.int32, (9, shard), 0)
+
+        def table_of(block):
+            group = tap * shard + block
+            return (((group // 9 - s + shard) % shard) * 9 + group % 9).reshape(9 * shard).astype(jnp.int32)
+
+        table_one = table_of(position)
+        table_two = table_of(2 * ((z + position % depth) % depth) + (c ^ (position // depth)))
+
+        from_row = lax.broadcasted_iota(jnp.int32, (dp * wide, dp * wide), 0)
+        to_lane = lax.broadcasted_iota(jnp.int32, (dp * wide, dp * wide), 1)
+        spread = (
+            (from_row // (dp * lane) == to_lane // lane % mels)
+            & (from_row // lane % dp == (d ^ (to_lane // wide)))
+            & (from_row % lane == to_lane % lane)
+        ).astype(bf16)
+        from_row = lax.broadcasted_iota(jnp.int32, (chan_in, chan_in), 0)
+        to_lane = lax.broadcasted_iota(jnp.int32, (chan_in, chan_in), 1)
+        sort_in = (
+            (from_row // (dp * lane_in) == to_lane // lane_in % shard)
+            & (from_row // lane_in % dp == (d ^ (to_lane // quarter)))
+            & (from_row % lane_in == to_lane % lane_in)
+        ).astype(bf16)
+
+        pieces_one = weight_in(conv1_weight, place)
+        own_frames = lax.broadcasted_iota(jnp.int32, (clip_count, frames), 1)
+        own_valid = (own_frames < lengths[:, None])[:, :, None, None]
+        masked = clip_maps * own_valid.astype(bf16)
+        sorted_in = [dot(masked[:, :, m].reshape(own_rows, chan_in), sort_in).astype(bf16) for m in range(mels)]
+        from_dp = []
+        for r in range(dp):
+            at = slice(r * quarter, (r + 1) * quarter)
+            part = jnp.concatenate([v[:, at] for v in sorted_in], axis=1)
+            from_dp.append(other_dp(part, r) if r else part)
+        group = jnp.concatenate(unswap(from_dp, d), axis=0)
+        maps_in = []
+        for k in range(depth):
+            mine = from_z(group, k) if k else group
+            maps_in.append(jnp.concatenate(core_order(mine, other_core(mine), c), axis=0))
+        wide_one = expand_weight(pieces_one, table_one, spread, True)
+
+        notes = jnp.concatenate([labels, lengths[:, None]], axis=1).astype(bf16)
+        notes = jnp.pad(notes, ((0, 0), (0, -(classes + 1) % 128)))
+        notes = gather_small(notes, d, z, c).reshape(clips, notes.shape[1])
+        all_labels = notes[:, :classes].astype(f32)
+        all_lengths = notes[:, classes].astype(jnp.int32)
+        frame_ids = lax.broadcasted_iota(jnp.int32, (clips, frames), 1)
+        valid = (frame_ids < all_lengths[:, None]).astype(f32).reshape(rows, 1)
+        valid_here = roll_to(valid.reshape(depth, step, 1), z, 0).reshape(rows, 1)
+        pixel_count = (jnp.sum(all_lengths) * mels).astype(f32)
+
+        pieces_two = weight_in(conv2_weight, place)
+        wide_two = expand_weight(pieces_two, table_two, spread, False)
+
+        fc_rows = fc1_weight.shape[0]
+        pad = -classes % 128
+        both_fc = jnp.concatenate([fc1_weight, jnp.pad(fc2_weight, ((0, 0), (0, pad)))], axis=1)
+        own_fc = lax.dynamic_slice_in_dim(both_fc, d * lane, lane, axis=0)
+        line = jnp.stack([own_fc] + [from_z(own_fc, k) for k in range(1, depth)])
+        line = roll_to(line, (depth - z) % depth, 0)
+        square = jnp.stack(unswap(gather_dp(line, 0), d), axis=1)
+        full_fc = jnp.stack(core_order(square, other_core(square), c), axis=1)
+        full_fc = full_fc.reshape(chan_mid, both_fc.shape[1])
+        full_fc1, full_fc2 = full_fc[:, : fc1_weight.shape[1]], full_fc[:, fc1_weight.shape[1] :][:, :classes]
+
+        own_start = (s * dp + d) * lane
+
+        def own_channels(vector):
+            own = lax.dynamic_slice_in_dim(vector, own_start, lane)
+            return jnp.concatenate([own] * mels)
+
+        gain_one, shift_one = own_channels(norm1_gain), own_channels(norm1_shift)
+        gain_two, shift_two = own_channels(norm2_gain), own_channels(norm2_shift)
+
+        def scatter_dp(outs):
+            total = outs[0].astype(f32)
+            for r in range(1, dp):
+                total = total + other_dp(outs[r], r).astype(f32)
+            return total
+
+        parts = [scatter_dp(convolve([v], wide_one, [(step, wide)] * dp, name="conv1")) for v in maps_in]
+        first_out = jnp.concatenate(parts, axis=0)
+        normed_one, inv_one = norm_of(first_out, valid_here, pixel_count)
+        pre_one = normed_one * gain_one + shift_one
+        act_one = (jax.nn.silu(pre_one) * valid_here).astype(bf16).reshape(depth, step, wide)
+
+        acts, parts = [], []
+        for p in range(depth):
+            own = pick(act_one, (p - z + depth) % depth)
+            line = [own] + [from_z(own, k) for k in range(1, depth)]
+            acts.append(line + [other_core(v) for v in line])
+            parts.append(scatter_dp(convolve(acts[p], wide_two, [(step, wide)] * dp, name="conv2")))
+        second_out = jnp.concatenate(parts, axis=0)
+        normed_two, inv_two = norm_of(second_out, valid, pixel_count)
+        pre_two = normed_two * gain_two + shift_two
+        sigma_two = jax.nn.sigmoid(pre_two)
+        act_two = pre_two * sigma_two * valid
+        slope_two = (sigma_two + act_two * (1.0 - sigma_two)) * valid
+
+        halves = frames // 2
+        pooled = jnp.sum(act_two.reshape(clips, halves, 2, wide), axis=2)
+        pooled = (pooled[:, :, :lane] + pooled[:, :, lane:]) / (2.0 * mels)
+        half_len = all_lengths // 2
+        half_ids = lax.broadcasted_iota(jnp.int32, (clips, halves), 1)
+        pooled_valid = (half_ids < half_len[:, None]).astype(f32)[:, :, None]
+        half_float = half_len.astype(f32)[:, None]
+        largest = jnp.max(jnp.where(pooled_valid > 0, pooled, -1e30), axis=1, keepdims=True)
+        exp_terms = jnp.exp(pooled - largest) * pooled_valid
+        exp_sum = jnp.sum(exp_terms, axis=1)
+        log_sum = largest[:, 0, :] + jnp.log(exp_sum)
+        mean_time = jnp.sum(pooled * pooled_valid, axis=1) / half_float
+        own_embedding = (log_sum + mean_time).astype(bf16)
+        embedding = gather_small(own_embedding, d, z, c).reshape(dp * shard, clips, lane)
+        embedding = jnp.moveaxis(embedding, 0, 1).reshape(clips, chan_mid)
+        hidden = dot(embedding, full_fc1) + fc1_bias
+        sigma = jax.nn.sigmoid(hidden)
+        gated = (hidden * sigma).astype(bf16)
+        logits = dot(gated, full_fc2) + fc2_bias
+        d_logits = (jax.nn.sigmoid(logits) - all_labels).astype(bf16)
+        d_gated = dot_transpose(d_logits, full_fc2)
+        d_hidden = (d_gated * (sigma + hidden * sigma * (1.0 - sigma))).astype(bf16)
+        own_fc1 = lax.dynamic_slice_in_dim(fc1_weight, d * lane, lane, axis=0)
+        d_embed = dot_transpose(d_hidden, own_fc1)
+        soft = exp_terms / exp_sum[:, None, :]
+        d_pooled = d_embed[:, None, :] * (soft + pooled_valid / half_float[:, :, None])
+
+        own_columns = lax.dynamic_slice_in_dim(embedding, s * fc_rows, fc_rows, axis=1)
+        fc1_grad = dot(own_columns.T, d_hidden)
+        own_columns = lax.dynamic_slice_in_dim(gated, s * fc_rows, fc_rows, axis=1)
+        fc2_grad = dot(own_columns.T, d_logits)
+        fc1_bias_grad = jnp.sum(d_hidden.astype(f32), axis=0)
+        fc2_bias_grad = jnp.sum(d_logits.astype(f32), axis=0)
+        own_logits = lax.dynamic_slice_in_dim(logits, (s * dp + d) * clip_count, clip_count, axis=0)
+
+        d_frames = jnp.concatenate([d_pooled, d_pooled], axis=2) / (2.0 * mels)
+        d_frames = jnp.broadcast_to(d_frames[:, :, None, :], (clips, halves, 2, wide))
+        dz_two = d_frames.reshape(rows, wide) * slope_two
+        shift_two_grad, shift_two_lanes = both_mels(jnp.sum(dz_two, axis=0))
+        gain_two_grad, gain_two_lanes = both_mels(jnp.sum(dz_two * normed_two, axis=0))
+        d_second = (
+            gain_two
+            * inv_two
+            * (dz_two - (shift_two_lanes + normed_two * gain_two_lanes) / pixel_count)
+            * valid
+        ).astype(bf16)
+
+        parts, grads = [], []
+        for p in range(depth):
+            grads.append(gather_dp(d_second[p * step : (p + 1) * step], p % 2))
+            mine, theirs = convolve(grads[p], wide_two, [(depth, step, wide)] * 2, back=True, name="back2")
+            line = mine.astype(f32) + other_core(theirs).astype(f32)
+            total = line[0]
+            for k in range(1, depth):
+                total = total + to_z(line[k].astype(bf16), k).astype(f32)
+            parts.append(total)
+        grad_two = weight_grad(acts, grads, table_two, spread, lane, False, shard, name="grad2")
+        conv2_grad = weight_out(grad_two, place)
+
+        d_act_one = roll_to(jnp.stack(parts), z, 0).reshape(rows, wide)
+        sigma_one = jax.nn.sigmoid(pre_one)
+        dz_one = d_act_one * valid_here * (sigma_one + pre_one * sigma_one * (1.0 - sigma_one))
+        shift_one_grad, shift_one_lanes = both_mels(jnp.sum(dz_one, axis=0))
+        gain_one_grad, gain_one_lanes = both_mels(jnp.sum(dz_one * normed_one, axis=0))
+        d_first = (
+            gain_one
+            * inv_one
+            * (dz_one - (shift_one_lanes + normed_one * gain_one_lanes) / pixel_count)
+            * valid_here
+        ).astype(bf16)
+
+        grads = []
+        total = 0.0
+        for k in range(depth):
+            grads.append(gather_dp(d_first[k * step : (k + 1) * step], k % 2))
+            (out,) = convolve(grads[k], wide_one, [(step, wide_in)], back=True, name="back1")
+            out = out.reshape(2, step // 2, wide_in)
+            line = pick(out, c).astype(f32) + other_core(pick(out, 1 - c)).astype(f32)
+            total = total + (to_z(line.astype(bf16), k).astype(f32) if k else line)
+        grad_one = weight_grad([[v] for v in maps_in], grads, table_one, spread, lane_in, True, shard, name="grad1")
+        conv1_grad = weight_out(grad_one, place)
+
+        total = total.astype(bf16).reshape(dp, own_rows, wide_in)
+        from_dp = [other_dp(pick(total, d ^ r), r) if r else pick(total, d) for r in range(dp)]
+        input_grad = []
+        for m in range(mels):
+            at = slice(m * quarter, (m + 1) * quarter)
+            mixed = jnp.concatenate([v[:, at] for v in from_dp], axis=1)
+            input_grad.append(dot_transpose(mixed, sort_in).reshape(clip_count, frames, chan_in))
+        input_grad = jnp.stack(input_grad, axis=2) * own_valid.astype(f32)
+
+        norm_grads = jnp.stack([gain_one_grad, shift_one_grad, gain_two_grad, shift_two_grad])
+        norm_grads = gather_small(norm_grads, d, z, c).reshape(dp * shard, 4, lane)
+        norm_grads = jnp.moveaxis(norm_grads, 0, 1).reshape(4, chan_mid)
+        return (
+            own_logits,
+            input_grad,
+            conv1_grad,
+            norm_grads[0],
+            norm_grads[1],
+            conv2_grad,
+            norm_grads[2],
+            norm_grads[3],
+            fc1_grad,
+            fc1_bias_grad,
+            fc2_grad,
+            fc2_bias_grad,
+        )
+
+    return on_device
 
 
 def patch_rows(grid_in):
@@ -265,6 +841,8 @@
         P("shard", None),
         P(),
     )
+    dp, shard = mesh.shape["dp"], mesh.shape["shard"]
+    step = make_device(dp, shard) if (dp, shard) == (4, 8) else on_device
     return jax.shard_map(
-        on_device, mesh=mesh, in_specs=in_specs, out_specs=out_specs, check_vma=False
-    )
+        step, mesh=mesh, in_specs=in_specs, out_specs=out_specs, check_vma=False
+    )

time: 3870 us -> 1010 us (0.26)
  waiting for transfers between devices: 3120 us -> 363 us
  starting transfers between devices: 0.57 us -> 256 us
  Pallas kernels: 0 us -> 214 us
  matrix products: 221 us -> 12.5 us
  blocking collectives: 193 us -> 0 us
  local copies, waits for them, and re-layouts: 214 us -> 54.3 us
    reduce_scatter x4 -> x0, waiting for transfers between devices: 2080 us -> none  [the longest x1 1420 us: on_device(): lax.psum_scatter(transpose_dot(patch_two, d_second), 'shard', scatter_dim...]
    all_gather x4 -> x0, waiting for transfers between devices: 822 us -> none  [the longest x1 505 us: on_device(): lax.all_gather(sent[1], 'shard', axis=0, tiled=True)]
    ppermute x0 -> x180, waiting for transfers between devices: none -> 363 us  [permute(): return lax.ppermute(value, axis, [(i, move(i) % size) for i in range(size)])]
    ppermute x0 -> x180, starting transfers between devices: none -> 256 us  [permute(): return lax.ppermute(value, axis, [(i, move(i) % size) for i in range(size)])]
    psum x1 -> x0, waiting for transfers between devices: 219 us -> none  [on_device(): lax.psum(conv1_part.astype(jnp.bfloat16), 'dp').astype(jnp.float32)]
    pallas_call x0 -> x24, Pallas kernels: none -> 214 us  [the longest x16 113 us: convolve(): pl.pallas_call(functools.partial(conv_kernel, len(rows_in), back, None, t...]
    dot_general x12 -> x10, matrix products: 221 us -> 12.5 us  [the longest x6 7.93 us: dot(): return jnp.dot(left, right, preferred_element_type=f32)]
    psum x4 -> x0, blocking collectives: 193 us -> none  [the longest x1 68 us: on_device(): lax.psum((jnp.sum(first_out * pixel_valid, axis=0), jnp.sum(first_out * f...]
  transfers between devices with their start and end apart: 9 -> 180, of which waited for: 6 -> 74; matrix products, arithmetic and copies ran while one was open for 12% -> 12% of each run, Pallas kernels for 0% -> 21%
where the time goes in v2:
time: 1010 us; the launch traced here: 996 us
  waiting for transfers between devices  363 us (36%)
  starting transfers between devices  256 us (25%)
  Pallas kernels  214 us (21%)
  other arithmetic  91.9 us (9%)
  local copies, waits for them, and re-layouts  54.3 us (5%)
  matrix products  12.5 us (1%)
    ppermute x180, waiting for transfers between devices, permute(): return lax.ppermute(value, axis, [(i, move(i) % size) for i in range(size)])  363 us
    ppermute x180, starting transfers between devices, permute(): return lax.ppermute(value, axis, [(i, move(i) % size) for i in range(size)])  256 us
    pallas_call x16, Pallas kernels, convolve(): pl.pallas_call(functools.partial(conv_kernel, len(rows_in), back, None, t...  113 us
    pallas_call x2, Pallas kernels, weight_grad(): pl.pallas_call(functools.partial(grad_kernel, chunks, len(x_chunks[0]), l...  56.8 us
    pallas_call x2, Pallas kernels, join_grad(): pl.pallas_call(functools.partial(join_kernel, dp, shard), grid=(9,), out_...  20.5 us
  transfers between devices with their start and end apart: 180, of which 74 were waited for; matrix products, arithmetic and copies ran while one was open for 12% of the time, Pallas kernels for 21%

profile of v2, /device:TPU:16, one launch (start us, length us, event | category | flops | bytes accessed | tf_op | source)
XLA Modules:
  0.0 996.4 jit_solution(1743134165676539345)
XLA Ops:
  58.9 12.7 %collective-permute-done.13.refs_3_ = bf16[9,32,256]{2,1,0:T(8,128)(2,1)S(1)} collective-permute-done((bf16[9,32,256]{2,1,0:T(8,128)(2,1)}, bf16[9,32,256]{2,1,0:T(8,128)(2,1)S(1)}, u32[]{:S(2)}, u32[]{:S(2)}) %collective-permute-start.13) | collective-permute-done | bytes 147488 | tf_op jit(solution)/shard_map/ppermute | solution.py:294
  78.1 19.7 %collective-permute-done.16.refs_6_ = bf16[9,32,256]{2,1,0:T(8,128)(2,1)S(1)} collective-permute-done((bf16[9,32,256]{2,1,0:T(8,128)(2,1)}, bf16[9,32,256]{2,1,0:T(8,128)(2,1)S(1)}, u32[]{:S(2)}, u32[]{:S(2)}) %collective-permute-start.16) | collective-permute-done | bytes 147488 | tf_op jit(solution)/shard_map/ppermute | solution.py:294
  99.9 8.0 expand_weight.2
  111.6 16.4 %collective-permute-start.10 = (bf16[512,512]{1,0:T(8,128)(2,1)}, bf16[512,512]{1,0:T(8,128)(2,1)S(1)}, u32[]{:S(2)}, u32[]{:S(2)}) collective-permute-start(bf16[512,512]{1,0:T(8,128)(2,1)} %pad_maximum_fusion.13), channel_id=1, source_target_pairs={{0,1},{1,0},{2,3},{3,2},{4,5},{5,4},{6,7},{7,6},{8,9},{9,8},{10,11... | collective-permute-start | bytes 1572872 | tf_op jit(solution)/shard_map/ppermute | solution.py:294
  142.2 7.0 collective-permute-done.26
  156.4 5.7 conv1.7
  167.2 5.8 conv1.6
  174.7 5.8 conv1.5
  201.1 6.2 collective-permute-done.24
  217.6 18.3 %collective-permute-start.39 = (bf16[1024,128]{1,0:T(8,128)(2,1)S(1)}, bf16[1024,128]{1,0:T(8,128)(2,1)S(1)}, u32[]{:S(2)}, u32[]{:S(2)}) collective-permute-start(bf16[1024,128]{1,0:T(8,128)(2,1)S(1)} %get-tuple-element.271.refs_0_), channel_id=1, source_target_pairs={{0,1},{1,0},{2,3},{3,2},{4,5},{5,4},{6,7},{7,6},{8,9},{9,8},{10,11... | collective-permute-start | bytes 786440 | tf_op jit(solution)/shard_map/ppermute | solution.py:294
  238.9 7.7 collective-permute-start.37
  249.0 14.7 %collective-permute-done.38.refs_3_ = bf16[1024,128]{1,0:T(8,128)(2,1)S(1)} collective-permute-done((bf16[1024,128]{1,0:T(8,128)(2,1)S(1)}, bf16[1024,128]{1,0:T(8,128)(2,1)S(1)}, u32[]{:S(2)}, u32[]{:S(2)}) %collective-permute-start.38) | collective-permute-done | bytes 262176 | tf_op jit(solution)/shard_map/ppermute | solution.py:294
  269.2 8.1 collective-permute-done.36.refs_1_
  287.4 12.0 %collective-permute-done.73.refs_1_.refs_25_ = bf16[1024,128]{1,0:T(8,128)(2,1)S(1)} collective-permute-done((bf16[1024,128]{1,0:T(8,128)(2,1)S(1)}, bf16[1024,128]{1,0:T(8,128)(2,1)S(1)}, u32[]{:S(2)}, u32[]{:S(2)}) %collective-permute-start.73) | collective-permute-done | bytes 262176 | tf_op jit(solution)/shard_map/ppermute | solution.py:294
  302.2 6.5 collective-permute-done.65.refs_3_.refs_19_
  325.3 6.0 collective-permute-done.55.refs_3_.refs_11_
  332.1 8.9 expand_weight.3
  344.0 8.1 conv2.7
  353.4 8.2 conv2.6
  363.0 8.1 conv2.5
  375.5 8.3 conv2.4
  385.9 28.3 %collective-permute-done.81 = bf16[1024,128]{1,0:T(8,128)(2,1)} collective-permute-done((bf16[1024,128]{1,0:T(8,128)(2,1)}, bf16[1024,128]{1,0:T(8,128)(2,1)}, u32[]{:S(2)}, u32[]{:S(2)}) %collective-permute-start.81) | collective-permute-done | bytes 262176 | tf_op jit(solution)/shard_map/ppermute | solution.py:294
  442.6 7.3 collective-permute-done.51
  457.1 7.5 collective-permute-start.85
  481.8 6.0 collective-permute-done.88
  546.1 8.5 back2.4
  556.4 32.8 %grad2.1 = bf16[72,64,256]{2,1,0:T(8,128)(2,1)} custom-call(s32[72]{0:T(128)} %get-tuple-element.336.table, bf16[1024,128]{1,0:T(8,128)(2,1)} %copy-done.83, bf16[1024,128]{1,0:T(8,128)(2,1)} %copy-done.174, bf16[1024,128]{1,0:T(8,128)(2,1)} %copy-done.172, bf16[1024,128]{1,0:T(8,128)(2,1)} %copy-done.170, bf16[1024,128]{1,0:T(8,128)(2,1)} %copy-done.169, ...), custom_call_target="tpu_custom_call" | custom-call | flops 12884901888 | bytes 14942208 | tf_op jit(solution)/shard_map/grad2/pallas_call | solution.py:218
  594.2 8.3 back2.5
  602.6 8.3 back2.6
  611.4 8.3 back2.7
  629.0 7.2 collective-permute-start.108
  638.6 14.1 %collective-permute-done.102 = bf16[1024,128]{1,0:T(8,128)(2,1)S(1)} collective-permute-done((bf16[1024,128]{1,0:T(8,128)(2,1)S(1)}, bf16[1024,128]{1,0:T(8,128)(2,1)S(1)}, u32[]{:S(2)}, u32[]{:S(2)}) %collective-permute-start.102) | collective-permute-done | bytes 262176 | tf_op jit(solution)/shard_map/ppermute | solution.py:294
  656.5 6.9 collective-permute-done.108
  678.1 7.9 collective-permute-done.115
  700.6 7.9 collective-permute-done.122
  708.5 9.4 collective-permute-done.124
  717.9 8.8 collective-permute-done.123
  796.4 5.9 back1.7
  804.7 24.1 %grad1.1 = bf16[72,32,256]{2,1,0:T(8,128)(2,1)} custom-call(s32[72]{0:T(128)} %get-tuple-element.337.table, bf16[1024,512]{1,0:T(8,128)(2,1)} %pad_maximum_fusion.6.refs_0_, bf16[1024,512]{1,0:T(8,128)(2,1)} %pad_maximum_fusion.7.refs_0_.refs_1_, bf16[1024,512]{1,0:T(8,128)(2,1)} %pad_maximum_fusion.8.refs_0_.refs_2_, ...), custom_call_target="tpu_custom_call" | custom-call | flops 6442450944 | bytes 9568256 | tf_op jit(solution)/shard_map/grad1/pallas_call | solution.py:218
  831.1 5.9 back1.6
  838.3 10.0 %collective-permute-done.165 = f32[4,2,4,64]{3,2,0,1:T(4,128)S(1)} collective-permute-done((f32[4,2,4,64]{3,2,0,1:T(4,128)S(1)}, f32[4,2,4,64]{3,2,0,1:T(4,128)S(1)}, u32[]{:S(2)}, u32[]{:S(2)}) %collective-permute-start.165) | collective-permute-done | bytes 8224 | tf_op jit(solution)/shard_map/ppermute | solution.py:294
  848.9 6.1 back1.5
  877.1 6.0 back1.4
  900.8 11.3 %collective-permute-done.178.refs_6_ = bf16[4,9,64,256]{3,2,1,0:T(8,128)(2,1)S(1)} collective-permute-done((bf16[4,9,64,256]{3,2,1,0:T(8,128)(2,1)S(1)}, bf16[4,9,64,256]{3,2,1,0:T(8,128)(2,1)S(1)}, u32[]{:S(2)}, u32[]{:S(2)}) %collective-permute-start.178) | collective-permute-done | bytes 1179680 | tf_op jit(solution)/shard_map/ppermute | solution.py:294
  913.4 6.8 collective-permute-done.179.refs_7_
  926.8 11.9 %join_grad.3 = f32[9,4,64,2048]{3,2,1,0:T(8,128)} custom-call(s32[2]{0:T(128)} %pad_add_fusion.place, bf16[4,9,64,256]{3,2,1,0:T(8,128)(2,1)} %copy-done.25, bf16[4,9,64,256]{3,2,1,0:T(8,128)(2,1)} %copy-done.24, bf16[4,9,64,256]{3,2,1,0:T(8,128)(2,1)} %copy-done.34, bf16[4,9,64,256]{3,2,1,0:T(8,128)(2,1)} %copy-done.36, bf16[4,9,64,256]{3,2,1,0:T(8,128)(2,1)} %copy-done.33, ...), custom_call_target="tpu_custom_call" | custom-call | bytes 28311552 | tf_op jit(solution)/shard_map/join_grad/pallas_call | solution.py:245
  954.1 16.7 %collective-permute-done.146 = bf16[128,512]{1,0:T(8,128)(2,1)S(1)} collective-permute-done((bf16[128,512]{1,0:T(8,128)(2,1)S(1)}, bf16[128,512]{1,0:T(8,128)(2,1)S(1)}, u32[]{:S(2)}, u32[]{:S(2)}) %collective-permute-start.146) | collective-permute-done | bytes 131104 | tf_op jit(solution)/shard_map/ppermute | solution.py:294
  987.6 8.6 join_grad.2
  (1025 shorter events, 498.7 us)
Async XLA Ops:
  12.7 38.8 %collective-permute-start.7 = (bf16[128,512]{1,0:T(8,128)(2,1)}, bf16[128,512]{1,0:T(8,128)(2,1)}, u32[]{:S(2)}, u32[]{:S(2)}) collective-permute-start(bf16[128,512]{1,0:T(8,128)(2,1)} %pad_maximum_fusion.16), channel_id=1, source_target_pairs={{0,24},{8,16},{16,8},{24,0},{1,25},{9,17},{17,9},{25,1},{2,26},{10... | collective-permute-start | bytes 393224 | tf_op jit(solution)/shard_map/ppermute | solution.py:294
  15.8 39.3 %collective-permute-start.8 = (bf16[128,512]{1,0:T(8,128)(2,1)}, bf16[128,512]{1,0:T(8,128)(2,1)}, u32[]{:S(2)}, u32[]{:S(2)}) collective-permute-start(bf16[128,512]{1,0:T(8,128)(2,1)} %pad_maximum_fusion.17), channel_id=1, source_target_pairs={{0,16},{8,24},{16,0},{24,8},{1,17},{9,25},{17,1},{25,9},{2,18},{10... | collective-permute-start | bytes 393224 | tf_op jit(solution)/shard_map/ppermute | solution.py:294
  56.9 41.0 %collective-permute-start.16 = (bf16[9,32,256]{2,1,0:T(8,128)(2,1)}, bf16[9,32,256]{2,1,0:T(8,128)(2,1)S(1)}, u32[]{:S(2)}, u32[]{:S(2)}) collective-permute-start(bf16[9,32,256]{2,1,0:T(8,128)(2,1)} %get-tuple-element.74), channel_id=1, source_target_pairs={{0,2},{1,3},{2,4},{3,5},{4,6},{5,7},{6,0},{7,1},{8,10},{9,11},{10,... | collective-permute-start | bytes 442376 | tf_op jit(solution)/shard_map/ppermute | solution.py:294
  58.9 39.4 %collective-permute-start.17 = (bf16[9,32,256]{2,1,0:T(8,128)(2,1)}, bf16[9,32,256]{2,1,0:T(8,128)(2,1)S(1)}, u32[]{:S(2)}, u32[]{:S(2)}) collective-permute-start(bf16[9,32,256]{2,1,0:T(8,128)(2,1)} %get-tuple-element.75), channel_id=1, source_target_pairs={{0,1},{1,2},{2,3},{3,4},{4,5},{5,6},{6,7},{7,0},{8,9},{9,10},{10,1... | collective-permute-start | bytes 442376 | tf_op jit(solution)/shard_map/ppermute | solution.py:294
  71.6 36.3 %collective-permute-start.90 = (bf16[64,2688]{1,0:T(8,128)(2,1)S(1)}, bf16[64,2688]{1,0:T(8,128)(2,1)S(1)}, u32[]{:S(2)}, u32[]{:S(2)}) collective-permute-start(bf16[64,2688]{1,0:T(8,128)(2,1)S(1)} %get-tuple-element.208), channel_id=1, source_target_pairs={{0,6},{1,7},{2,0},{3,1},{4,2},{5,3},{6,4},{7,5},{8,14},{9,15},{10,... | collective-permute-start | bytes 1032200 | tf_op jit(solution)/shard_map/ppermute | solution.py:294
  74.8 36.8 %collective-permute-start.91 = (bf16[64,2688]{1,0:T(8,128)(2,1)S(1)}, bf16[64,2688]{1,0:T(8,128)(2,1)S(1)}, u32[]{:S(2)}, u32[]{:S(2)}) collective-permute-start(bf16[64,2688]{1,0:T(8,128)(2,1)S(1)} %get-tuple-element.208), channel_id=1, source_target_pairs={{0,4},{1,5},{2,6},{3,7},{4,0},{5,1},{6,2},{7,3},{8,12},{9,13},{10,... | collective-permute-start | bytes 1032200 | tf_op jit(solution)/shard_map/ppermute | solution.py:294
  78.1 52.5 %collective-permute-start.92 = (bf16[64,2688]{1,0:T(8,128)(2,1)S(1)}, bf16[64,2688]{1,0:T(8,128)(2,1)S(1)}, u32[]{:S(2)}, u32[]{:S(2)}) collective-permute-start(bf16[64,2688]{1,0:T(8,128)(2,1)S(1)} %get-tuple-element.208), channel_id=1, source_target_pairs={{0,2},{1,3},{2,4},{3,5},{4,6},{5,7},{6,0},{7,1},{8,10},{9,11},{10,... | collective-permute-start | bytes 1032200 | tf_op jit(solution)/shard_map/ppermute | solution.py:294
  97.9 42.8 %collective-permute-start.21 = (bf16[512,512]{1,0:T(8,128)(2,1)}, bf16[512,512]{1,0:T(8,128)(2,1)S(1)}, u32[]{:S(2)}, u32[]{:S(2)}) collective-permute-start(bf16[512,512]{1,0:T(8,128)(2,1)} %pad_maximum_fusion.13), channel_id=1, source_target_pairs={{0,6},{1,7},{2,0},{3,1},{4,2},{5,3},{6,4},{7,5},{8,14},{9,15},{10,... | collective-permute-start | bytes 1572872 | tf_op jit(solution)/shard_map/ppermute | solution.py:294
  98.2 43.6 %collective-permute-start.31 = (bf16[512,512]{1,0:T(8,128)(2,1)}, bf16[512,512]{1,0:T(8,128)(2,1)S(1)}, u32[]{:S(2)}, u32[]{:S(2)}) collective-permute-start(bf16[512,512]{1,0:T(8,128)(2,1)} %pad_maximum_fusion.13), channel_id=1, source_target_pairs={{0,2},{1,3},{2,4},{3,5},{4,6},{5,7},{6,0},{7,1},{8,10},{9,11},{10,... | collective-permute-start | bytes 1572872 | tf_op jit(solution)/shard_map/ppermute | solution.py:294
  107.9 41.4 %collective-permute-start.26 = (bf16[512,512]{1,0:T(8,128)(2,1)}, bf16[512,512]{1,0:T(8,128)(2,1)S(1)}, u32[]{:S(2)}, u32[]{:S(2)}) collective-permute-start(bf16[512,512]{1,0:T(8,128)(2,1)} %pad_maximum_fusion.13), channel_id=1, source_target_pairs={{0,4},{1,5},{2,6},{3,7},{4,0},{5,1},{6,2},{7,3},{8,12},{9,13},{10,... | collective-permute-start | bytes 1572872 | tf_op jit(solution)/shard_map/ppermute | solution.py:294
  149.3 66.7 %collective-permute-start.43 = (bf16[9,64,256]{2,1,0:T(8,128)(2,1)}, bf16[9,64,256]{2,1,0:T(8,128)(2,1)S(1)}, u32[]{:S(2)}, u32[]{:S(2)}) collective-permute-start(bf16[9,64,256]{2,1,0:T(8,128)(2,1)} %get-tuple-element.93), channel_id=1, source_target_pairs={{0,7},{1,0},{2,1},{3,2},{4,3},{5,4},{6,5},{7,6},{8,15},{9,8},{10,9... | collective-permute-start | bytes 884744 | tf_op jit(solution)/shard_map/ppermute | solution.py:294
  152.6 65.0 %collective-permute-start.44 = (bf16[9,64,256]{2,1,0:T(8,128)(2,1)}, bf16[9,64,256]{2,1,0:T(8,128)(2,1)}, u32[]{:S(2)}, u32[]{:S(2)}) collective-permute-start(bf16[9,64,256]{2,1,0:T(8,128)(2,1)} %get-tuple-element.94), channel_id=1, source_target_pairs={{0,6},{1,7},{2,0},{3,1},{4,2},{5,3},{6,4},{7,5},{8,14},{9,15},{10,... | collective-permute-start | bytes 884744 | tf_op jit(solution)/shard_map/ppermute | solution.py:294
  207.3 30.8 %collective-permute-start.46 = (bf16[9,64,256]{2,1,0:T(8,128)(2,1)S(1)}, bf16[9,64,256]{2,1,0:T(8,128)(2,1)S(1)}, u32[]{:S(2)}, u32[]{:S(2)}) collective-permute-start(bf16[9,64,256]{2,1,0:T(8,128)(2,1)S(1)} %copy-done.167), channel_id=1, source_target_pairs={{0,4},{1,5},{2,6},{3,7},{4,0},{5,1},{6,2},{7,3},{8,12},{9,13},{10,... | collective-permute-start | bytes 884744 | tf_op jit(solution)/shard_map/ppermute | solution.py:294
  216.0 30.9 %collective-permute-start.48 = (bf16[9,64,256]{2,1,0:T(8,128)(2,1)S(1)}, bf16[9,64,256]{2,1,0:T(8,128)(2,1)S(1)}, u32[]{:S(2)}, u32[]{:S(2)}) collective-permute-start(bf16[9,64,256]{2,1,0:T(8,128)(2,1)S(1)} %copy-done.165), channel_id=1, source_target_pairs={{0,2},{1,3},{2,4},{3,5},{4,6},{5,7},{6,0},{7,1},{8,10},{9,11},{10,... | collective-permute-start | bytes 884744 | tf_op jit(solution)/shard_map/ppermute | solution.py:294
  217.6 29.4 %collective-permute-start.39 = (bf16[1024,128]{1,0:T(8,128)(2,1)S(1)}, bf16[1024,128]{1,0:T(8,128)(2,1)S(1)}, u32[]{:S(2)}, u32[]{:S(2)}) collective-permute-start(bf16[1024,128]{1,0:T(8,128)(2,1)S(1)} %get-tuple-element.271.refs_0_), channel_id=1, source_target_pairs={{0,1},{1,0},{2,3},{3,2},{4,5},{5,4},{6,7},{7,6},{8,9},{9,8},{10,11... | collective-permute-start | bytes 786440 | tf_op jit(solution)/shard_map/ppermute | solution.py:294
  246.9 30.4 %collective-permute-start.36 = (bf16[1024,128]{1,0:T(8,128)(2,1)S(1)}, bf16[1024,128]{1,0:T(8,128)(2,1)S(1)}, u32[]{:S(2)}, u32[]{:S(2)}) collective-permute-start(bf16[1024,128]{1,0:T(8,128)(2,1)S(1)} %get-tuple-element.271.refs_0_), channel_id=1, source_target_pairs={{0,6},{1,7},{2,0},{3,1},{4,2},{5,3},{6,4},{7,5},{8,14},{9,15},{10,... | collective-permute-start | bytes 786440 | tf_op jit(solution)/shard_map/ppermute | solution.py:294
  246.9 32.9 %collective-permute-start.76 = (bf16[1024,128]{1,0:T(8,128)(2,1)S(1)}, bf16[1024,128]{1,0:T(8,128)(2,1)S(1)}, u32[]{:S(2)}, u32[]{:S(2)}) collective-permute-start(bf16[1024,128]{1,0:T(8,128)(2,1)S(1)} %get-tuple-element.272.refs_0_.refs_24_), channel_id=1, source_target_pairs={{0,1},{1,0},{2,3},{3,2},{4,5},{5,4},{6,7},{7,6},{8,9},{9,8},{10,11... | collective-permute-start | bytes 786440 | tf_op jit(solution)/shard_map/ppermute | solution.py:294
  247.0 33.6 %collective-permute-start.75 = (bf16[1024,128]{1,0:T(8,128)(2,1)S(1)}, bf16[1024,128]{1,0:T(8,128)(2,1)S(1)}, u32[]{:S(2)}, u32[]{:S(2)}) collective-permute-start(bf16[1024,128]{1,0:T(8,128)(2,1)S(1)} %get-tuple-element.272.refs_0_.refs_24_), channel_id=1, source_target_pairs={{0,2},{1,3},{2,4},{3,5},{4,6},{5,7},{6,0},{7,1},{8,10},{9,11},{10,... | collective-permute-start | bytes 786440 | tf_op jit(solution)/shard_map/ppermute | solution.py:294
  267.0 75.6 %collective-permute-start.93 = (bf16[4,64,2688]{2,1,0:T(8,128)(2,1)}, bf16[4,64,2688]{2,1,0:T(8,128)(2,1)}, u32[]{:S(2)}, u32[]{:S(2)}) collective-permute-start(bf16[4,64,2688]{2,1,0:T(8,128)(2,1)} %constant_dynamic-slice_fusion.3), channel_id=1, source_target_pairs={{0,8},{8,0},{16,24},{24,16},{1,9},{9,1},{17,25},{25,17},{2,10},{10... | collective-permute-start | bytes 4128776 | tf_op jit(solution)/shard_map/ppermute | solution.py:294
  341.0 77.5 %collective-permute-start.95 = (bf16[4,64,2688]{2,1,0:T(8,128)(2,1)}, bf16[4,64,2688]{2,1,0:T(8,128)(2,1)S(1)}, u32[]{:S(2)}, u32[]{:S(2)}) collective-permute-start(bf16[4,64,2688]{2,1,0:T(8,128)(2,1)} %constant_dynamic-slice_fusion.3), channel_id=1, source_target_pairs={{0,16},{8,24},{16,0},{24,8},{1,17},{9,25},{17,1},{25,9},{2,18},{10... | collective-permute-start | bytes 4128776 | tf_op jit(solution)/shard_map/ppermute | solution.py:294
  343.3 75.8 %collective-permute-start.94 = (bf16[4,64,2688]{2,1,0:T(8,128)(2,1)}, bf16[4,64,2688]{2,1,0:T(8,128)(2,1)S(1)}, u32[]{:S(2)}, u32[]{:S(2)}) collective-permute-start(bf16[4,64,2688]{2,1,0:T(8,128)(2,1)} %collective-permute-done.93), channel_id=1, source_target_pairs={{0,16},{8,24},{16,0},{24,8},{1,17},{9,25},{17,1},{25,9},{2,18},{10... | collective-permute-start | bytes 4128776 | tf_op jit(solution)/shard_map/ppermute | solution.py:294
  372.7 41.5 %collective-permute-start.81 = (bf16[1024,128]{1,0:T(8,128)(2,1)}, bf16[1024,128]{1,0:T(8,128)(2,1)}, u32[]{:S(2)}, u32[]{:S(2)}) collective-permute-start(bf16[1024,128]{1,0:T(8,128)(2,1)} %get-tuple-element.114), channel_id=1, source_target_pairs={{0,16},{8,24},{16,0},{24,8},{1,17},{9,25},{17,1},{25,9},{2,18},{10... | collective-permute-start | bytes 786440 | tf_op jit(solution)/shard_map/ppermute | solution.py:294
  374.7 41.0 %collective-permute-start.82 = (bf16[1024,128]{1,0:T(8,128)(2,1)}, bf16[1024,128]{1,0:T(8,128)(2,1)}, u32[]{:S(2)}, u32[]{:S(2)}) collective-permute-start(bf16[1024,128]{1,0:T(8,128)(2,1)} %get-tuple-element.115), channel_id=1, source_target_pairs={{0,24},{8,16},{16,8},{24,0},{1,25},{9,17},{17,9},{25,1},{2,26},{10... | collective-permute-start | bytes 786440 | tf_op jit(solution)/shard_map/ppermute | solution.py:294
  384.4 43.4 %collective-permute-start.70 = (bf16[1024,128]{1,0:T(8,128)(2,1)}, bf16[1024,128]{1,0:T(8,128)(2,1)S(1)}, u32[]{:S(2)}, u32[]{:S(2)}) collective-permute-start(bf16[1024,128]{1,0:T(8,128)(2,1)} %get-tuple-element.109), channel_id=1, source_target_pairs={{0,8},{8,0},{16,24},{24,16},{1,9},{9,1},{17,25},{25,17},{2,10},{10... | collective-permute-start | bytes 786440 | tf_op jit(solution)/shard_map/ppermute | solution.py:294
  430.8 62.0 %collective-permute-start.96 = (bf16[4,4,64,2688]{3,2,1,0:T(8,128)(2,1)}, bf16[4,4,64,2688]{3,2,1,0:T(8,128)(2,1)}, u32[]{:S(2)}, u32[]{:S(2)}) collective-permute-start(bf16[4,4,64,2688]{3,2,1,0:T(8,128)(2,1)} %pad_maximum_fusion.1), channel_id=1, source_target_pairs={{0,1},{1,0},{2,3},{3,2},{4,5},{5,4},{6,7},{7,6},{8,9},{9,8},{10,11... | collective-permute-start | bytes 16515080 | tf_op jit(solution)/shard_map/ppermute | solution.py:294
  554.7 65.1 %collective-permute-start.100 = (bf16[4,1024,128]{2,1,0:T(8,128)(2,1)}, bf16[4,1024,128]{2,1,0:T(8,128)(2,1)S(1)}, u32[]{:S(2)}, u32[]{:S(2)}) collective-permute-start(bf16[4,1024,128]{2,1,0:T(8,128)(2,1)} %get-tuple-element.117), channel_id=1, source_target_pairs={{0,1},{1,0},{2,3},{3,2},{4,5},{5,4},{6,7},{7,6},{8,9},{9,8},{10,11... | collective-permute-start | bytes 3145736 | tf_op jit(solution)/shard_map/ppermute | solution.py:294
  592.0 157.1 %collective-permute-start.170 = (bf16[9,64,256]{2,1,0:T(8,128)(2,1)}, bf16[9,64,256]{2,1,0:T(8,128)(2,1)S(1)}, u32[]{:S(2)}, u32[]{:S(2)}) collective-permute-start(bf16[9,64,256]{2,1,0:T(8,128)(2,1)} %get-tuple-element.221), channel_id=1, source_target_pairs={{0,4},{1,5},{2,6},{3,7},{4,0},{5,1},{6,2},{7,3},{8,12},{9,13},{10,... | collective-permute-start | bytes 884744 | tf_op jit(solution)/shard_map/ppermute | solution.py:294
  594.1 155.8 %collective-permute-start.173 = (bf16[9,64,256]{2,1,0:T(8,128)(2,1)}, bf16[9,64,256]{2,1,0:T(8,128)(2,1)S(1)}, u32[]{:S(2)}, u32[]{:S(2)}) collective-permute-start(bf16[9,64,256]{2,1,0:T(8,128)(2,1)} %get-tuple-element.222), channel_id=1, source_target_pairs={{0,1},{1,2},{2,3},{3,4},{4,5},{5,6},{6,7},{7,0},{8,9},{9,10},{10,1... | collective-permute-start | bytes 884744 | tf_op jit(solution)/shard_map/ppermute | solution.py:294
  629.0 34.3 %collective-permute-start.108 = (bf16[1024,128]{1,0:T(8,128)(2,1)S(1)}, bf16[1024,128]{1,0:T(8,128)(2,1)S(1)}, u32[]{:S(2)}, u32[]{:S(2)}) collective-permute-start(bf16[1024,128]{1,0:T(8,128)(2,1)S(1)} %get-tuple-element.261), channel_id=1, source_target_pairs={{0,2},{1,3},{2,4},{3,5},{4,6},{5,7},{6,0},{7,1},{8,10},{9,11},{10,... | collective-permute-start | bytes 786440 | tf_op jit(solution)/shard_map/ppermute | solution.py:294
  637.0 31.9 %collective-permute-start.110 = (bf16[1024,128]{1,0:T(8,128)(2,1)S(1)}, bf16[1024,128]{1,0:T(8,128)(2,1)S(1)}, u32[]{:S(2)}, u32[]{:S(2)}) collective-permute-start(bf16[1024,128]{1,0:T(8,128)(2,1)S(1)} %get-tuple-element.262), channel_id=1, source_target_pairs={{0,6},{1,7},{2,0},{3,1},{4,2},{5,3},{6,4},{7,5},{8,14},{9,15},{10,... | collective-permute-start | bytes 786440 | tf_op jit(solution)/shard_map/ppermute | solution.py:294
  697.1 29.5 %collective-permute-start.123 = (bf16[1024,128]{1,0:T(8,128)(2,1)S(1)}, bf16[1024,128]{1,0:T(8,128)(2,1)S(1)}, u32[]{:S(2)}, u32[]{:S(2)}) collective-permute-start(bf16[1024,128]{1,0:T(8,128)(2,1)S(1)} %get-tuple-element.253), channel_id=1, source_target_pairs={{0,4},{1,5},{2,6},{3,7},{4,0},{5,1},{6,2},{7,3},{8,12},{9,13},{10,... | collective-permute-start | bytes 786440 | tf_op jit(solution)/shard_map/ppermute | solution.py:294
  708.5 45.0 %collective-permute-start.172 = (bf16[9,64,256]{2,1,0:T(8,128)(2,1)S(1)}, bf16[9,64,256]{2,1,0:T(8,128)(2,1)S(1)}, u32[]{:S(2)}, u32[]{:S(2)}) collective-permute-start(bf16[9,64,256]{2,1,0:T(8,128)(2,1)S(1)} %copy-done.70), channel_id=1, source_target_pairs={{0,2},{1,3},{2,4},{3,5},{4,6},{5,7},{6,0},{7,1},{8,10},{9,11},{10,... | collective-permute-start | bytes 884744 | tf_op jit(solution)/shard_map/ppermute | solution.py:294
  717.8 36.6 %collective-permute-start.171 = (bf16[9,64,256]{2,1,0:T(8,128)(2,1)S(1)}, bf16[9,64,256]{2,1,0:T(8,128)(2,1)S(1)}, u32[]{:S(2)}, u32[]{:S(2)}) collective-permute-start(bf16[9,64,256]{2,1,0:T(8,128)(2,1)S(1)} %copy-done.69), channel_id=1, source_target_pairs={{0,3},{1,4},{2,5},{3,6},{4,7},{5,0},{6,1},{7,2},{8,11},{9,12},{10,... | collective-permute-start | bytes 884744 | tf_op jit(solution)/shard_map/ppermute | solution.py:294
  789.7 66.3 %collective-permute-start.176 = (bf16[4,9,64,256]{3,2,1,0:T(8,128)(2,1)S(1)}, bf16[4,9,64,256]{3,2,1,0:T(8,128)(2,1)S(1)}, u32[]{:S(2)}, u32[]{:S(2)}) collective-permute-start(bf16[4,9,64,256]{3,2,1,0:T(8,128)(2,1)S(1)} %pad_maximum_fusion.4.refs_0_), channel_id=1, source_target_pairs={{0,16},{8,24},{16,0},{24,8},{1,17},{9,25},{17,1},{25,9},{2,18},{10... | collective-permute-start | bytes 3538952 | tf_op jit(solution)/shard_map/ppermute | solution.py:294
  792.1 69.5 %collective-permute-start.174 = (bf16[4,9,64,256]{3,2,1,0:T(8,128)(2,1)S(1)}, bf16[4,9,64,256]{3,2,1,0:T(8,128)(2,1)S(1)}, u32[]{:S(2)}, u32[]{:S(2)}) collective-permute-start(bf16[4,9,64,256]{3,2,1,0:T(8,128)(2,1)S(1)} %pad_maximum_fusion.4.refs_0_), channel_id=1, source_target_pairs={{0,8},{8,0},{16,24},{24,16},{1,9},{9,1},{17,25},{25,17},{2,10},{10... | collective-permute-start | bytes 3538952 | tf_op jit(solution)/shard_map/ppermute | solution.py:294
  795.5 69.5 %collective-permute-start.177 = (bf16[4,9,64,256]{3,2,1,0:T(8,128)(2,1)S(1)}, bf16[4,9,64,256]{3,2,1,0:T(8,128)(2,1)S(1)}, u32[]{:S(2)}, u32[]{:S(2)}) collective-permute-start(bf16[4,9,64,256]{3,2,1,0:T(8,128)(2,1)S(1)} %pad_maximum_fusion.5.refs_1_), channel_id=1, source_target_pairs={{0,16},{8,24},{16,0},{24,8},{1,17},{9,25},{17,1},{25,9},{2,18},{10... | collective-permute-start | bytes 3538952 | tf_op jit(solution)/shard_map/ppermute | solution.py:294
  802.4 34.7 %collective-permute-start.166 = (f32[4,2,4,64]{3,2,0,1:T(4,128)S(1)}, f32[4,2,4,64]{3,2,0,1:T(4,128)S(1)}, u32[]{:S(2)}, u32[]{:S(2)}) collective-permute-start(f32[4,2,4,64]{3,2,0,1:T(4,128)S(1)} %pad_maximum_fusion.22), channel_id=1, source_target_pairs={{0,8},{8,0},{16,24},{24,16},{1,9},{9,1},{17,25},{25,17},{2,10},{10... | collective-permute-start | bytes 24584 | tf_op jit(solution)/shard_map/ppermute | solution.py:294
  804.0 44.3 %collective-permute-start.165 = (f32[4,2,4,64]{3,2,0,1:T(4,128)S(1)}, f32[4,2,4,64]{3,2,0,1:T(4,128)S(1)}, u32[]{:S(2)}, u32[]{:S(2)}) collective-permute-start(f32[4,2,4,64]{3,2,0,1:T(4,128)S(1)} %pad_maximum_fusion.22), channel_id=1, source_target_pairs={{0,16},{8,24},{16,0},{24,8},{1,17},{9,25},{17,1},{25,9},{2,18},{10... | collective-permute-start | bytes 24584 | tf_op jit(solution)/shard_map/ppermute | solution.py:294
  884.2 36.0 %collective-permute-start.179 = (bf16[4,9,64,256]{3,2,1,0:T(8,128)(2,1)S(1)}, bf16[4,9,64,256]{3,2,1,0:T(8,128)(2,1)S(1)}, u32[]{:S(2)}, u32[]{:S(2)}) collective-permute-start(bf16[4,9,64,256]{3,2,1,0:T(8,128)(2,1)S(1)} %collective-permute-done.177.refs_5_), channel_id=1, source_target_pairs={{0,8},{8,0},{16,24},{24,16},{1,9},{9,1},{17,25},{25,17},{2,10},{10... | collective-permute-start | bytes 3538952 | tf_op jit(solution)/shard_map/ppermute | solution.py:294
  894.9 43.8 %collective-permute-start.154 = (bf16[4,9,32,256]{3,2,1,0:T(8,128)(2,1)S(1)}, bf16[4,9,32,256]{3,2,1,0:T(8,128)(2,1)S(1)}, u32[]{:S(2)}, u32[]{:S(2)}) collective-permute-start(bf16[4,9,32,256]{3,2,1,0:T(8,128)(2,1)S(1)} %pad_maximum_fusion.11.refs_0_), channel_id=1, source_target_pairs={{0,8},{8,0},{16,24},{24,16},{1,9},{9,1},{17,25},{25,17},{2,10},{10... | collective-permute-start | bytes 1769480 | tf_op jit(solution)/shard_map/ppermute | solution.py:294
  895.7 44.1 %collective-permute-start.157 = (bf16[4,9,32,256]{3,2,1,0:T(8,128)(2,1)S(1)}, bf16[4,9,32,256]{3,2,1,0:T(8,128)(2,1)S(1)}, u32[]{:S(2)}, u32[]{:S(2)}) collective-permute-start(bf16[4,9,32,256]{3,2,1,0:T(8,128)(2,1)S(1)} %pad_maximum_fusion.12.refs_1_), channel_id=1, source_target_pairs={{0,16},{8,24},{16,0},{24,8},{1,17},{9,25},{17,1},{25,9},{2,18},{10... | collective-permute-start | bytes 1769480 | tf_op jit(solution)/shard_map/ppermute | solution.py:294
  898.3 43.0 %collective-permute-start.143 = (bf16[512,512]{1,0:T(8,128)(2,1)}, bf16[512,512]{1,0:T(8,128)(2,1)}, u32[]{:S(2)}, u32[]{:S(2)}) collective-permute-start(bf16[512,512]{1,0:T(8,128)(2,1)} %fusion.32), channel_id=1, source_target_pairs={{0,6},{1,7},{2,0},{3,1},{4,2},{5,3},{6,4},{7,5},{8,14},{9,15},{10,... | collective-permute-start | bytes 1572872 | tf_op jit(solution)/shard_map/ppermute | solution.py:294
  912.1 33.8 %collective-permute-start.138 = (bf16[512,512]{1,0:T(8,128)(2,1)}, bf16[512,512]{1,0:T(8,128)(2,1)}, u32[]{:S(2)}, u32[]{:S(2)}) collective-permute-start(bf16[512,512]{1,0:T(8,128)(2,1)} %fusion.33), channel_id=1, source_target_pairs={{0,4},{1,5},{2,6},{3,7},{4,0},{5,1},{6,2},{7,3},{8,12},{9,13},{10,... | collective-permute-start | bytes 1572872 | tf_op jit(solution)/shard_map/ppermute | solution.py:294
  920.2 30.1 %collective-permute-start.133 = (bf16[512,512]{1,0:T(8,128)(2,1)}, bf16[512,512]{1,0:T(8,128)(2,1)}, u32[]{:S(2)}, u32[]{:S(2)}) collective-permute-start(bf16[512,512]{1,0:T(8,128)(2,1)} %fusion.34), channel_id=1, source_target_pairs={{0,2},{1,3},{2,4},{3,5},{4,6},{5,7},{6,0},{7,1},{8,10},{9,11},{10,... | collective-permute-start | bytes 1572872 | tf_op jit(solution)/shard_map/ppermute | solution.py:294
  938.7 46.7 %collective-permute-start.156 = (bf16[4,9,32,256]{3,2,1,0:T(8,128)(2,1)S(1)}, bf16[4,9,32,256]{3,2,1,0:T(8,128)(2,1)S(1)}, u32[]{:S(2)}, u32[]{:S(2)}) collective-permute-start(bf16[4,9,32,256]{3,2,1,0:T(8,128)(2,1)S(1)} %pad_maximum_fusion.11.refs_0_), channel_id=1, source_target_pairs={{0,16},{8,24},{16,0},{24,8},{1,17},{9,25},{17,1},{25,9},{2,18},{10... | collective-permute-start | bytes 1769480 | tf_op jit(solution)/shard_map/ppermute | solution.py:294
  939.8 45.7 %collective-permute-start.155 = (bf16[4,9,32,256]{3,2,1,0:T(8,128)(2,1)S(1)}, bf16[4,9,32,256]{3,2,1,0:T(8,128)(2,1)S(1)}, u32[]{:S(2)}, u32[]{:S(2)}) collective-permute-start(bf16[4,9,32,256]{3,2,1,0:T(8,128)(2,1)S(1)} %pad_maximum_fusion.12.refs_1_), channel_id=1, source_target_pairs={{0,8},{8,0},{16,24},{24,16},{1,9},{9,1},{17,25},{25,17},{2,10},{10... | collective-permute-start | bytes 1769480 | tf_op jit(solution)/shard_map/ppermute | solution.py:294
  941.3 44.2 %collective-permute-start.158 = (bf16[4,9,32,256]{3,2,1,0:T(8,128)(2,1)S(1)}, bf16[4,9,32,256]{3,2,1,0:T(8,128)(2,1)S(1)}, u32[]{:S(2)}, u32[]{:S(2)}) collective-permute-start(bf16[4,9,32,256]{3,2,1,0:T(8,128)(2,1)S(1)} %collective-permute-done.154.refs_2_), channel_id=1, source_target_pairs={{0,16},{8,24},{16,0},{24,8},{1,17},{9,25},{17,1},{25,9},{2,18},{10... | collective-permute-start | bytes 1769480 | tf_op jit(solution)/shard_map/ppermute | solution.py:294
  945.8 39.7 %collective-permute-start.159 = (bf16[4,9,32,256]{3,2,1,0:T(8,128)(2,1)S(1)}, bf16[4,9,32,256]{3,2,1,0:T(8,128)(2,1)S(1)}, u32[]{:S(2)}, u32[]{:S(2)}) collective-permute-start(bf16[4,9,32,256]{3,2,1,0:T(8,128)(2,1)S(1)} %collective-permute-done.157.refs_5_), channel_id=1, source_target_pairs={{0,8},{8,0},{16,24},{24,16},{1,9},{9,1},{17,25},{25,17},{2,10},{10... | collective-permute-start | bytes 1769480 | tf_op jit(solution)/shard_map/ppermute | solution.py:294
  (361 other events, 5918.3 us)

commit v3 on v2

--- a/solution.py
+++ b/solution.py
@@ -54,19 +54,20 @@
         held[pl.ds(9 * step, 9)] = pieces[step][...]
     part = held.shape[1]
 
-    def one(position, carry):
-        for a in range(3):
-            taps = [held[table[(3 * a + b) * shard + position]] for b in range(3)]
-            for m in range(2):
-                pair = jnp.concatenate([taps[m + 1], taps[m]], axis=1)
-                wide = jnp.dot(pair, spread[...], preferred_element_type=f32).astype(bf16)
+    for a in range(3):
+        taps = [
+            jnp.concatenate([held[table[(3 * a + b) * shard + position]] for position in range(shard)], axis=0)
+            for b in range(3)
+        ]
+        for m in range(2):
+            pair = jnp.concatenate([taps[m + 1], taps[m]], axis=1)
+            wide = jnp.dot(pair, spread[...], preferred_element_type=f32).astype(bf16)
+            for position in range(shard):
+                rows = wide[position * part : (position + 1) * part]
                 if by_mel:
-                    out[a, m, position] = wide
+                    out[a, m, position] = rows
                 else:
-                    out[a, position, pl.ds(m * part, part)] = wide
-        return carry
-
-    lax.fori_loop(0, shard, one, 0)
+                    out[a, position, pl.ds(m * part, part)] = rows
 
 
 def expand_weight(pieces, table, spread, by_mel):
@@ -86,7 +87,7 @@
     return wide.reshape(3, 2 * shard * part, 2 * columns)
 
 
-def conv_kernel(count, back, split, tile, *refs):
+def conv_kernel(count, back, tile, *refs):
     rows_in, taps, outs, (first, last) = refs[:count], refs[count], refs[count + 1 : -2], refs[-2:]
     height = first.shape[0] - 8
     width = first.shape[1]
@@ -135,15 +136,24 @@
     lax.fori_loop(0, height // tile, two, 0)
 
 
-def convolve(rows_in, taps, out_shapes, back=False, tile=256, name="convolve"):
-    height = rows_in[0].shape[-2]
+def whole(shape):
+    return pl.BlockSpec(shape, lambda i: (0,) * len(shape))
+
+
+def convolve(rows_in, taps, out_shapes, back=False, chunk=None, name="convolve"):
+    height = out_shapes[0][-2]
     width = taps.shape[1] if back else taps.shape[2]
-    moved = 2 * (sum(r.size for r in rows_in) + taps.size + sum(math.prod(s) for s in out_shapes))
+    specs = [whole(v.shape) for v in rows_in]
+    if chunk is not None:
+        count, _, lanes = rows_in[0].shape
+        specs = [pl.BlockSpec((count, height, lanes), lambda i: (0, chunk, 0))]
+    moved = 2 * (taps.size + sum(math.prod(s) for s in out_shapes)) + 2 * height * taps.shape[2 if back else 1]
     return pl.pallas_call(
-        functools.partial(conv_kernel, len(rows_in), back, None, tile),
+        functools.partial(conv_kernel, len(rows_in), back, height // 2),
+        grid=(1,),
         out_shape=[jax.ShapeDtypeStruct(s, bf16) for s in out_shapes],
-        in_specs=[VM] * (len(rows_in) + 1),
-        out_specs=[VM] * len(out_shapes),
+        in_specs=specs + [whole(taps.shape)],
+        out_specs=[whole(s) for s in out_shapes],
         scratch_shapes=[pltpu.VMEM((height + 8, width), f32)] * 2,
         compiler_params=params(),
         cost_estimate=cost(2 * height * taps.size, moved),
@@ -151,20 +161,16 @@
     )(*rows_in, taps)
 
 
-def grad_kernel(chunks, x_count, g_count, part, by_mel, shard, tile, table, *refs):
-    n = chunks * x_count
-    x_refs, g_refs = refs[:n], refs[n : n + chunks * g_count]
-    spread, outs = refs[n + chunks * g_count], refs[n + chunks * g_count + 1 : -2]
-    total, moved = refs[-2:]
+def grad_kernel(chunks, x_count, g_count, first, count, by_mel, shard, tile, table, *refs):
+    n, m = chunks * x_count, chunks * g_count
+    x_refs, g_refs = refs[:n], refs[n : n + m]
+    spread = refs[n + m]
+    out, total, moved, done, sem = refs[-5:]
     height = g_refs[0].shape[0]
     half = spread.shape[0] // 2
+    width = 2 * half
+    part = out.shape[1]
     total[...] = jnp.zeros_like(total)
-
-    def block(ref, at):
-        return ref[at] if len(ref.shape) == 2 else jnp.concatenate(
-            [ref[i, at] for i in range(ref.shape[0])], axis=1)
-
-    width = 2 * half
     moved[0:8] = jnp.zeros((8, width), f32)
     moved[height + 8 :] = jnp.zeros((8, width), f32)
     for chunk in range(chunks):
@@ -178,7 +184,12 @@
         def one(i, carry, xs=xs):
             start = pl.multiple_of(i * tile, tile)
             at = pl.ds(start, tile)
-            rows = jnp.concatenate([block(ref, at) for ref in xs], axis=1)
+            if by_mel:
+                rows = jnp.concatenate(
+                    [xs[0][at, (mel * shard + first) * part : (mel * shard + first + count) * part]
+                     for mel in range(2)], axis=1)
+            else:
+                rows = jnp.concatenate([xs[0][i, at] for i in range(count)], axis=1)
             around = moved[pl.ds(start, tile + 16)]
             three = jnp.concatenate(
                 [around[9 - a : 9 - a + tile].astype(bf16) for a in range(3)], axis=1)
@@ -191,40 +202,67 @@
     def fold(position, carry):
         for a in range(3):
             if by_mel:
-                at = [pl.multiple_of((m * shard + position) * part, part) for m in range(2)]
+                at = [pl.multiple_of((mel * count + position) * part, part) for mel in range(2)]
             else:
-                at = [pl.multiple_of((2 * position + m) * part, part) for m in range(2)]
-            rows = [total[pl.ds(start, part), a * width : (a + 1) * width].astype(bf16) for start in at]
+                at = [pl.multiple_of((2 * position + mel) * part, part) for mel in range(2)]
             top, bottom = [
-                lax.dot_general(r, spread[...], (((1,), (1,)), ((), ())), preferred_element_type=f32)
-                for r in rows
+                lax.dot_general(
+                    total[pl.ds(start, part), a * width : (a + 1) * width].astype(bf16),
+                    spread[...], (((1,), (1,)), ((), ())), preferred_element_type=f32)
+                for start in at
             ]
             taps = [top[:, half:], top[:, :half] + bottom[:, half:], bottom[:, :half]]
             for b in range(3):
-                outs[0][table[(3 * a + b) * shard + position]] = taps[b].astype(bf16)
+                done[(3 * a + b) * count + position] = taps[b].astype(bf16)
         return carry
 
-    lax.fori_loop(0, shard, fold, 0)
-
-
-def weight_grad(x_chunks, g_chunks, table, spread, part, by_mel, shard, tile=256, name="weight_grad"):
-    chunks = len(x_chunks)
-    xs = [x for chunk in x_chunks for x in chunk]
+    lax.fori_loop(0, count, fold, 0)
+    copies = [
+        pltpu.make_async_copy(
+            done.at[tap * count + position], out.at[table[tap * shard + first + position]],
+            sem.at[tap * count + position])
+        for tap in range(9) for position in range(count)
+    ]
+    for copy in copies:
+        copy.start()
+    for copy in copies:
+        copy.wait()
+
+
+def weight_grad(x_chunks, g_chunks, table, spread, part, by_mel, shard, first, count, before=None, name="weight_grad"):
+    xs = [v for v, _ in x_chunks]
     gs = [g for chunk in g_chunks for g in chunk]
     height = gs[0].shape[0]
     wide = spread.shape[0]
-    deep = 2 * shard * part
-    flops = 2 * chunks * height * deep * wide * 3
+    deep = 2 * count * part
+    flops = 2 * len(x_chunks) * height * deep * wide * 3
+    inputs = [table] + xs + gs + [spread]
+    specs = [pl.BlockSpec(memory_space=pltpu.SMEM)]
+    for v, row in x_chunks:
+        if by_mel:
+            specs.append(pl.BlockSpec((height, v.shape[1]), lambda i, row=row: (row, 0)))
+        else:
+            specs.append(pl.BlockSpec((count, height, v.shape[2]), lambda i, row=row: (first // count, row, 0)))
+    specs += [whole(v.shape) for v in gs + [spread]]
+    if before is not None:
+        inputs, specs = inputs + [before], specs + [HB]
     return pl.pallas_call(
-        functools.partial(grad_kernel, chunks, len(x_chunks[0]), len(g_chunks[0]), part, by_mel, shard, tile),
+        functools.partial(grad_kernel, len(x_chunks), 1, len(g_chunks[0]), first, count, by_mel, shard, height),
+        grid=(1,),
         out_shape=jax.ShapeDtypeStruct((9 * shard, part, wide // 2), bf16),
-        in_specs=[SM] + [VM] * (len(xs) + len(gs) + 1),
-        out_specs=VM,
-        scratch_shapes=[pltpu.VMEM((deep, 3 * wide), f32), pltpu.VMEM((height + 16, wide), f32)],
+        in_specs=specs,
+        out_specs=HB,
+        input_output_aliases={} if before is None else {len(inputs) - 1: 0},
+        scratch_shapes=[
+            pltpu.VMEM((deep, 3 * wide), f32),
+            pltpu.VMEM((height + 16, wide), f32),
+            pltpu.VMEM((9 * count, part, wide // 2), bf16),
+            pltpu.SemaphoreType.DMA((9 * count,)),
+        ],
         compiler_params=params(),
-        cost_estimate=cost(flops, sum(2 * v.size for v in xs + gs) + 9 * shard * part * wide),
+        cost_estimate=cost(flops, 2 * len(xs) * height * deep + sum(2 * v.size for v in gs) + 9 * count * part * wide),
         name=name,
-    )(table, *xs, *gs, spread)
+    )(*inputs)
 
 
 def join_kernel(dp, shard, place, *refs):
@@ -255,6 +293,128 @@
     return out.reshape(9 * dp * part, shard * width)
 
 
+def valid_rows(frames, lanes, length):
+    return (lax.broadcasted_iota(jnp.int32, (frames, lanes), 0) < length).astype(f32)
+
+
+def pack_maps_kernel(frames, order, offset, length, maps, *refs):
+    outs, (mask, held, packed, flags) = refs[:-4], refs[-4:]
+    step = outs[0].shape[0]
+    held[...] = maps[...].astype(f32)
+    packed[...] = jnp.zeros_like(packed)
+    flags[...] = jnp.zeros_like(flags)
+
+    def one(k, carry):
+        source = pl.ds(pl.multiple_of(order[k] * frames, frames), frames)
+        at = pl.ds(pl.multiple_of(offset[k], 8), frames)
+        packed[at] = held[source]
+        flags[at] = valid_rows(frames, flags.shape[1], length[k])
+        return carry
+
+    lax.fori_loop(0, order.shape[0], one, 0)
+    for p, out in enumerate(outs):
+        out[...] = packed[p * step : (p + 1) * step].astype(bf16)
+    mask[...] = flags[: mask.shape[0]]
+
+
+def pack_maps(maps, packing, frames, height, chunks):
+    rows, lanes = maps.shape
+    *parts, mask = pl.pallas_call(
+        functools.partial(pack_maps_kernel, frames),
+        out_shape=[jax.ShapeDtypeStruct((height // chunks, lanes), bf16)] * chunks
+        + [jax.ShapeDtypeStruct((height, 128), f32)],
+        in_specs=[SM] * 3 + [VM],
+        out_specs=[VM] * (chunks + 1),
+        scratch_shapes=[
+            pltpu.VMEM((rows, lanes), f32),
+            pltpu.VMEM((height + frames, lanes), f32),
+            pltpu.VMEM((height + frames, 128), f32),
+        ],
+        compiler_params=params(),
+        cost_estimate=cost(0, 8 * rows * lanes),
+        name="pack_maps",
+    )(*packing, maps)
+    return parts, mask
+
+
+def unpack_maps_kernel(frames, order, offset, *refs):
+    parts, (out, held, spaced) = refs[:-3], refs[-3:]
+    step = parts[0].shape[0]
+    for p, part in enumerate(parts):
+        held[p * step : (p + 1) * step] = part[...].astype(f32)
+    held[len(parts) * step :] = jnp.zeros((frames, held.shape[1]), f32)
+
+    def one(k, carry):
+        target = pl.ds(pl.multiple_of(order[k] * frames, frames), frames)
+        spaced[target] = held[pl.ds(pl.multiple_of(offset[k], 8), frames)]
+        return carry
+
+    lax.fori_loop(0, order.shape[0], one, 0)
+    out[...] = spaced[...].astype(bf16)
+
+
+def unpack_maps(parts, packing, frames, rows):
+    step, lanes = parts[0].shape
+    return pl.pallas_call(
+        functools.partial(unpack_maps_kernel, frames),
+        out_shape=jax.ShapeDtypeStruct((rows, lanes), bf16),
+        in_specs=[SM] * 2 + [VM] * len(parts),
+        out_specs=VM,
+        scratch_shapes=[
+            pltpu.VMEM((len(parts) * step + frames, lanes), f32),
+            pltpu.VMEM((rows, lanes), f32),
+        ],
+        compiler_params=params(),
+        cost_estimate=cost(0, 8 * rows * lanes),
+        name="unpack_maps",
+    )(*packing[:2], *parts)
+
+
+def unpack_rows_kernel(frames, order, offset, length, value, out, held):
+    height = value.shape[0]
+    held[:height] = value[...]
+    held[height:] = jnp.zeros((frames, held.shape[1]), f32)
+
+    def one(k, carry):
+        target = pl.ds(pl.multiple_of(order[k] * frames, frames), frames)
+        rows = held[pl.ds(pl.multiple_of(offset[k], 8), frames)]
+        out[target] = rows * valid_rows(frames, rows.shape[1], length[k])
+        return carry
+
+    lax.fori_loop(0, order.shape[0], one, 0)
+
+
+def pack_rows_kernel(frames, order, offset, length, value, out, held):
+    held[...] = jnp.zeros_like(held)
+
+    def one(k, carry):
+        rows = value[pl.ds(pl.multiple_of(order[k] * frames, frames), frames)]
+        target = pl.ds(pl.multiple_of(offset[k], 8), frames)
+        held[target] = rows * valid_rows(frames, rows.shape[1], length[k])
+        return carry
+
+    lax.fori_loop(0, order.shape[0], one, 0)
+    out[...] = held[: out.shape[0]]
+
+
+def move_rows(value, packing, frames, height, packed):
+    lanes = value.shape[1]
+    held = height if packed else value.shape[0]
+    return pl.pallas_call(
+        functools.partial(pack_rows_kernel if packed else unpack_rows_kernel, frames),
+        out_shape=jax.ShapeDtypeStruct((height, lanes), f32),
+        in_specs=[SM] * 3 + [VM],
+        out_specs=VM,
+        scratch_shapes=[pltpu.VMEM((held + frames, lanes), f32)],
+        compiler_params=params(),
+        cost_estimate=cost(0, 8 * height * lanes),
+        name="pack_rows" if packed else "unpack_rows",
+    )(*packing, value)
+
+
+under_way_w, under_way_xy, chunks = 7, 3, 4
+
+
 def roll_to(stacked, start, axis):
     size = stacked.shape[axis]
     doubled = jnp.concatenate([stacked, stacked], axis=axis)
@@ -289,55 +449,82 @@
 
 def make_device(dp, shard):
     depth = shard // 2
+    lanes = {}
+
+    def after(value, *earlier):
+        return lax.optimization_barrier((value,) + earlier)[0]
+
+    def queued(lane, value, send, most=2):
+        sent = lanes.setdefault(lane, [])
+        if len(sent) >= most:
+            value = after(value, sent[-most])
+        sent.append(send(value))
+        return sent[-1]
 
     def permute(value, axis, size, move):
         return lax.ppermute(value, axis, [(i, move(i) % size) for i in range(size)])
 
     def from_z(value, k):
-        return permute(value, "shard", shard, lambda i: i - 2 * k)
+        return queued("z", value, lambda v: permute(v, "shard", shard, lambda i: i - 2 * k), under_way_z)
 
     def to_z(value, k):
-        return permute(value, "shard", shard, lambda i: i + 2 * k)
-
-    def from_shard(value, k):
-        return permute(value, "shard", shard, lambda i: i - k)
+        return queued("z", value, lambda v: permute(v, "shard", shard, lambda i: i + 2 * k), under_way_z)
+
+    def from_shard(value, k, *earlier):
+        value = after(value, *earlier)
+        return queued("z", value, lambda v: permute(v, "shard", shard, lambda i: i - k), under_way_w)
 
     def other_core(value):
         return permute(value, "shard", shard, lambda i: i ^ 1)
 
     def other_dp(value, r):
-        return permute(value, "dp", dp, lambda i: i ^ r)
+        return queued("xy", value, lambda v: permute(v, "dp", dp, lambda i: i ^ r), under_way_xy)
 
     def gather_dp(value, order):
         one, two = other_dp(value, 1), other_dp(value, 2)
         three = other_dp(one, 2) if order == 0 else other_dp(two, 1)
         return [value, one, two, three]
 
+    def gather_chunks(values):
+        near = []
+        for p, value in enumerate(values):
+            near.append([value, other_dp(value, 1), other_dp(value, 2)])
+            if p:
+                near[p - 1].append(other_dp(near[p - 1][1 + (p - 1) % 2], 2 - (p - 1) % 2))
+        near[-1].append(other_dp(near[-1][1 + p % 2], 2 - p % 2))
+        return near
+
+    def tied(values, *earlier):
+        return [after(values[0], *earlier)] + list(values[1:])
+
     def unswap(parts, d):
         low = [jnp.where(d % 2 == 1, parts[r ^ 1], parts[r]) for r in range(dp)]
         return [jnp.where(d // 2 == 1, low[r ^ 2], low[r]) for r in range(dp)]
 
+    far = [k for k in range(1, depth) if 2 * k != depth] + [depth // 2]
+
     def core_order(mine, theirs, c):
         return [jnp.where(c == 0, mine, theirs), jnp.where(c == 0, theirs, mine)]
 
     def gather_small(value, d, z, c):
-        line = jnp.stack([value] + [from_z(value, k) for k in range(1, depth)])
-        line = roll_to(line, (depth - z) % depth, 0)
-        pair = jnp.stack(core_order(line, other_core(line), c), axis=1)
-        return jnp.stack(unswap([pair] + [other_dp(pair, r) for r in range(1, dp)], d), axis=2)
-
-    def weight_in(weight, place):
-        pieces = split_weight(weight, place, dp, shard)
-        return [pieces[0]] + [from_shard(pieces[k], k) for k in range(1, shard)]
-
-    def weight_out(grad, place):
-        part, width = grad.shape[1:]
-        pieces = grad.reshape(shard, 9, part, width)
-        parts = [pieces[0]] + [from_shard(pieces[shard - k], k) for k in range(1, shard)]
+        near = [permute(value, "dp", dp, lambda i, r=r: i ^ r) for r in range(1, dp)]
+        square = jnp.stack(unswap([value] + near, d))
+        far = [permute(square, "shard", shard, lambda i, k=k: i - 2 * k) for k in range(1, depth)]
+        line = roll_to(jnp.stack([square] + far), (depth - z) % depth, 0)
+        return jnp.stack(core_order(line, other_core(line), c), axis=1)
+
+    def weight_in(pieces, done=()):
+        done = dict(done)
+        return [pieces[0]] + [from_shard(pieces[k], k, *done.get(k, ())) for k in range(1, shard)]
+
+    def send_grad(grad, done=()):
+        done = dict(done)
+        pieces = grad.reshape((shard, 9) + grad.shape[1:])
+        return [pieces[0]] + [from_shard(pieces[shard - k], k, *done.get(k, ())) for k in range(1, shard)]
+
+    def near_grad(parts):
         half = shard // 2
-        low = gather_dp(jnp.stack(parts[:half]), 0)
-        high = gather_dp(jnp.stack(parts[half:]), 1)
-        return join_grad([h for pair in zip(low, high) for h in pair], place, dp, shard)
+        return [gather_dp(jnp.stack(parts[:half]), 0), gather_dp(jnp.stack(parts[half:]), 1)]
 
     def on_device(
         clip_maps,
@@ -354,6 +541,7 @@
         fc2_weight,
         fc2_bias,
     ):
+        lanes.clear()
         d, s = lax.axis_index("dp"), lax.axis_index("shard")
         z, c = s // 2, s % 2
         place = jnp.stack([d, s]).astype(jnp.int32)
@@ -362,7 +550,6 @@
         classes = labels.shape[1]
         clips = clip_count * dp * shard
         rows = clips * frames
-        step = rows // depth
         own_rows = clip_count * frames
         lane = chan_mid // (dp * shard)
         lane_in = chan_in // (dp * shard)
@@ -377,8 +564,7 @@
             group = tap * shard + block
             return (((group // 9 - s + shard) % shard) * 9 + group % 9).reshape(9 * shard).astype(jnp.int32)
 
-        table_one = table_of(position)
-        table_two = table_of(2 * ((z + position % depth) % depth) + (c ^ (position // depth)))
+        table = table_of(position)
 
         from_row = lax.broadcasted_iota(jnp.int32, (dp * wide, dp * wide), 0)
         to_lane = lax.broadcasted_iota(jnp.int32, (dp * wide, dp * wide), 1)
@@ -395,9 +581,10 @@
             & (from_row % lane_in == to_lane % lane_in)
         ).astype(bf16)
 
-        pieces_one = weight_in(conv1_weight, place)
+        pieces_one = weight_in(split_weight(conv1_weight, place, dp, shard))
         own_frames = lax.broadcasted_iota(jnp.int32, (clip_count, frames), 1)
         own_valid = (own_frames < lengths[:, None])[:, :, None, None]
+        clip_maps = after(clip_maps, pieces_one[0])
         masked = clip_maps * own_valid.astype(bf16)
         sorted_in = [dot(masked[:, :, m].reshape(own_rows, chan_in), sort_in).astype(bf16) for m in range(mels)]
         from_dp = []
@@ -406,178 +593,233 @@
             part = jnp.concatenate([v[:, at] for v in sorted_in], axis=1)
             from_dp.append(other_dp(part, r) if r else part)
         group = jnp.concatenate(unswap(from_dp, d), axis=0)
-        maps_in = []
-        for k in range(depth):
-            mine = from_z(group, k) if k else group
-            maps_in.append(jnp.concatenate(core_order(mine, other_core(mine), c), axis=0))
-        wide_one = expand_weight(pieces_one, table_one, spread, True)
-
-        notes = jnp.concatenate([labels, lengths[:, None]], axis=1).astype(bf16)
-        notes = jnp.pad(notes, ((0, 0), (0, -(classes + 1) % 128)))
-        notes = gather_small(notes, d, z, c).reshape(clips, notes.shape[1])
-        all_labels = notes[:, :classes].astype(f32)
-        all_lengths = notes[:, classes].astype(jnp.int32)
-        frame_ids = lax.broadcasted_iota(jnp.int32, (clips, frames), 1)
-        valid = (frame_ids < all_lengths[:, None]).astype(f32).reshape(rows, 1)
-        valid_here = roll_to(valid.reshape(depth, step, 1), z, 0).reshape(rows, 1)
+        all_maps = lax.all_gather(group, "shard", tiled=True)
+        wide_one = expand_weight(pieces_one, table, spread, True)
+        split_two = split_weight(after(conv2_weight, from_dp[1]), place, dp, shard)
+
+        all_lengths = gather_small(lengths, d, z, c).reshape(clips)
+        kinds = jnp.stack([all_lengths > frames // 2, (all_lengths > frames // 4) & (all_lengths <= frames // 2), all_lengths <= frames // 4])
+        kinds = kinds.astype(jnp.int32)
+        taken = jnp.array([frames, frames // 2, frames // 4], jnp.int32)[:, None]
+        before = lax.broadcasted_iota(jnp.int32, (clips, clips), 0) < lax.broadcasted_iota(jnp.int32, (clips, clips), 1)
+        among = jnp.sum(kinds[:, :, None] * before.astype(jnp.int32)[None], axis=1)
+        number = jnp.sum(kinds, axis=1, keepdims=True)
+        first_rank = jnp.concatenate([jnp.zeros((1, 1), jnp.int32), number[:1], number[:1] + number[1:2]])
+        used = number * taken
+        first_row = jnp.concatenate([jnp.zeros((1, 1), jnp.int32), used[:1], used[:1] + used[1:2]])
+        rank = jnp.sum(kinds * (first_rank + among), axis=0)
+        start = jnp.sum(kinds * (first_row + among * taken), axis=0)
+        ranked = (rank[None, :] == lax.broadcasted_iota(jnp.int32, (clips, clips), 0)).astype(jnp.int32)
+        clip_ids = lax.broadcasted_iota(jnp.int32, (clips,), 0)
+        packing = [jnp.sum(ranked * v[None, :], axis=1) for v in (clip_ids, start, all_lengths)]
         pixel_count = (jnp.sum(all_lengths) * mels).astype(f32)
 
-        pieces_two = weight_in(conv2_weight, place)
-        wide_two = expand_weight(pieces_two, table_two, spread, False)
-
-        fc_rows = fc1_weight.shape[0]
-        pad = -classes % 128
-        both_fc = jnp.concatenate([fc1_weight, jnp.pad(fc2_weight, ((0, 0), (0, pad)))], axis=1)
-        own_fc = lax.dynamic_slice_in_dim(both_fc, d * lane, lane, axis=0)
-        line = jnp.stack([own_fc] + [from_z(own_fc, k) for k in range(1, depth)])
-        line = roll_to(line, (depth - z) % depth, 0)
-        square = jnp.stack(unswap(gather_dp(line, 0), d), axis=1)
-        full_fc = jnp.stack(core_order(square, other_core(square), c), axis=1)
-        full_fc = full_fc.reshape(chan_mid, both_fc.shape[1])
-        full_fc1, full_fc2 = full_fc[:, : fc1_weight.shape[1]], full_fc[:, fc1_weight.shape[1] :][:, :classes]
-
-        own_start = (s * dp + d) * lane
-
-        def own_channels(vector):
-            own = lax.dynamic_slice_in_dim(vector, own_start, lane)
-            return jnp.concatenate([own] * mels)
-
-        gain_one, shift_one = own_channels(norm1_gain), own_channels(norm1_shift)
-        gain_two, shift_two = own_channels(norm2_gain), own_channels(norm2_shift)
-
-        def scatter_dp(outs):
-            total = outs[0].astype(f32)
-            for r in range(1, dp):
-                total = total + other_dp(outs[r], r).astype(f32)
-            return total
-
-        parts = [scatter_dp(convolve([v], wide_one, [(step, wide)] * dp, name="conv1")) for v in maps_in]
-        first_out = jnp.concatenate(parts, axis=0)
-        normed_one, inv_one = norm_of(first_out, valid_here, pixel_count)
-        pre_one = normed_one * gain_one + shift_one
-        act_one = (jax.nn.silu(pre_one) * valid_here).astype(bf16).reshape(depth, step, wide)
-
-        acts, parts = [], []
-        for p in range(depth):
-            own = pick(act_one, (p - z + depth) % depth)
-            line = [own] + [from_z(own, k) for k in range(1, depth)]
-            acts.append(line + [other_core(v) for v in line])
-            parts.append(scatter_dp(convolve(acts[p], wide_two, [(step, wide)] * dp, name="conv2")))
-        second_out = jnp.concatenate(parts, axis=0)
-        normed_two, inv_two = norm_of(second_out, valid, pixel_count)
-        pre_two = normed_two * gain_two + shift_two
-        sigma_two = jax.nn.sigmoid(pre_two)
-        act_two = pre_two * sigma_two * valid
-        slope_two = (sigma_two + act_two * (1.0 - sigma_two)) * valid
-
-        halves = frames // 2
-        pooled = jnp.sum(act_two.reshape(clips, halves, 2, wide), axis=2)
-        pooled = (pooled[:, :, :lane] + pooled[:, :, lane:]) / (2.0 * mels)
-        half_len = all_lengths // 2
-        half_ids = lax.broadcasted_iota(jnp.int32, (clips, halves), 1)
-        pooled_valid = (half_ids < half_len[:, None]).astype(f32)[:, :, None]
-        half_float = half_len.astype(f32)[:, None]
-        largest = jnp.max(jnp.where(pooled_valid > 0, pooled, -1e30), axis=1, keepdims=True)
-        exp_terms = jnp.exp(pooled - largest) * pooled_valid
-        exp_sum = jnp.sum(exp_terms, axis=1)
-        log_sum = largest[:, 0, :] + jnp.log(exp_sum)
-        mean_time = jnp.sum(pooled * pooled_valid, axis=1) / half_float
-        own_embedding = (log_sum + mean_time).astype(bf16)
-        embedding = gather_small(own_embedding, d, z, c).reshape(dp * shard, clips, lane)
-        embedding = jnp.moveaxis(embedding, 0, 1).reshape(clips, chan_mid)
-        hidden = dot(embedding, full_fc1) + fc1_bias
-        sigma = jax.nn.sigmoid(hidden)
-        gated = (hidden * sigma).astype(bf16)
-        logits = dot(gated, full_fc2) + fc2_bias
-        d_logits = (jax.nn.sigmoid(logits) - all_labels).astype(bf16)
-        d_gated = dot_transpose(d_logits, full_fc2)
-        d_hidden = (d_gated * (sigma + hidden * sigma * (1.0 - sigma))).astype(bf16)
-        own_fc1 = lax.dynamic_slice_in_dim(fc1_weight, d * lane, lane, axis=0)
-        d_embed = dot_transpose(d_hidden, own_fc1)
-        soft = exp_terms / exp_sum[:, None, :]
-        d_pooled = d_embed[:, None, :] * (soft + pooled_valid / half_float[:, :, None])
-
-        own_columns = lax.dynamic_slice_in_dim(embedding, s * fc_rows, fc_rows, axis=1)
-        fc1_grad = dot(own_columns.T, d_hidden)
-        own_columns = lax.dynamic_slice_in_dim(gated, s * fc_rows, fc_rows, axis=1)
-        fc2_grad = dot(own_columns.T, d_logits)
-        fc1_bias_grad = jnp.sum(d_hidden.astype(f32), axis=0)
-        fc2_bias_grad = jnp.sum(d_logits.astype(f32), axis=0)
-        own_logits = lax.dynamic_slice_in_dim(logits, (s * dp + d) * clip_count, clip_count, axis=0)
-
-        d_frames = jnp.concatenate([d_pooled, d_pooled], axis=2) / (2.0 * mels)
-        d_frames = jnp.broadcast_to(d_frames[:, :, None, :], (clips, halves, 2, wide))
-        dz_two = d_frames.reshape(rows, wide) * slope_two
-        shift_two_grad, shift_two_lanes = both_mels(jnp.sum(dz_two, axis=0))
-        gain_two_grad, gain_two_lanes = both_mels(jnp.sum(dz_two * normed_two, axis=0))
-        d_second = (
-            gain_two
-            * inv_two
-            * (dz_two - (shift_two_lanes + normed_two * gain_two_lanes) / pixel_count)
-            * valid
-        ).astype(bf16)
-
-        parts, grads = [], []
-        for p in range(depth):
-            grads.append(gather_dp(d_second[p * step : (p + 1) * step], p % 2))
-            mine, theirs = convolve(grads[p], wide_two, [(depth, step, wide)] * 2, back=True, name="back2")
-            line = mine.astype(f32) + other_core(theirs).astype(f32)
-            total = line[0]
-            for k in range(1, depth):
-                total = total + to_z(line[k].astype(bf16), k).astype(f32)
-            parts.append(total)
-        grad_two = weight_grad(acts, grads, table_two, spread, lane, False, shard, name="grad2")
-        conv2_grad = weight_out(grad_two, place)
-
-        d_act_one = roll_to(jnp.stack(parts), z, 0).reshape(rows, wide)
-        sigma_one = jax.nn.sigmoid(pre_one)
-        dz_one = d_act_one * valid_here * (sigma_one + pre_one * sigma_one * (1.0 - sigma_one))
-        shift_one_grad, shift_one_lanes = both_mels(jnp.sum(dz_one, axis=0))
-        gain_one_grad, gain_one_lanes = both_mels(jnp.sum(dz_one * normed_one, axis=0))
-        d_first = (
-            gain_one
-            * inv_one
-            * (dz_one - (shift_one_lanes + normed_one * gain_one_lanes) / pixel_count)
-            * valid_here
-        ).astype(bf16)
-
-        grads = []
-        total = 0.0
-        for k in range(depth):
-            grads.append(gather_dp(d_first[k * step : (k + 1) * step], k % 2))
-            (out,) = convolve(grads[k], wide_one, [(step, wide_in)], back=True, name="back1")
-            out = out.reshape(2, step // 2, wide_in)
-            line = pick(out, c).astype(f32) + other_core(pick(out, 1 - c)).astype(f32)
-            total = total + (to_z(line.astype(bf16), k).astype(f32) if k else line)
-        grad_one = weight_grad([[v] for v in maps_in], grads, table_one, spread, lane_in, True, shard, name="grad1")
-        conv1_grad = weight_out(grad_one, place)
-
-        total = total.astype(bf16).reshape(dp, own_rows, wide_in)
-        from_dp = [other_dp(pick(total, d ^ r), r) if r else pick(total, d) for r in range(dp)]
-        input_grad = []
-        for m in range(mels):
-            at = slice(m * quarter, (m + 1) * quarter)
-            mixed = jnp.concatenate([v[:, at] for v in from_dp], axis=1)
-            input_grad.append(dot_transpose(mixed, sort_in).reshape(clip_count, frames, chan_in))
-        input_grad = jnp.stack(input_grad, axis=2) * own_valid.astype(f32)
-
-        norm_grads = jnp.stack([gain_one_grad, shift_one_grad, gain_two_grad, shift_two_grad])
-        norm_grads = gather_small(norm_grads, d, z, c).reshape(dp * shard, 4, lane)
-        norm_grads = jnp.moveaxis(norm_grads, 0, 1).reshape(4, chan_mid)
-        return (
-            own_logits,
-            input_grad,
-            conv1_grad,
-            norm_grads[0],
-            norm_grads[1],
-            conv2_grad,
-            norm_grads[2],
-            norm_grads[3],
-            fc1_grad,
-            fc1_bias_grad,
-            fc2_grad,
-            fc2_bias_grad,
-        )
+        def after_maps(height):
+            lanes.clear()
+            step, half = height // chunks, height // 2
+            def scatter_dp(outs):
+                total = outs[0].astype(f32)
+                for r in range(1, dp):
+                    total = total + other_dp(outs[r], r).astype(f32)
+                return total
+
+            maps_in, valid = pack_maps(all_maps, packing, frames, height, chunks)
+            pieces_two = weight_in(split_two)
+            parts = []
+            for p in range(chunks):
+                value = after(maps_in[p], *[(), (), (), pieces_two[1:2]][p])
+                outs = convolve([value], wide_one, [(step, wide)] * dp, name="conv1")
+                parts.append(scatter_dp(outs))
+            parts = tied(parts, *pieces_two[2:4])
+            first_out = jnp.concatenate(parts, axis=0)
+
+            wide_two = expand_weight(pieces_two, table, spread, False)
+
+            own_start = (s * dp + d) * lane
+
+            def own_channels(vector):
+                own = lax.dynamic_slice_in_dim(vector, own_start, lane)
+                return jnp.concatenate([own] * mels)
+
+            gain_one, shift_one = own_channels(norm1_gain), own_channels(norm1_shift)
+            gain_two, shift_two = own_channels(norm2_gain), own_channels(norm2_shift)
+
+            normed_one, inv_one = norm_of(first_out, valid, pixel_count)
+            pre_one = normed_one * gain_one + shift_one
+            act_one = (jax.nn.silu(pre_one) * valid).astype(bf16)
+            acts = [
+                lax.all_gather(after(act_one[:half], *pieces_two[4:6]), "shard"),
+                lax.all_gather(after(act_one[half:], *pieces_two[6:], wide_two), "shard"),
+            ]
+            pad = -classes % 128
+            some_labels = jnp.pad(labels.astype(bf16), ((0, 0), (0, pad)))
+            some_labels = after(some_labels, act_one)
+            all_labels = gather_small(some_labels, d, z, c)
+            own_fc2 = lax.dynamic_slice_in_dim(jnp.pad(fc2_weight, ((0, 0), (0, pad))), d * lane, lane, axis=0)
+            far = [permute(after(own_fc2, act_one), "shard", shard, lambda i, k=k: i - 2 * k) for k in range(1, depth)]
+            line = roll_to(jnp.stack([own_fc2] + far), (depth - z) % depth, 0)
+            near = [permute(line, "dp", dp, lambda i, r=r: i ^ r) for r in range(1, dp)]
+            square = jnp.stack(unswap([line] + near, d), axis=1)
+            full_fc2 = jnp.stack(core_order(square, other_core(square), c), axis=1)
+            full_fc2 = full_fc2.reshape(chan_mid, classes + pad)[:, :classes]
+            all_labels = all_labels.reshape(clips, classes + pad)[:, :classes].astype(f32)
+            fc_rows = fc1_weight.shape[0]
+            full_fc1 = lax.all_gather(after(fc1_weight, act_one), "shard", tiled=True)
+            parts, outs = [], []
+            for p in range(chunks):
+                value = after(acts[p // 2], *outs[:1])
+                if p >= 2:
+                    value = after(value, parts[p - 2], *((all_labels, full_fc2) if p == 2 else ()))
+                outs = convolve([value], wide_two, [(step, wide)] * dp, chunk=p % 2, name="conv2")
+                parts.append(scatter_dp(outs))
+            second_out = jnp.concatenate(parts, axis=0)
+            normed_two, inv_two = norm_of(second_out, valid, pixel_count)
+            pre_two = normed_two * gain_two + shift_two
+            sigma_two = jax.nn.sigmoid(pre_two)
+            act_two = pre_two * sigma_two * valid
+            slope_two = (sigma_two + act_two * (1.0 - sigma_two)) * valid
+
+            halves = frames // 2
+            act_two = move_rows(act_two, packing, frames, rows, False)
+            pooled = jnp.sum(act_two.reshape(clips, halves, 2, wide), axis=2)
+            pooled = (pooled[:, :, :lane] + pooled[:, :, lane:]) / (2.0 * mels)
+            half_len = all_lengths // 2
+            half_ids = lax.broadcasted_iota(jnp.int32, (clips, halves), 1)
+            pooled_valid = (half_ids < half_len[:, None]).astype(f32)[:, :, None]
+            half_float = half_len.astype(f32)[:, None]
+            largest = jnp.max(jnp.where(pooled_valid > 0, pooled, -1e30), axis=1, keepdims=True)
+            exp_terms = jnp.exp(pooled - largest) * pooled_valid
+            exp_sum = jnp.sum(exp_terms, axis=1)
+            log_sum = largest[:, 0, :] + jnp.log(exp_sum)
+            mean_time = jnp.sum(pooled * pooled_valid, axis=1) / half_float
+            own_embedding = (log_sum + mean_time).astype(bf16)
+            embedding = gather_small(own_embedding.T, d, z, c).reshape(chan_mid, clips)
+            own_columns = lax.dynamic_slice_in_dim(embedding, s * fc_rows, fc_rows, axis=0)
+            embedding = embedding.T
+            hidden = dot(embedding, full_fc1) + fc1_bias
+            sigma = jax.nn.sigmoid(hidden)
+            gated = (hidden * sigma).astype(bf16)
+            logits = dot(gated, full_fc2) + fc2_bias
+            d_logits = (jax.nn.sigmoid(logits) - all_labels).astype(bf16)
+            d_gated = dot_transpose(d_logits, full_fc2)
+            d_hidden = (d_gated * (sigma + hidden * sigma * (1.0 - sigma))).astype(bf16)
+            own_fc1 = lax.dynamic_slice_in_dim(fc1_weight, d * lane, lane, axis=0)
+            d_embed = dot_transpose(d_hidden, own_fc1)
+            soft = exp_terms / exp_sum[:, None, :]
+            d_pooled = d_embed[:, None, :] * (soft + pooled_valid / half_float[:, :, None])
+
+            fc1_grad = dot(own_columns, d_hidden)
+            own_columns = lax.dynamic_slice_in_dim(gated, s * fc_rows, fc_rows, axis=1)
+            fc2_grad = dot(own_columns.T, d_logits)
+            fc1_bias_grad = jnp.sum(d_hidden.astype(f32), axis=0)
+            fc2_bias_grad = jnp.sum(d_logits.astype(f32), axis=0)
+            own_clips = (s * dp + d) * clip_count
+            own_logits = lax.dynamic_slice_in_dim(logits, own_clips, clip_count, axis=0)
+
+            d_frames = jnp.concatenate([d_pooled, d_pooled], axis=2) / (2.0 * mels)
+            d_frames = jnp.broadcast_to(d_frames[:, :, None, :], (clips, halves, 2, wide))
+            dz_two = move_rows(d_frames.reshape(rows, wide), packing, frames, height, True) * slope_two
+            shift_two_grad, shift_two_lanes = both_mels(jnp.sum(dz_two, axis=0))
+            gain_two_grad, gain_two_lanes = both_mels(jnp.sum(dz_two * normed_two, axis=0))
+            d_second = (
+                gain_two
+                * inv_two
+                * (dz_two - (shift_two_lanes + normed_two * gain_two_lanes) / pixel_count)
+                * valid
+            ).astype(bf16)
+
+            grads_two = gather_chunks(list(d_second.reshape(chunks, step, wide)))
+            parts, outs = [], []
+            for p in range(chunks):
+                ready = tied(grads_two[p], *outs[-1:], *(grads_two[p + 1][1:3] if p + 1 < chunks else ()))
+                outs += convolve(ready, wide_two, [(shard, step, wide)], back=True, name="back2")
+                if p % 2:
+                    out = jnp.concatenate(outs[-2:], axis=1)
+                    parts.append(lax.psum_scatter(out, "shard", scatter_dimension=0))
+
+            grad_two = None
+            count = shard // 4
+            act_chunks = [(acts[p // 2], p % 2) for p in range(chunks)]
+            for first in range(0, shard, count):
+                ready = [tied(grads_two[0], outs[-1])] + grads_two[1:]
+                grad_two = weight_grad(
+                    act_chunks, ready, table, spread, lane, False, shard, first, count, grad_two, name="grad2",
+                )
+            sent_two = send_grad(grad_two)
+            parts = tied(parts, grad_two, *sent_two[1:3])
+
+            d_act_one = jnp.concatenate(parts, axis=0).astype(f32)
+            sigma_one = jax.nn.sigmoid(pre_one)
+            dz_one = d_act_one * valid * (sigma_one + pre_one * sigma_one * (1.0 - sigma_one))
+            shift_one_grad, shift_one_lanes = both_mels(jnp.sum(dz_one, axis=0))
+            gain_one_grad, gain_one_lanes = both_mels(jnp.sum(dz_one * normed_one, axis=0))
+            d_first = (
+                gain_one
+                * inv_one
+                * (dz_one - (shift_one_lanes + normed_one * gain_one_lanes) / pixel_count)
+                * valid
+            ).astype(bf16)
+            values = list(d_first.reshape(chunks, step, wide))
+            norm_grads = jnp.stack([gain_one_grad, shift_one_grad, gain_two_grad, shift_two_grad])
+            norm_grads = gather_small(norm_grads, d, z, c)
+            grads_one = gather_chunks(values)
+            outs = []
+            for p in range(chunks):
+                ready = tied(grads_one[p], *outs[-1:], *(grads_one[p + 1][1:3] if p + 1 < chunks else ()))
+                ready = tied(ready, *[(), (norm_grads,), (), ()][p])
+                outs += convolve(ready, wide_one, [(step, wide_in)], back=True, name="back1")
+            near_two = near_grad([after(v, grads_one[-1][3]) for v in sent_two])
+
+            grad_one = None
+            count = shard // 2
+            for first in range(0, shard, count):
+                ready = [tied(grads_one[0], outs[-1], *(near_two[0][1:3] if first else ()))] + grads_one[1:]
+                grad_one = weight_grad(
+                    [(v, 0) for v in maps_in], ready, table, spread, lane_in, True, shard, first, count, grad_one, name="grad1",
+                )
+            d_in = unpack_maps(outs, packing, frames, rows).reshape(shard, rows // shard, wide_in)
+            total = lax.psum_scatter(d_in, "shard", scatter_dimension=0)
+            sent_one = send_grad(grad_one, {1: near_two[0][1:3], 4: near_two[1][1:3]})
+            conv2_grad = join_grad([h for pair in zip(*near_two) for h in pair], place, dp, shard)
+            total = total.reshape(dp, own_rows, wide_in)
+            from_dp = [other_dp(pick(total, d ^ r), r) if r else pick(total, d) for r in range(dp)]
+            near_one = near_grad(sent_one)
+            conv1_grad = join_grad([h for pair in zip(*near_one) for h in pair], place, dp, shard)
+
+            norm_grads = norm_grads.reshape(dp * shard, 4, lane)
+            norm_grads = jnp.moveaxis(norm_grads, 0, 1).reshape(4, chan_mid)
+
+            input_grad = []
+            for m in range(mels):
+                at = slice(m * quarter, (m + 1) * quarter)
+                mixed = jnp.concatenate([v[:, at] for v in from_dp], axis=1)
+                input_grad.append(dot_transpose(mixed, sort_in).reshape(clip_count, frames, chan_in))
+            input_grad = jnp.stack(input_grad, axis=2) * own_valid.astype(f32)
+
+            return (
+                own_logits,
+                input_grad,
+                conv1_grad,
+                norm_grads[0],
+                norm_grads[1],
+                conv2_grad,
+                norm_grads[2],
+                norm_grads[3],
+                fc1_grad,
+                fc1_bias_grad,
+                fc2_grad,
+                fc2_bias_grad,
+            )
+
+        def rest(height):
+            def run():
+                return after_maps(height)
+
+            return run
+
+        few = rows * 21 // 32
+        assert few % (32 * chunks) == 0
+        return lax.cond(jnp.sum(used) <= few, rest(few), rest(rows))
 
     return on_device
 

time: 1010 us -> 803 us (0.80)
  starting transfers between devices: 256 us -> 149 us
  waiting for transfers between devices: 363 us -> 317 us
  other arithmetic: 91.9 us -> 51.5 us
  Pallas kernels: 214 us -> 190 us
  local copies, waits for them, and re-layouts: 54.3 us -> 33.5 us
  between operations: 4.56 us -> 19.5 us
    ppermute x180 -> x129, starting transfers between devices: 256 us -> 149 us  [permute(): return lax.ppermute(value, axis, [(i, move(i) % size) for i in range(size)])]
    ppermute x180 -> x129, waiting for transfers between devices: 363 us -> 315 us  [permute(): return lax.ppermute(value, axis, [(i, move(i) % size) for i in range(size)])]
    unnamed x485 -> x57, local copies, waits for them, and re-layouts: 18 us -> 1.87 us
    pallas_call x18 -> x26, Pallas kernels: 170 us -> 155 us  [the longest x16 80.3 us: convolve(): pl.pallas_call(functools.partial(conv_kernel, len(rows_in), back, height...]
    convert_element_type x14 -> x11, other arithmetic: 20.9 us -> 6.67 us  [the longest x1 4.34 us: on_device(): sort_in = ((from_row // (dp * lane_in) == to_lane // lane_in % shard) & (...]
    another operation x26 -> x29, other arithmetic: 21.8 us -> 10.1 us  [the longest x2 2.61 us: after_maps(): square = jnp.stack(unswap([line] + near, d), axis=1)]
    cond x0 -> x275, local copies, waits for them, and re-layouts: none -> 11.5 us
  transfers between devices with their start and end apart: 180 -> 136, of which waited for: 74 -> 57; matrix products, arithmetic and copies ran while one was open for 12% -> 8% of each run, Pallas kernels for 21% -> 20%
where the time goes in v3:
time: 803 us; the launch traced here: 788 us
  waiting for transfers between devices  317 us (39%)
  Pallas kernels  190 us (24%)
  starting transfers between devices  149 us (19%)
  other arithmetic  51.5 us (6%)
  local copies, waits for them, and re-layouts  33.5 us (4%)
  between operations  19.5 us (2%)
  matrix products  17.2 us (2%)
  loops' own time  9.87 us (1%)
    ppermute x129, waiting for transfers between devices, permute(): return lax.ppermute(value, axis, [(i, move(i) % size) for i in range(size)])  315 us
    ppermute x129, starting transfers between devices, permute(): return lax.ppermute(value, axis, [(i, move(i) % size) for i in range(size)])  149 us
    pallas_call x16, Pallas kernels, convolve(): pl.pallas_call(functools.partial(conv_kernel, len(rows_in), back, height...  80.3 us
    pallas_call x6, Pallas kernels, weight_grad(): pl.pallas_call(functools.partial(grad_kernel, len(x_chunks), 1, len(g_chu...  53.9 us
    pallas_call x2, Pallas kernels, join_grad(): pl.pallas_call(functools.partial(join_kernel, dp, shard), grid=(9,), out_...  20.6 us
  transfers between devices with their start and end apart: 136, of which 57 were waited for; matrix products, arithmetic and copies ran while one was open for 8% of the time, Pallas kernels for 20%

profile of v3, /device:TPU:16, one launch (start us, length us, event | category | flops | bytes accessed | tf_op | source)
XLA Modules:
  0.0 787.8 jit_solution(11802564255037170692)
XLA Ops:
  36.6 27.1 %collective-permute-done.227 = s32[4,4]{1,0:T(4,128)S(1)} collective-permute-done((s32[4,4]{1,0:T(4,128)S(1)}, s32[4,4]{1,0:T(4,128)S(1)}, u32[]{:S(2)}, u32[]{:S(2)}) %collective-permute-start.227) | collective-permute-done | bytes 96 | tf_op jit(solution)/shard_map/ppermute | solution.py:465
  63.7 4.6 collective-permute-done.228
  97.6 681.8 %conditional.1 = (f32[1152,2048]{1,0:T(8,128)}, f32[2048]{0:T(1024)S(1)}, f32[2048]{0:T(1024)S(1)}, f32[2304,2048]{1,0:T(8,128)}, f32[2048]{0:T(1024)S(1)}, /*in...) conditional(s32[]{:T(128)} %convert_element_type.354, ...), branch_computations={%region_10.28_spmd, %region_28.46_spmd} | conditional | flops 62064443392 | bytes 806988032 | solution.py:822
  108.0 6.7 pack_maps.3
  157.1 8.5 %collective-permute-done.125 = bf16[672,128]{1,0:T(8,128)(2,1)S(1)} collective-permute-done((bf16[672,128]{1,0:T(8,128)(2,1)}, bf16[672,128]{1,0:T(8,128)(2,1)S(1)}, u32[]{:S(2)}, u32[]{:S(2)}) %collective-permute-start.125) | collective-permute-done | bytes 172064 | tf_op jit(solution)/shard_map/cond/branch_1_fun/ppermute | solution.py:465
  168.5 10.2 %collective-permute-done.130.refs_7_ = bf16[9,64,256]{2,1,0:T(8,128)(2,1)S(1)} collective-permute-done((bf16[9,64,256]{2,1,0:T(8,128)(2,1)}, bf16[9,64,256]{2,1,0:T(8,128)(2,1)S(1)}, u32[]{:S(2)}, u32[]{:S(2)}) %collective-permute-start.130) | collective-permute-done | bytes 294944 | tf_op jit(solution)/shard_map/cond/branch_1_fun/ppermute | solution.py:465
  182.7 5.2 expand_weight.4
  201.2 6.9 collective-permute-done.140
  208.4 4.5 collective-permute-done.142
  213.0 5.1 collective-permute-start.143
  223.6 6.3 collective-permute-done.149
  229.9 6.1 collective-permute-done.148
  238.4 6.0 conv2.12
  247.9 6.0 conv2.13
  258.4 6.1 conv2.14
  269.3 6.0 conv2.15
  280.5 4.8 collective-permute-done.156
  295.7 5.1 reduce_sum.303
  315.8 19.0 %collective-permute-done.160 = bf16[4,64,128]{1,2,0:T(8,128)(2,1)S(1)} collective-permute-done((bf16[4,64,128]{1,2,0:T(8,128)(2,1)S(1)}, bf16[4,64,128]{1,2,0:T(8,128)(2,1)S(1)}, u32[]{:S(2)}, u32[]{:S(2)}) %collective-permute-start.160) | collective-permute-done | bytes 65568 | tf_op jit(solution)/shard_map/cond/branch_1_fun/ppermute | solution.py:465
  341.2 5.1 fusion.48
  382.3 6.4 back2.12
  389.4 6.4 back2.13
  401.9 4.5 collective-permute-done.172.refs_1_.refs_17_
  407.8 6.5 back2.14
  414.9 6.4 back2.15
  424.5 8.2 %grad2.12.refs_21_ = bf16[72,64,256]{2,1,0:T(8,128)(2,1)} custom-call(s32[72]{0:T(128)S(1)} %copy-done.209, bf16[8,1344,128]{2,1,0:T(8,128)(2,1)} %bitcast.404, bf16[8,1344,128]{2,1,0:T(8,128)(2,1)} %bitcast.405, bf16[8,1344,128]{2,1,0:T(8,128)(2,1)} %bitcast.414, bf16[8,1344,128]{2,1,0:T(8,128)(2,1)} %bitcast.415, bf16[672,128]{1,0:T(8,128)(2,1)} %copy-done.42, ...), custom_call_target="tpu_custom_call" | custom-call | flops 2113929216 | bytes 4718592 | tf_op jit(solution)/shard_map/cond/branch_1_fun/grad2/pallas_call | solution.py:249
  432.7 8.1 %grad2.13.refs_21_ = bf16[72,64,256]{2,1,0:T(8,128)(2,1)} custom-call(s32[72]{0:T(128)S(1)} %copy-done.209, bf16[8,1344,128]{2,1,0:T(8,128)(2,1)} %bitcast.406, bf16[8,1344,128]{2,1,0:T(8,128)(2,1)} %bitcast.407, bf16[8,1344,128]{2,1,0:T(8,128)(2,1)} %bitcast.416, bf16[8,1344,128]{2,1,0:T(8,128)(2,1)} %bitcast.417, ...), custom_call_target="tpu_custom_call", output_to_operand_aliasing={{}: (22, {})} | custom-call | flops 2113929216 | bytes 4718592 | tf_op jit(solution)/shard_map/cond/branch_1_fun/grad2/pallas_call | solution.py:249
  440.9 8.2 %grad2.14.refs_21_ = bf16[72,64,256]{2,1,0:T(8,128)(2,1)} custom-call(s32[72]{0:T(128)S(1)} %copy-done.209, bf16[8,1344,128]{2,1,0:T(8,128)(2,1)} %bitcast.408, bf16[8,1344,128]{2,1,0:T(8,128)(2,1)} %bitcast.409, bf16[8,1344,128]{2,1,0:T(8,128)(2,1)} %bitcast.418, bf16[8,1344,128]{2,1,0:T(8,128)(2,1)} %bitcast.419, ...), custom_call_target="tpu_custom_call", output_to_operand_aliasing={{}: (22, {})} | custom-call | flops 2113929216 | bytes 4718592 | tf_op jit(solution)/shard_map/cond/branch_1_fun/grad2/pallas_call | solution.py:249
  449.0 8.2 %grad2.15 = bf16[72,64,256]{2,1,0:T(8,128)(2,1)} custom-call(s32[72]{0:T(128)S(1)} %copy-done.209, bf16[8,1344,128]{2,1,0:T(8,128)(2,1)} %bitcast.410, bf16[8,1344,128]{2,1,0:T(8,128)(2,1)} %bitcast.411, bf16[8,1344,128]{2,1,0:T(8,128)(2,1)} %bitcast.420, bf16[8,1344,128]{2,1,0:T(8,128)(2,1)} %bitcast.421, ...), custom_call_target="tpu_custom_call", output_to_operand_aliasing={{}: (22, {})} | custom-call | flops 2113929216 | bytes 4718592 | tf_op jit(solution)/shard_map/cond/branch_1_fun/grad2/pallas_call | solution.py:249
  462.8 9.1 %collective-permute-done.176 = bf16[9,64,256]{2,1,0:T(8,128)(2,1)} collective-permute-done((bf16[9,64,256]{2,1,0:T(8,128)(2,1)S(1)}, bf16[9,64,256]{2,1,0:T(8,128)(2,1)}, u32[]{:S(2)}, u32[]{:S(2)}) %collective-permute-start.176) | collective-permute-done | bytes 294944 | tf_op jit(solution)/shard_map/cond/branch_1_fun/ppermute | solution.py:465
  471.9 8.9 %collective-permute-done.177 = bf16[9,64,256]{2,1,0:T(8,128)(2,1)} collective-permute-done((bf16[9,64,256]{2,1,0:T(8,128)(2,1)S(1)}, bf16[9,64,256]{2,1,0:T(8,128)(2,1)}, u32[]{:S(2)}, u32[]{:S(2)}) %collective-permute-start.177) | collective-permute-done | bytes 294944 | tf_op jit(solution)/shard_map/cond/branch_1_fun/ppermute | solution.py:465
  537.2 5.8 unpack_maps.3
  544.0 16.5 %collective-permute-done.201 = bf16[9,64,256]{2,1,0:T(8,128)(2,1)S(1)} collective-permute-done((bf16[9,64,256]{2,1,0:T(8,128)(2,1)S(1)}, bf16[9,64,256]{2,1,0:T(8,128)(2,1)S(1)}, u32[]{:S(2)}, u32[]{:S(2)}) %collective-permute-start.201) | collective-permute-done | bytes 294944 | tf_op jit(solution)/shard_map/cond/branch_1_fun/ppermute | solution.py:465
  563.6 4.9 collective-permute-start.198
  568.5 11.2 %collective-permute-done.200 = bf16[9,64,256]{2,1,0:T(8,128)(2,1)S(1)} collective-permute-done((bf16[9,64,256]{2,1,0:T(8,128)(2,1)S(1)}, bf16[9,64,256]{2,1,0:T(8,128)(2,1)S(1)}, u32[]{:S(2)}, u32[]{:S(2)}) %collective-permute-start.200) | collective-permute-done | bytes 294944 | tf_op jit(solution)/shard_map/cond/branch_1_fun/ppermute | solution.py:465
  580.2 24.1 %collective-permute-done.198 = bf16[9,64,256]{2,1,0:T(8,128)(2,1)S(1)} collective-permute-done((bf16[9,64,256]{2,1,0:T(8,128)(2,1)S(1)}, bf16[9,64,256]{2,1,0:T(8,128)(2,1)S(1)}, u32[]{:S(2)}, u32[]{:S(2)}) %collective-permute-start.198) | collective-permute-done | bytes 294944 | tf_op jit(solution)/shard_map/cond/branch_1_fun/ppermute | solution.py:465
  604.4 9.3 %collective-permute-done.197 = bf16[9,64,256]{2,1,0:T(8,128)(2,1)S(1)} collective-permute-done((bf16[9,64,256]{2,1,0:T(8,128)(2,1)S(1)}, bf16[9,64,256]{2,1,0:T(8,128)(2,1)S(1)}, u32[]{:S(2)}, u32[]{:S(2)}) %collective-permute-start.197) | collective-permute-done | bytes 294944 | tf_op jit(solution)/shard_map/cond/branch_1_fun/ppermute | solution.py:465
  617.9 10.7 %grad1.6.refs_21_ = bf16[72,32,256]{2,1,0:T(8,128)(2,1)} custom-call(s32[72]{0:T(128)S(1)} %copy-done.209, bf16[672,512]{1,0:T(8,128)(2,1)} %get-tuple-element.318.refs_0_, bf16[672,512]{1,0:T(8,128)(2,1)} %get-tuple-element.327.refs_0_.refs_1_, bf16[672,512]{1,0:T(8,128)(2,1)} %get-tuple-element.335.refs_0_.refs_2_, ...), custom_call_target="tpu_custom_call" | custom-call | flops 2113929216 | bytes 4718592 | tf_op jit(solution)/shard_map/cond/branch_1_fun/grad1/pallas_call | solution.py:249
  628.6 10.6 %grad1.7 = bf16[72,32,256]{2,1,0:T(8,128)(2,1)} custom-call(s32[72]{0:T(128)S(1)} %copy-done.209, bf16[672,512]{1,0:T(8,128)(2,1)} %get-tuple-element.318.refs_0_, bf16[672,512]{1,0:T(8,128)(2,1)} %get-tuple-element.327.refs_0_.refs_1_, bf16[672,512]{1,0:T(8,128)(2,1)} %get-tuple-element.335.refs_0_.refs_2_, ...), custom_call_target="tpu_custom_call", output_to_operand_aliasing={{}: (22, {})} | custom-call | flops 2113929216 | bytes 4718592 | tf_op jit(solution)/shard_map/cond/branch_1_fun/grad1/pallas_call | solution.py:249
  645.6 20.5 %collective-permute-done.206.refs_5_ = bf16[4,9,64,256]{3,2,1,0:T(8,128)(2,1)} collective-permute-done((bf16[4,9,64,256]{3,2,1,0:T(8,128)(2,1)S(1)}, bf16[4,9,64,256]{3,2,1,0:T(8,128)(2,1)}, u32[]{:S(2)}, u32[]{:S(2)}) %collective-permute-start.206) | collective-permute-done | bytes 1179680 | tf_op jit(solution)/shard_map/cond/branch_1_fun/ppermute | solution.py:465
  669.4 6.1 collective-permute-start.213
  683.5 13.3 %collective-permute-done.204 = bf16[128,512]{1,0:T(8,128)(2,1)S(1)} collective-permute-done((bf16[128,512]{1,0:T(8,128)(2,1)S(1)}, bf16[128,512]{1,0:T(8,128)(2,1)S(1)}, u32[]{:S(2)}, u32[]{:S(2)}) %collective-permute-start.204) | collective-permute-done | bytes 131104 | tf_op jit(solution)/shard_map/cond/branch_1_fun/ppermute | solution.py:465
  704.6 6.2 collective-permute-done.214
  711.9 12.1 %join_grad.7 = f32[9,4,64,2048]{3,2,1,0:T(8,128)} custom-call(s32[2]{0:T(128)S(1)} %copy-done.221, bf16[4,9,64,256]{3,2,1,0:T(8,128)(2,1)} %copy-done.39, bf16[4,9,64,256]{3,2,1,0:T(8,128)(2,1)} %copy-done.41, bf16[4,9,64,256]{3,2,1,0:T(8,128)(2,1)} %collective-permute-done.202.refs_2_, bf16[4,9,64,256]{3,2,1,0:T(8,128)(2,1)} %collective-permute-done.203.refs_3_, ...), custom_call_target="tpu_custom_call" | custom-call | bytes 28311552 | tf_op jit(solution)/shard_map/cond/branch_1_fun/join_grad/pallas_call | solution.py:283
  732.7 10.0 %collective-permute-done.221.refs_5_ = bf16[4,9,32,256]{3,2,1,0:T(8,128)(2,1)S(1)} collective-permute-done((bf16[4,9,32,256]{3,2,1,0:T(8,128)(2,1)S(1)}, bf16[4,9,32,256]{3,2,1,0:T(8,128)(2,1)S(1)}, u32[]{:S(2)}, u32[]{:S(2)}) %collective-permute-start.221) | collective-permute-done | bytes 589856 | tf_op jit(solution)/shard_map/cond/branch_1_fun/ppermute | solution.py:465
  742.7 12.2 %collective-permute-done.222.refs_6_ = bf16[4,9,32,256]{3,2,1,0:T(8,128)(2,1)S(1)} collective-permute-done((bf16[4,9,32,256]{3,2,1,0:T(8,128)(2,1)S(1)}, bf16[4,9,32,256]{3,2,1,0:T(8,128)(2,1)S(1)}, u32[]{:S(2)}, u32[]{:S(2)}) %collective-permute-start.222) | collective-permute-done | bytes 589856 | tf_op jit(solution)/shard_map/cond/branch_1_fun/ppermute | solution.py:465
  758.5 11.4 %collective-permute-done.223.refs_7_ = bf16[4,9,32,256]{3,2,1,0:T(8,128)(2,1)S(1)} collective-permute-done((bf16[4,9,32,256]{3,2,1,0:T(8,128)(2,1)S(1)}, bf16[4,9,32,256]{3,2,1,0:T(8,128)(2,1)S(1)}, u32[]{:S(2)}, u32[]{:S(2)}) %collective-permute-start.223) | collective-permute-done | bytes 589856 | tf_op jit(solution)/shard_map/cond/branch_1_fun/ppermute | solution.py:465
  770.8 8.6 %join_grad.6 = f32[9,4,32,2048]{3,2,1,0:T(8,128)} custom-call(s32[2]{0:T(128)S(1)} %copy-done.221, bf16[4,9,32,256]{3,2,1,0:T(8,128)(2,1)} %copy-done.81, bf16[4,9,32,256]{3,2,1,0:T(8,128)(2,1)} %copy-done.83, bf16[4,9,32,256]{3,2,1,0:T(8,128)(2,1)} %copy-done.111, bf16[4,9,32,256]{3,2,1,0:T(8,128)(2,1)} %copy-done.117, bf16[4,9,32,256]{3,2,1,0:T(8,128)(2,1)} %copy-done.109, ...), custom_call_target="tpu_custom_call" | custom-call | bytes 14155776 | tf_op jit(solution)/shard_map/cond/branch_1_fun/join_grad/pallas_call | solution.py:283
  (782 shorter events, 334.7 us)
Async XLA Ops:
  7.2 89.8 %all-gather.24.cloned.1.call-start = ((), (), s32[]{:S(2)}) async-start(), calls=%async_computation.18 | async-start | bytes 4718592 | tf_op jit(solution)/shard_map/all_gather | solution.py:596
  30.8 50.2 %collective-permute-start.235 = (bf16[9,32,256]{2,1,0:T(8,128)(2,1)S(1)}, bf16[9,32,256]{2,1,0:T(8,128)(2,1)S(1)}, u32[]{:S(2)}, u32[]{:S(2)}) collective-permute-start(bf16[9,32,256]{2,1,0:T(8,128)(2,1)S(1)} %copy-done.286), channel_id=1, source_target_pairs={{0,6},{1,7},{2,0},{3,1},{4,2},{5,3},{6,4},{7,5},{8,14},{9,15},{10,... | collective-permute-start | bytes 442376 | tf_op jit(solution)/shard_map/ppermute | solution.py:465
  31.2 51.8 %collective-permute-start.234 = (bf16[9,32,256]{2,1,0:T(8,128)(2,1)S(1)}, bf16[9,32,256]{2,1,0:T(8,128)(2,1)S(1)}, u32[]{:S(2)}, u32[]{:S(2)}) collective-permute-start(bf16[9,32,256]{2,1,0:T(8,128)(2,1)S(1)} %copy-done.285), channel_id=1, source_target_pairs={{0,7},{1,0},{2,1},{3,2},{4,3},{5,4},{6,5},{7,6},{8,15},{9,8},{10,9... | collective-permute-start | bytes 442376 | tf_op jit(solution)/shard_map/ppermute | solution.py:465
  32.8 57.4 %collective-permute-start.236 = (bf16[9,32,256]{2,1,0:T(8,128)(2,1)S(1)}, bf16[9,32,256]{2,1,0:T(8,128)(2,1)S(1)}, u32[]{:S(2)}, u32[]{:S(2)}) collective-permute-start(bf16[9,32,256]{2,1,0:T(8,128)(2,1)S(1)} %copy-done.284), channel_id=1, source_target_pairs={{0,5},{1,6},{2,7},{3,0},{4,1},{5,2},{6,3},{7,4},{8,13},{9,14},{10,... | collective-permute-start | bytes 442376 | tf_op jit(solution)/shard_map/ppermute | solution.py:465
  36.5 53.7 %collective-permute-start.237 = (bf16[9,32,256]{2,1,0:T(8,128)(2,1)S(1)}, bf16[9,32,256]{2,1,0:T(8,128)(2,1)S(1)}, u32[]{:S(2)}, u32[]{:S(2)}) collective-permute-start(bf16[9,32,256]{2,1,0:T(8,128)(2,1)S(1)} %copy-done.283), channel_id=1, source_target_pairs={{0,4},{1,5},{2,6},{3,7},{4,0},{5,1},{6,2},{7,3},{8,12},{9,13},{10,... | collective-permute-start | bytes 442376 | tf_op jit(solution)/shard_map/ppermute | solution.py:465
  36.5 27.2 %collective-permute-start.227 = (s32[4,4]{1,0:T(4,128)S(1)}, s32[4,4]{1,0:T(4,128)S(1)}, u32[]{:S(2)}, u32[]{:S(2)}) collective-permute-start(s32[4,4]{1,0:T(4,128)S(1)} %pad_add_fusion.1), channel_id=1, source_target_pairs={{0,6},{1,7},{2,0},{3,1},{4,2},{5,3},{6,4},{7,5},{8,14},{9,15},{10,... | collective-permute-start | bytes 200 | tf_op jit(solution)/shard_map/ppermute | solution.py:465
  73.9 16.3 %collective-permute-start.238 = (bf16[9,32,256]{2,1,0:T(8,128)(2,1)S(1)}, bf16[9,32,256]{2,1,0:T(8,128)(2,1)S(1)}, u32[]{:S(2)}, u32[]{:S(2)}) collective-permute-start(bf16[9,32,256]{2,1,0:T(8,128)(2,1)S(1)} %copy-done.282), channel_id=1, source_target_pairs={{0,3},{1,4},{2,5},{3,6},{4,7},{5,0},{6,1},{7,2},{8,11},{9,12},{10,... | collective-permute-start | bytes 442376 | tf_op jit(solution)/shard_map/ppermute | solution.py:465
  105.5 132.9 %all-gather.20.cloned.1.call-start = ((), (), s32[]{:S(2)}) async-start(), calls=%async_computation.16 | async-start | bytes 3096576 | tf_op jit(solution)/shard_map/cond/branch_1_fun/all_gather | solution.py:651
  105.6 29.6 %collective-permute-start.123 = (bf16[9,64,256]{2,1,0:T(8,128)(2,1)}, bf16[9,64,256]{2,1,0:T(8,128)(2,1)S(1)}, u32[]{:S(2)}, u32[]{:S(2)}) collective-permute-start(bf16[9,64,256]{2,1,0:T(8,128)(2,1)} %get-tuple-element.344), channel_id=1, source_target_pairs={{0,7},{1,0},{2,1},{3,2},{4,3},{5,4},{6,5},{7,6},{8,15},{9,8},{10,9... | collective-permute-start | bytes 884744 | tf_op jit(solution)/shard_map/cond/branch_1_fun/ppermute | solution.py:465
  106.0 31.6 %collective-permute-start.116 = (bf16[9,64,256]{2,1,0:T(8,128)(2,1)}, bf16[9,64,256]{2,1,0:T(8,128)(2,1)S(1)}, u32[]{:S(2)}, u32[]{:S(2)}) collective-permute-start(bf16[9,64,256]{2,1,0:T(8,128)(2,1)} %get-tuple-element.325), channel_id=1, source_target_pairs={{0,5},{1,6},{2,7},{3,0},{4,1},{5,2},{6,3},{7,4},{8,13},{9,14},{10,... | collective-permute-start | bytes 884744 | tf_op jit(solution)/shard_map/cond/branch_1_fun/ppermute | solution.py:465
  137.7 30.6 %collective-permute-start.128 = (bf16[9,64,256]{2,1,0:T(8,128)(2,1)S(1)}, bf16[9,64,256]{2,1,0:T(8,128)(2,1)}, u32[]{:S(2)}, u32[]{:S(2)}) collective-permute-start(bf16[9,64,256]{2,1,0:T(8,128)(2,1)S(1)} %copy-done.261), channel_id=1, source_target_pairs={{0,3},{1,4},{2,5},{3,6},{4,7},{5,0},{6,1},{7,2},{8,11},{9,12},{10,... | collective-permute-start | bytes 884744 | tf_op jit(solution)/shard_map/cond/branch_1_fun/ppermute | solution.py:465
  137.8 30.5 %collective-permute-start.127 = (bf16[9,64,256]{2,1,0:T(8,128)(2,1)S(1)}, bf16[9,64,256]{2,1,0:T(8,128)(2,1)}, u32[]{:S(2)}, u32[]{:S(2)}) collective-permute-start(bf16[9,64,256]{2,1,0:T(8,128)(2,1)S(1)} %copy-done.259), channel_id=1, source_target_pairs={{0,4},{1,5},{2,6},{3,7},{4,0},{5,1},{6,2},{7,3},{8,12},{9,13},{10,... | collective-permute-start | bytes 884744 | tf_op jit(solution)/shard_map/cond/branch_1_fun/ppermute | solution.py:465
  168.3 85.6 %all-gather.22.cloned.1.call-start = ((), (), s32[]{:S(2)}) async-start(), calls=%async_computation.17 | async-start | bytes 3096576 | tf_op jit(solution)/shard_map/cond/branch_1_fun/all_gather | solution.py:652
  187.9 153.3 %all-gather.18.cloned.1.call-start = ((), (), s32[]{:S(2)}) async-start(), calls=%async_computation.12 | async-start | bytes 9437184 | tf_op jit(solution)/shard_map/cond/branch_1_fun/all_gather | solution.py:667
  188.5 292.3 %reduce-scatter.13.cloned.1.call-start = ((), (), s32[]{:S(2)}) async-start(), calls=%async_computation.13 | async-start | bytes 3096576 | tf_op jit(solution)/shard_map/cond/branch_1_fun/reduce_scatter | solution.py:738
  195.2 22.9 %collective-permute-start.146 = (bf16[64,640]{1,0:T(8,128)(2,1)S(1)}, bf16[64,640]{1,0:T(8,128)(2,1)S(1)}, u32[]{:S(2)}, u32[]{:S(2)}) collective-permute-start(bf16[64,640]{1,0:T(8,128)(2,1)S(1)} %get-tuple-element.387), channel_id=1, source_target_pairs={{0,2},{1,3},{2,4},{3,5},{4,6},{5,7},{6,0},{7,1},{8,10},{9,11},{10,... | collective-permute-start | bytes 245768 | tf_op jit(solution)/shard_map/cond/branch_1_fun/ppermute | solution.py:465
  195.2 22.9 %collective-permute-start.145 = (bf16[64,640]{1,0:T(8,128)(2,1)S(1)}, bf16[64,640]{1,0:T(8,128)(2,1)S(1)}, u32[]{:S(2)}, u32[]{:S(2)}) collective-permute-start(bf16[64,640]{1,0:T(8,128)(2,1)S(1)} %get-tuple-element.387), channel_id=1, source_target_pairs={{0,4},{1,5},{2,6},{3,7},{4,0},{5,1},{6,2},{7,3},{8,12},{9,13},{10,... | collective-permute-start | bytes 245768 | tf_op jit(solution)/shard_map/cond/branch_1_fun/ppermute | solution.py:465
  196.6 21.5 %collective-permute-start.144 = (bf16[64,640]{1,0:T(8,128)(2,1)S(1)}, bf16[64,640]{1,0:T(8,128)(2,1)S(1)}, u32[]{:S(2)}, u32[]{:S(2)}) collective-permute-start(bf16[64,640]{1,0:T(8,128)(2,1)S(1)} %get-tuple-element.387), channel_id=1, source_target_pairs={{0,6},{1,7},{2,0},{3,1},{4,2},{5,3},{6,4},{7,5},{8,14},{9,15},{10,... | collective-permute-start | bytes 245768 | tf_op jit(solution)/shard_map/cond/branch_1_fun/ppermute | solution.py:465
  219.3 16.7 %collective-permute-start.148 = (bf16[4,64,640]{2,1,0:T(8,128)(2,1)}, bf16[4,64,640]{2,1,0:T(8,128)(2,1)}, u32[]{:S(2)}, u32[]{:S(2)}) collective-permute-start(bf16[4,64,640]{2,1,0:T(8,128)(2,1)} %constant_dynamic-slice_fusion.8), channel_id=1, source_target_pairs={{0,16},{8,24},{16,0},{24,8},{1,17},{9,25},{17,1},{25,9},{2,18},{10... | collective-permute-start | bytes 983048 | tf_op jit(solution)/shard_map/cond/branch_1_fun/ppermute | solution.py:465
  219.9 16.1 %collective-permute-start.147 = (bf16[4,64,640]{2,1,0:T(8,128)(2,1)}, bf16[4,64,640]{2,1,0:T(8,128)(2,1)}, u32[]{:S(2)}, u32[]{:S(2)}) collective-permute-start(bf16[4,64,640]{2,1,0:T(8,128)(2,1)} %constant_dynamic-slice_fusion.8), channel_id=1, source_target_pairs={{0,24},{8,16},{16,8},{24,0},{1,25},{9,17},{17,9},{25,1},{2,26},{10... | collective-permute-start | bytes 983048 | tf_op jit(solution)/shard_map/cond/branch_1_fun/ppermute | solution.py:465
  307.9 27.5 %collective-permute-start.150 = (bf16[4,4,64,640]{3,2,1,0:T(8,128)(2,1)S(1)}, bf16[4,4,64,640]{3,2,1,0:T(8,128)(2,1)S(1)}, u32[]{:S(2)}, u32[]{:S(2)}) collective-permute-start(bf16[4,4,64,640]{3,2,1,0:T(8,128)(2,1)S(1)} %pad_maximum_fusion.30), channel_id=1, source_target_pairs={{0,1},{1,0},{2,3},{3,2},{4,5},{5,4},{6,7},{7,6},{8,9},{9,8},{10,11... | collective-permute-start | bytes 3932168 | tf_op jit(solution)/shard_map/cond/branch_1_fun/ppermute | solution.py:465
  311.0 23.8 %collective-permute-start.161 = (bf16[4,64,128]{1,2,0:T(8,128)(2,1)S(1)}, bf16[4,64,128]{1,2,0:T(8,128)(2,1)S(1)}, u32[]{:S(2)}, u32[]{:S(2)}) collective-permute-start(bf16[4,64,128]{1,2,0:T(8,128)(2,1)S(1)} %pad_maximum_fusion.37), channel_id=1, source_target_pairs={{0,4},{1,5},{2,6},{3,7},{4,0},{5,1},{6,2},{7,3},{8,12},{9,13},{10,... | collective-permute-start | bytes 196616 | tf_op jit(solution)/shard_map/cond/branch_1_fun/ppermute | solution.py:465
  313.4 21.4 %collective-permute-start.160 = (bf16[4,64,128]{1,2,0:T(8,128)(2,1)S(1)}, bf16[4,64,128]{1,2,0:T(8,128)(2,1)S(1)}, u32[]{:S(2)}, u32[]{:S(2)}) collective-permute-start(bf16[4,64,128]{1,2,0:T(8,128)(2,1)S(1)} %pad_maximum_fusion.37), channel_id=1, source_target_pairs={{0,6},{1,7},{2,0},{3,1},{4,2},{5,3},{6,4},{7,5},{8,14},{9,15},{10,... | collective-permute-start | bytes 196616 | tf_op jit(solution)/shard_map/cond/branch_1_fun/ppermute | solution.py:465
  313.9 21.1 %collective-permute-start.162 = (bf16[4,64,128]{1,2,0:T(8,128)(2,1)S(1)}, bf16[4,64,128]{1,2,0:T(8,128)(2,1)S(1)}, u32[]{:S(2)}, u32[]{:S(2)}) collective-permute-start(bf16[4,64,128]{1,2,0:T(8,128)(2,1)S(1)} %pad_maximum_fusion.37), channel_id=1, source_target_pairs={{0,2},{1,3},{2,4},{3,5},{4,6},{5,7},{6,0},{7,1},{8,10},{9,11},{10,... | collective-permute-start | bytes 196616 | tf_op jit(solution)/shard_map/cond/branch_1_fun/ppermute | solution.py:465
  398.9 83.9 %reduce-scatter.15.cloned.1.call-start = ((), (), s32[]{:S(2)}) async-start(), calls=%async_computation.14 | async-start | bytes 3096576 | tf_op jit(solution)/shard_map/cond/branch_1_fun/reduce_scatter | solution.py:738
  424.5 251.1 %reduce-scatter.17.cloned.1.call-start = ((), (), s32[]{:S(2)}) async-start(), calls=%async_computation.15 | async-start | bytes 4718592 | tf_op jit(solution)/shard_map/cond/branch_1_fun/reduce_scatter | solution.py:781
  460.2 20.6 %collective-permute-start.177 = (bf16[9,64,256]{2,1,0:T(8,128)(2,1)S(1)}, bf16[9,64,256]{2,1,0:T(8,128)(2,1)}, u32[]{:S(2)}, u32[]{:S(2)}) collective-permute-start(bf16[9,64,256]{2,1,0:T(8,128)(2,1)S(1)} %get-tuple-element.429), channel_id=1, source_target_pairs={{0,6},{1,7},{2,0},{3,1},{4,2},{5,3},{6,4},{7,5},{8,14},{9,15},{10,... | collective-permute-start | bytes 884744 | tf_op jit(solution)/shard_map/cond/branch_1_fun/ppermute | solution.py:465
  544.0 16.5 %collective-permute-start.201 = (bf16[9,64,256]{2,1,0:T(8,128)(2,1)S(1)}, bf16[9,64,256]{2,1,0:T(8,128)(2,1)S(1)}, u32[]{:S(2)}, u32[]{:S(2)}) collective-permute-start(bf16[9,64,256]{2,1,0:T(8,128)(2,1)S(1)} %copy-done.135), channel_id=1, source_target_pairs={{0,5},{1,6},{2,7},{3,0},{4,1},{5,2},{6,3},{7,4},{8,13},{9,14},{10,... | collective-permute-start | bytes 884744 | tf_op jit(solution)/shard_map/cond/branch_1_fun/ppermute | solution.py:465
  561.8 52.1 %collective-permute-start.202 = (bf16[4,9,64,256]{3,2,1,0:T(8,128)(2,1)S(1)}, bf16[4,9,64,256]{3,2,1,0:T(8,128)(2,1)}, u32[]{:S(2)}, u32[]{:S(2)}) collective-permute-start(bf16[4,9,64,256]{3,2,1,0:T(8,128)(2,1)S(1)} %pad_maximum_fusion.31.refs_0_), channel_id=1, source_target_pairs={{0,8},{8,0},{16,24},{24,16},{1,9},{9,1},{17,25},{25,17},{2,10},{10... | collective-permute-start | bytes 3538952 | tf_op jit(solution)/shard_map/cond/branch_1_fun/ppermute | solution.py:465
  561.8 52.3 %collective-permute-start.205 = (bf16[4,9,64,256]{3,2,1,0:T(8,128)(2,1)S(1)}, bf16[4,9,64,256]{3,2,1,0:T(8,128)(2,1)S(1)}, u32[]{:S(2)}, u32[]{:S(2)}) collective-permute-start(bf16[4,9,64,256]{3,2,1,0:T(8,128)(2,1)S(1)} %pad_maximum_fusion.31.refs_0_), channel_id=1, source_target_pairs={{0,16},{8,24},{16,0},{24,8},{1,17},{9,25},{17,1},{25,9},{2,18},{10... | collective-permute-start | bytes 3538952 | tf_op jit(solution)/shard_map/cond/branch_1_fun/ppermute | solution.py:465
  563.5 16.2 %collective-permute-start.200 = (bf16[9,64,256]{2,1,0:T(8,128)(2,1)S(1)}, bf16[9,64,256]{2,1,0:T(8,128)(2,1)S(1)}, u32[]{:S(2)}, u32[]{:S(2)}) collective-permute-start(bf16[9,64,256]{2,1,0:T(8,128)(2,1)S(1)} %copy-done.133), channel_id=1, source_target_pairs={{0,1},{1,2},{2,3},{3,4},{4,5},{5,6},{6,7},{7,0},{8,9},{9,10},{10,1... | collective-permute-start | bytes 884744 | tf_op jit(solution)/shard_map/cond/branch_1_fun/ppermute | solution.py:465
  563.5 16.7 %collective-permute-start.199 = (bf16[9,64,256]{2,1,0:T(8,128)(2,1)S(1)}, bf16[9,64,256]{2,1,0:T(8,128)(2,1)S(1)}, u32[]{:S(2)}, u32[]{:S(2)}) collective-permute-start(bf16[9,64,256]{2,1,0:T(8,128)(2,1)S(1)} %copy-done.131), channel_id=1, source_target_pairs={{0,2},{1,3},{2,4},{3,5},{4,6},{5,7},{6,0},{7,1},{8,10},{9,11},{10,... | collective-permute-start | bytes 884744 | tf_op jit(solution)/shard_map/cond/branch_1_fun/ppermute | solution.py:465
  563.6 40.7 %collective-permute-start.198 = (bf16[9,64,256]{2,1,0:T(8,128)(2,1)S(1)}, bf16[9,64,256]{2,1,0:T(8,128)(2,1)S(1)}, u32[]{:S(2)}, u32[]{:S(2)}) collective-permute-start(bf16[9,64,256]{2,1,0:T(8,128)(2,1)S(1)} %copy-done.129), channel_id=1, source_target_pairs={{0,3},{1,4},{2,5},{3,6},{4,7},{5,0},{6,1},{7,2},{8,11},{9,12},{10,... | collective-permute-start | bytes 884744 | tf_op jit(solution)/shard_map/cond/branch_1_fun/ppermute | solution.py:465
  579.8 33.9 %collective-permute-start.197 = (bf16[9,64,256]{2,1,0:T(8,128)(2,1)S(1)}, bf16[9,64,256]{2,1,0:T(8,128)(2,1)S(1)}, u32[]{:S(2)}, u32[]{:S(2)}) collective-permute-start(bf16[9,64,256]{2,1,0:T(8,128)(2,1)S(1)} %copy-done.127), channel_id=1, source_target_pairs={{0,4},{1,5},{2,6},{3,7},{4,0},{5,1},{6,2},{7,3},{8,12},{9,13},{10,... | collective-permute-start | bytes 884744 | tf_op jit(solution)/shard_map/cond/branch_1_fun/ppermute | solution.py:465
  613.9 31.7 %collective-permute-start.208 = (bf16[4,9,64,256]{3,2,1,0:T(8,128)(2,1)}, bf16[4,9,64,256]{3,2,1,0:T(8,128)(2,1)}, u32[]{:S(2)}, u32[]{:S(2)}) collective-permute-start(bf16[4,9,64,256]{3,2,1,0:T(8,128)(2,1)} %collective-permute-done.202.refs_2_), channel_id=1, source_target_pairs={{0,16},{8,24},{16,0},{24,8},{1,17},{9,25},{17,1},{25,9},{2,18},{10... | collective-permute-start | bytes 3538952 | tf_op jit(solution)/shard_map/cond/branch_1_fun/ppermute | solution.py:465
  615.3 50.9 %collective-permute-start.206 = (bf16[4,9,64,256]{3,2,1,0:T(8,128)(2,1)S(1)}, bf16[4,9,64,256]{3,2,1,0:T(8,128)(2,1)}, u32[]{:S(2)}, u32[]{:S(2)}) collective-permute-start(bf16[4,9,64,256]{3,2,1,0:T(8,128)(2,1)S(1)} %pad_maximum_fusion.32.refs_1_), channel_id=1, source_target_pairs={{0,16},{8,24},{16,0},{24,8},{1,17},{9,25},{17,1},{25,9},{2,18},{10... | collective-permute-start | bytes 3538952 | tf_op jit(solution)/shard_map/cond/branch_1_fun/ppermute | solution.py:465
  617.0 60.3 %collective-permute-start.203 = (bf16[4,9,64,256]{3,2,1,0:T(8,128)(2,1)S(1)}, bf16[4,9,64,256]{3,2,1,0:T(8,128)(2,1)}, u32[]{:S(2)}, u32[]{:S(2)}) collective-permute-start(bf16[4,9,64,256]{3,2,1,0:T(8,128)(2,1)S(1)} %pad_maximum_fusion.32.refs_1_), channel_id=1, source_target_pairs={{0,8},{8,0},{16,24},{24,16},{1,9},{9,1},{17,25},{25,17},{2,10},{10... | collective-permute-start | bytes 3538952 | tf_op jit(solution)/shard_map/cond/branch_1_fun/ppermute | solution.py:465
  641.4 37.2 %collective-permute-start.211 = (bf16[9,32,256]{2,1,0:T(8,128)(2,1)S(1)}, bf16[9,32,256]{2,1,0:T(8,128)(2,1)S(1)}, u32[]{:S(2)}, u32[]{:S(2)}) collective-permute-start(bf16[9,32,256]{2,1,0:T(8,128)(2,1)S(1)} %get-tuple-element.476), channel_id=1, source_target_pairs={{0,7},{1,0},{2,1},{3,2},{4,3},{5,4},{6,5},{7,6},{8,15},{9,8},{10,9... | collective-permute-start | bytes 442376 | tf_op jit(solution)/shard_map/cond/branch_1_fun/ppermute | solution.py:465
  666.1 45.7 %collective-permute-start.209 = (bf16[4,9,64,256]{3,2,1,0:T(8,128)(2,1)}, bf16[4,9,64,256]{3,2,1,0:T(8,128)(2,1)}, u32[]{:S(2)}, u32[]{:S(2)}) collective-permute-start(bf16[4,9,64,256]{3,2,1,0:T(8,128)(2,1)} %collective-permute-done.206.refs_5_), channel_id=1, source_target_pairs={{0,8},{8,0},{16,24},{24,16},{1,9},{9,1},{17,25},{25,17},{2,10},{10... | collective-permute-start | bytes 3538952 | tf_op jit(solution)/shard_map/cond/branch_1_fun/ppermute | solution.py:465
  677.3 19.6 %collective-permute-start.204 = (bf16[128,512]{1,0:T(8,128)(2,1)S(1)}, bf16[128,512]{1,0:T(8,128)(2,1)S(1)}, u32[]{:S(2)}, u32[]{:S(2)}) collective-permute-start(bf16[128,512]{1,0:T(8,128)(2,1)S(1)} %get-tuple-element.463), channel_id=1, source_target_pairs={{0,8},{8,0},{16,24},{24,16},{1,9},{9,1},{17,25},{25,17},{2,10},{10... | collective-permute-start | bytes 393224 | tf_op jit(solution)/shard_map/cond/branch_1_fun/ppermute | solution.py:465
  678.6 18.3 %collective-permute-start.207 = (bf16[128,512]{1,0:T(8,128)(2,1)S(1)}, bf16[128,512]{1,0:T(8,128)(2,1)S(1)}, u32[]{:S(2)}, u32[]{:S(2)}) collective-permute-start(bf16[128,512]{1,0:T(8,128)(2,1)S(1)} %get-tuple-element.466), channel_id=1, source_target_pairs={{0,16},{8,24},{16,0},{24,8},{1,17},{9,25},{17,1},{25,9},{2,18},{10... | collective-permute-start | bytes 393224 | tf_op jit(solution)/shard_map/cond/branch_1_fun/ppermute | solution.py:465
  679.8 19.3 %collective-permute-start.215 = (bf16[9,32,256]{2,1,0:T(8,128)(2,1)}, bf16[9,32,256]{2,1,0:T(8,128)(2,1)}, u32[]{:S(2)}, u32[]{:S(2)}) collective-permute-start(bf16[9,32,256]{2,1,0:T(8,128)(2,1)} %get-tuple-element.481), channel_id=1, source_target_pairs={{0,3},{1,4},{2,5},{3,6},{4,7},{5,0},{6,1},{7,2},{8,11},{9,12},{10,... | collective-permute-start | bytes 442376 | tf_op jit(solution)/shard_map/cond/branch_1_fun/ppermute | solution.py:465
  680.4 19.7 %collective-permute-start.216 = (bf16[9,32,256]{2,1,0:T(8,128)(2,1)}, bf16[9,32,256]{2,1,0:T(8,128)(2,1)}, u32[]{:S(2)}, u32[]{:S(2)}) collective-permute-start(bf16[9,32,256]{2,1,0:T(8,128)(2,1)} %get-tuple-element.482), channel_id=1, source_target_pairs={{0,2},{1,3},{2,4},{3,5},{4,6},{5,7},{6,0},{7,1},{8,10},{9,11},{10,... | collective-permute-start | bytes 442376 | tf_op jit(solution)/shard_map/cond/branch_1_fun/ppermute | solution.py:465
  698.2 27.9 %collective-permute-start.220 = (bf16[4,9,32,256]{3,2,1,0:T(8,128)(2,1)S(1)}, bf16[4,9,32,256]{3,2,1,0:T(8,128)(2,1)S(1)}, u32[]{:S(2)}, u32[]{:S(2)}) collective-permute-start(bf16[4,9,32,256]{3,2,1,0:T(8,128)(2,1)S(1)} %pad_maximum_fusion.34.refs_0_), channel_id=1, source_target_pairs={{0,16},{8,24},{16,0},{24,8},{1,17},{9,25},{17,1},{25,9},{2,18},{10... | collective-permute-start | bytes 1769480 | tf_op jit(solution)/shard_map/cond/branch_1_fun/ppermute | solution.py:465
  698.3 31.8 %collective-permute-start.218 = (bf16[4,9,32,256]{3,2,1,0:T(8,128)(2,1)S(1)}, bf16[4,9,32,256]{3,2,1,0:T(8,128)(2,1)S(1)}, u32[]{:S(2)}, u32[]{:S(2)}) collective-permute-start(bf16[4,9,32,256]{3,2,1,0:T(8,128)(2,1)S(1)} %pad_maximum_fusion.34.refs_0_), channel_id=1, source_target_pairs={{0,8},{8,0},{16,24},{24,16},{1,9},{9,1},{17,25},{25,17},{2,10},{10... | collective-permute-start | bytes 1769480 | tf_op jit(solution)/shard_map/cond/branch_1_fun/ppermute | solution.py:465
  726.1 16.6 %collective-permute-start.221 = (bf16[4,9,32,256]{3,2,1,0:T(8,128)(2,1)S(1)}, bf16[4,9,32,256]{3,2,1,0:T(8,128)(2,1)S(1)}, u32[]{:S(2)}, u32[]{:S(2)}) collective-permute-start(bf16[4,9,32,256]{3,2,1,0:T(8,128)(2,1)S(1)} %pad_maximum_fusion.35.refs_1_), channel_id=1, source_target_pairs={{0,16},{8,24},{16,0},{24,8},{1,17},{9,25},{17,1},{25,9},{2,18},{10... | collective-permute-start | bytes 1769480 | tf_op jit(solution)/shard_map/cond/branch_1_fun/ppermute | solution.py:465
  730.0 24.9 %collective-permute-start.222 = (bf16[4,9,32,256]{3,2,1,0:T(8,128)(2,1)S(1)}, bf16[4,9,32,256]{3,2,1,0:T(8,128)(2,1)S(1)}, u32[]{:S(2)}, u32[]{:S(2)}) collective-permute-start(bf16[4,9,32,256]{3,2,1,0:T(8,128)(2,1)S(1)} %collective-permute-done.218.refs_2_), channel_id=1, source_target_pairs={{0,16},{8,24},{16,0},{24,8},{1,17},{9,25},{17,1},{25,9},{2,18},{10... | collective-permute-start | bytes 1769480 | tf_op jit(solution)/shard_map/cond/branch_1_fun/ppermute | solution.py:465
  731.4 27.1 %collective-permute-start.219 = (bf16[4,9,32,256]{3,2,1,0:T(8,128)(2,1)S(1)}, bf16[4,9,32,256]{3,2,1,0:T(8,128)(2,1)S(1)}, u32[]{:S(2)}, u32[]{:S(2)}) collective-permute-start(bf16[4,9,32,256]{3,2,1,0:T(8,128)(2,1)S(1)} %pad_maximum_fusion.35.refs_1_), channel_id=1, source_target_pairs={{0,8},{8,0},{16,24},{24,16},{1,9},{9,1},{17,25},{25,17},{2,10},{10... | collective-permute-start | bytes 1769480 | tf_op jit(solution)/shard_map/cond/branch_1_fun/ppermute | solution.py:465
  (239 other events, 2918.9 us)
Sparse Core Ops, SparseCore 0:
  27.3 61.3 all-gather.23
  168.5 39.7 all-gather.19
  210.5 34.1 all-gather.21
  246.1 88.9 all-gather.17
  399.0 32.4 reduce-scatter.12
  434.3 48.4 reduce-scatter.14
  543.2 85.0 reduce-scatter.16

commit v4 on v3

--- a/solution.py
+++ b/solution.py
@@ -21,26 +21,28 @@
     return pl.CostEstimate(flops=int(flops), bytes_accessed=int(moved), transcendentals=0)
 
 
-def split_kernel(shard, place, weight, *refs):
-    outs, (own, sem) = refs[:shard], refs[shard:]
+def split_kernel(depth, place, weight, *refs):
+    outs, (own, sem) = refs[:depth], refs[depth:]
     copy = pltpu.make_async_copy(weight.at[:, place[0]], own, sem)
     copy.start()
     copy.wait()
-    for step in range(shard):
-        column = lax.rem(place[1] - step + shard, shard)
-        width = outs[step].shape[2]
-        outs[step][...] = own[:, :, pl.ds(pl.multiple_of(column * width, width), width)]
+    line, core = lax.div(place[1], 2), lax.rem(place[1], 2)
+    for step in range(depth):
+        for other in range(2):
+            column = 2 * lax.rem(line - step + depth, depth) + lax.bitwise_xor(core, other)
+            width = outs[step].shape[3]
+            outs[step][other] = own[:, :, pl.ds(pl.multiple_of(column * width, width), width)]
 
 
 def split_weight(weight, place, dp, shard):
     rows, columns = weight.shape
-    part = rows // (9 * dp)
-    chunk = jax.ShapeDtypeStruct((9, part, columns // shard), bf16)
+    part, depth = rows // (9 * dp), shard // 2
+    chunk = jax.ShapeDtypeStruct((2, 9, part, columns // shard), bf16)
     return pl.pallas_call(
-        functools.partial(split_kernel, shard),
-        out_shape=[chunk] * shard,
+        functools.partial(split_kernel, depth),
+        out_shape=[chunk] * depth,
         in_specs=[SM, HB],
-        out_specs=[VM] * shard,
+        out_specs=[VM] * depth,
         scratch_shapes=[pltpu.VMEM((9, part, columns), bf16), pltpu.SemaphoreType.DMA(())],
         compiler_params=params(),
         cost_estimate=cost(0, 4 * rows * columns // dp),
@@ -49,11 +51,12 @@
 
 
 def expand_kernel(shard, by_mel, table, *refs):
-    pieces, (spread, out, held) = refs[:shard], refs[shard:]
-    for step in range(shard):
-        held[pl.ds(9 * step, 9)] = pieces[step][...]
+    depth = shard // 2
+    pieces, across, (spread, out, held) = refs[:depth], refs[depth], refs[depth + 1 :]
+    for step in range(depth):
+        held[pl.ds(9 * step, 9)] = pieces[step][0]
+        held[pl.ds(9 * (depth + step), 9)] = across[step]
     part = held.shape[1]
-
     for a in range(3):
         taps = [
             jnp.concatenate([held[table[(3 * a + b) * shard + position]] for position in range(shard)], axis=0)
@@ -70,20 +73,20 @@
                     out[a, position, pl.ds(m * part, part)] = rows
 
 
-def expand_weight(pieces, table, spread, by_mel):
-    shard = len(pieces)
-    _, part, columns = pieces[0].shape
+def expand_weight(pieces, across, table, spread, by_mel):
+    shard = 2 * len(pieces)
+    _, _, part, columns = pieces[0].shape
     shape = (3, 2, shard, part, 2 * columns) if by_mel else (3, shard, 2 * part, 2 * columns)
     wide = pl.pallas_call(
         functools.partial(expand_kernel, shard, by_mel),
         out_shape=jax.ShapeDtypeStruct(shape, bf16),
-        in_specs=[SM] + [VM] * (shard + 1),
+        in_specs=[SM] + [VM] * (len(pieces) + 2),
         out_specs=VM,
         scratch_shapes=[pltpu.VMEM((9 * shard, part, columns), bf16)],
         compiler_params=params(),
         cost_estimate=cost(2 * 6 * shard * part * 4 * columns * columns, 30 * shard * part * columns),
         name="expand_weight",
-    )(table, *pieces, spread)
+    )(table, *pieces, across, spread)
     return wide.reshape(3, 2 * shard * part, 2 * columns)
 
 
@@ -265,23 +268,25 @@
     )(*inputs)
 
 
-def join_kernel(dp, shard, place, *refs):
+def join_kernel(dp, depth, place, *refs):
     parts, out = refs[:-1], refs[-1]
-    half = shard // 2
-    width = parts[0].shape[3]
+    half = depth // 2
+    width = parts[0].shape[4]
+    line, core = lax.div(place[1], 2), lax.rem(place[1], 2)
     for source in range(dp):
         group = lax.bitwise_xor(place[0], source)
-        for step in range(shard):
-            column = lax.rem(place[1] + step, shard)
-            value = parts[2 * source + step // half][step % half, 0]
-            out[0, group, :, pl.ds(pl.multiple_of(column * width, width), width)] = value.astype(f32)
+        for step in range(depth):
+            for other in range(2):
+                column = 2 * lax.rem(line - step + depth, depth) + lax.bitwise_xor(core, other)
+                value = parts[2 * source + step // half][step % half, other, 0]
+                out[0, group, :, pl.ds(pl.multiple_of(column * width, width), width)] = value.astype(f32)
 
 
 def join_grad(parts, place, dp, shard):
-    half, _, part, width = parts[0].shape
-    block = pl.BlockSpec((half, 1, part, width), lambda i: (0, i, 0, 0))
+    half, _, _, part, width = parts[0].shape
+    block = pl.BlockSpec((half, 2, 1, part, width), lambda i: (0, 0, i, 0, 0))
     out = pl.pallas_call(
-        functools.partial(join_kernel, dp, shard),
+        functools.partial(join_kernel, dp, shard // 2),
         grid=(9,),
         out_shape=jax.ShapeDtypeStruct((9, dp, part, shard * width), f32),
         in_specs=[SM] + [block] * len(parts),
@@ -412,7 +417,7 @@
     )(*packing, value)
 
 
-under_way_w, under_way_xy, chunks = 7, 3, 4
+under_way_xy, chunks = 3, 4
 
 
 def roll_to(stacked, start, axis):
@@ -470,9 +475,9 @@
     def to_z(value, k):
         return queued("z", value, lambda v: permute(v, "shard", shard, lambda i: i + 2 * k), under_way_z)
 
-    def from_shard(value, k, *earlier):
+    def to_z(value, k, most, *earlier):
         value = after(value, *earlier)
-        return queued("z", value, lambda v: permute(v, "shard", shard, lambda i: i - k), under_way_w)
+        return queued("z", value, lambda v: permute(v, "shard", shard, lambda i: i + 2 * k), most)
 
     def other_core(value):
         return permute(value, "shard", shard, lambda i: i ^ 1)
@@ -486,10 +491,10 @@
         return [value, one, two, three]
 
     def gather_chunks(values):
-        near = []
-        for p, value in enumerate(values):
+        near = [[values[0], other_dp(values[0], 1), other_dp(values[0], 2), other_dp(values[0], 3)]]
+        for p, value in enumerate(values[1:], 1):
             near.append([value, other_dp(value, 1), other_dp(value, 2)])
-            if p:
+            if p > 1:
                 near[p - 1].append(other_dp(near[p - 1][1 + (p - 1) % 2], 2 - (p - 1) % 2))
         near[-1].append(other_dp(near[-1][1 + p % 2], 2 - p % 2))
         return near
@@ -513,18 +518,26 @@
         line = roll_to(jnp.stack([square] + far), (depth - z) % depth, 0)
         return jnp.stack(core_order(line, other_core(line), c), axis=1)
 
-    def weight_in(pieces, done=()):
-        done = dict(done)
-        return [pieces[0]] + [from_shard(pieces[k], k, *done.get(k, ())) for k in range(1, shard)]
+    def weight_in(pieces, most):
+        pieces = [pieces[0]] + [to_z(pieces[k], -k, most) for k in range(1, depth)]
+        return pieces, other_core(jnp.stack([v[1] for v in pieces]))
 
     def send_grad(grad, done=()):
         done = dict(done)
-        pieces = grad.reshape((shard, 9) + grad.shape[1:])
-        return [pieces[0]] + [from_shard(pieces[shard - k], k, *done.get(k, ())) for k in range(1, shard)]
-
-    def near_grad(parts):
-        half = shard // 2
-        return [gather_dp(jnp.stack(parts[:half]), 0), gather_dp(jnp.stack(parts[half:]), 1)]
+        pieces = grad.reshape((2, depth, 9) + grad.shape[1:])
+        pieces = jnp.stack([pieces[0], other_core(pieces[1])], axis=1)
+        return [pieces[0]] + [to_z(pieces[k], k, 3, *done.get(k, ())) for k in range(1, depth)]
+
+    def near_grad(parts, *earlier):
+        def along(value, r, *earlier):
+            return permute(after(value, *earlier), "dp", dp, lambda i: i ^ r)
+
+        half = depth // 2
+        low, high = jnp.stack(parts[:half]), jnp.stack(parts[half:])
+        low_one, high_two = along(low, 1), along(high, 2)
+        low_three, high_one = along(low_one, 2, high_two), along(high, 1, low_one)
+        low_two, high_three = along(low, 2, low_three, *earlier), along(high_two, 1, high_one, *earlier)
+        return [[low, low_one, low_two, low_three], [high, high_one, high_two, high_three]]
 
     def on_device(
         clip_maps,
@@ -562,7 +575,9 @@
 
         def table_of(block):
             group = tap * shard + block
-            return (((group // 9 - s + shard) % shard) * 9 + group % 9).reshape(9 * shard).astype(jnp.int32)
+            owner = group // 9
+            place = (owner % 2 ^ c) * depth + (owner // 2 - z + depth) % depth
+            return (place * 9 + group % 9).reshape(9 * shard).astype(jnp.int32)
 
         table = table_of(position)
 
@@ -581,7 +596,7 @@
             & (from_row % lane_in == to_lane % lane_in)
         ).astype(bf16)
 
-        pieces_one = weight_in(split_weight(conv1_weight, place, dp, shard))
+        pieces_one, across_one = weight_in(split_weight(conv1_weight, place, dp, shard), 3)
         own_frames = lax.broadcasted_iota(jnp.int32, (clip_count, frames), 1)
         own_valid = (own_frames < lengths[:, None])[:, :, None, None]
         clip_maps = after(clip_maps, pieces_one[0])
@@ -593,11 +608,15 @@
             part = jnp.concatenate([v[:, at] for v in sorted_in], axis=1)
             from_dp.append(other_dp(part, r) if r else part)
         group = jnp.concatenate(unswap(from_dp, d), axis=0)
-        all_maps = lax.all_gather(group, "shard", tiled=True)
-        wide_one = expand_weight(pieces_one, table, spread, True)
+        all_maps = lax.all_gather(after(group, pieces_one[1]), "shard", tiled=True)
+        wide_one = expand_weight(pieces_one, across_one, table, spread, True)
         split_two = split_weight(after(conv2_weight, from_dp[1]), place, dp, shard)
 
-        all_lengths = gather_small(lengths, d, z, c).reshape(clips)
+        notes = jnp.concatenate([labels, lengths[:, None]], axis=1).astype(bf16)
+        notes = gather_small(jnp.pad(notes, ((0, 0), (0, -(classes + 1) % 128))), d, z, c)
+        notes = notes.reshape(clips, notes.shape[-1])
+        all_labels = notes[:, :classes].astype(f32)
+        all_lengths = notes[:, classes].astype(jnp.int32)
         kinds = jnp.stack([all_lengths > frames // 2, (all_lengths > frames // 4) & (all_lengths <= frames // 2), all_lengths <= frames // 4])
         kinds = kinds.astype(jnp.int32)
         taken = jnp.array([frames, frames // 2, frames // 4], jnp.int32)[:, None]
@@ -624,16 +643,16 @@
                 return total
 
             maps_in, valid = pack_maps(all_maps, packing, frames, height, chunks)
-            pieces_two = weight_in(split_two)
+            pieces_two, across_two = weight_in(split_two, 3)
             parts = []
             for p in range(chunks):
-                value = after(maps_in[p], *[(), (), (), pieces_two[1:2]][p])
+                value = after(maps_in[p], *())
                 outs = convolve([value], wide_one, [(step, wide)] * dp, name="conv1")
                 parts.append(scatter_dp(outs))
-            parts = tied(parts, *pieces_two[2:4])
+            parts = tied(parts, *pieces_two[1:2])
             first_out = jnp.concatenate(parts, axis=0)
 
-            wide_two = expand_weight(pieces_two, table, spread, False)
+            wide_two = expand_weight(pieces_two, across_two, table, spread, False)
 
             own_start = (s * dp + d) * lane
 
@@ -648,30 +667,30 @@
             pre_one = normed_one * gain_one + shift_one
             act_one = (jax.nn.silu(pre_one) * valid).astype(bf16)
             acts = [
-                lax.all_gather(after(act_one[:half], *pieces_two[4:6]), "shard"),
-                lax.all_gather(after(act_one[half:], *pieces_two[6:], wide_two), "shard"),
+                lax.all_gather(after(act_one[:half], *pieces_two[2:3]), "shard"),
+                lax.all_gather(after(act_one[half:], wide_two), "shard"),
             ]
-            pad = -classes % 128
-            some_labels = jnp.pad(labels.astype(bf16), ((0, 0), (0, pad)))
-            some_labels = after(some_labels, act_one)
-            all_labels = gather_small(some_labels, d, z, c)
-            own_fc2 = lax.dynamic_slice_in_dim(jnp.pad(fc2_weight, ((0, 0), (0, pad))), d * lane, lane, axis=0)
-            far = [permute(after(own_fc2, act_one), "shard", shard, lambda i, k=k: i - 2 * k) for k in range(1, depth)]
-            line = roll_to(jnp.stack([own_fc2] + far), (depth - z) % depth, 0)
-            near = [permute(line, "dp", dp, lambda i, r=r: i ^ r) for r in range(1, dp)]
-            square = jnp.stack(unswap([line] + near, d), axis=1)
-            full_fc2 = jnp.stack(core_order(square, other_core(square), c), axis=1)
-            full_fc2 = full_fc2.reshape(chan_mid, classes + pad)[:, :classes]
-            all_labels = all_labels.reshape(clips, classes + pad)[:, :classes].astype(f32)
             fc_rows = fc1_weight.shape[0]
-            full_fc1 = lax.all_gather(after(fc1_weight, act_one), "shard", tiled=True)
+            own_fc1 = lax.dynamic_slice_in_dim(fc1_weight, d * lane, lane, axis=0)
+            some_fc1 = lax.all_gather(after(own_fc1, wide_two), "shard", tiled=True)
+            own_fc2 = jnp.pad(fc2_weight, ((0, 0), (0, -classes % 128)))
+            own_fc2 = after(lax.dynamic_slice_in_dim(own_fc2, d * lane, lane, axis=0), act_one)
+            line = [own_fc2] + [permute(own_fc2, "shard", shard, lambda i, k=k: i - 2 * k) for k in range(1, depth)]
+            line = roll_to(jnp.stack(line), (depth - z) % depth, 0)
             parts, outs = [], []
             for p in range(chunks):
                 value = after(acts[p // 2], *outs[:1])
                 if p >= 2:
-                    value = after(value, parts[p - 2], *((all_labels, full_fc2) if p == 2 else ()))
+                    value = after(value, parts[p - 2])
                 outs = convolve([value], wide_two, [(step, wide)] * dp, chunk=p % 2, name="conv2")
                 parts.append(scatter_dp(outs))
+                if p == 1:
+                    line = after(line, outs[0])
+                    near = [permute(line, "dp", dp, lambda i, r=r: i ^ r) for r in range(1, dp)]
+                    square = jnp.stack(unswap([line] + near, d), axis=1)
+                    full_fc2 = jnp.stack(core_order(square, other_core(square), c), axis=1)
+                    full_fc2 = full_fc2.reshape(chan_mid, own_fc2.shape[1])[:, :classes]
+            parts = tied(parts, full_fc2)
             second_out = jnp.concatenate(parts, axis=0)
             normed_two, inv_two = norm_of(second_out, valid, pixel_count)
             pre_two = normed_two * gain_two + shift_two
@@ -693,17 +712,23 @@
             log_sum = largest[:, 0, :] + jnp.log(exp_sum)
             mean_time = jnp.sum(pooled * pooled_valid, axis=1) / half_float
             own_embedding = (log_sum + mean_time).astype(bf16)
-            embedding = gather_small(own_embedding.T, d, z, c).reshape(chan_mid, clips)
-            own_columns = lax.dynamic_slice_in_dim(embedding, s * fc_rows, fc_rows, axis=0)
-            embedding = embedding.T
-            hidden = dot(embedding, full_fc1) + fc1_bias
+            own_embedding = own_embedding.T
+            line = [own_embedding] + [permute(own_embedding, "shard", shard, lambda i, k=k: i - 2 * k) for k in range(1, depth)]
+            line = roll_to(jnp.stack(line), (depth - z) % depth, 0)
+            line = jnp.stack(core_order(line, other_core(line), c), axis=1).reshape(shard * lane, clips)
+            part = lax.dynamic_slice_in_dim(line, c * (clips // 2), clips // 2, axis=1)
+            part = transpose_dot(part, some_fc1).astype(bf16)
+            near = [permute(part, "dp", dp, lambda i, r=r: i ^ r) for r in range(1, dp)]
+            part = sum(v.astype(f32) for v in unswap([part] + near, d))
+            hidden = jnp.concatenate(core_order(part, other_core(part), c), axis=0) + fc1_bias
+            near = [permute(after(own_embedding, part), "dp", dp, lambda i, r=r: i ^ r) for r in range(1, dp)]
+            own_columns = jnp.concatenate(unswap([own_embedding] + near, d), axis=0)
             sigma = jax.nn.sigmoid(hidden)
             gated = (hidden * sigma).astype(bf16)
             logits = dot(gated, full_fc2) + fc2_bias
             d_logits = (jax.nn.sigmoid(logits) - all_labels).astype(bf16)
             d_gated = dot_transpose(d_logits, full_fc2)
             d_hidden = (d_gated * (sigma + hidden * sigma * (1.0 - sigma))).astype(bf16)
-            own_fc1 = lax.dynamic_slice_in_dim(fc1_weight, d * lane, lane, axis=0)
             d_embed = dot_transpose(d_hidden, own_fc1)
             soft = exp_terms / exp_sum[:, None, :]
             d_pooled = d_embed[:, None, :] * (soft + pooled_valid / half_float[:, :, None])
@@ -745,8 +770,7 @@
                 grad_two = weight_grad(
                     act_chunks, ready, table, spread, lane, False, shard, first, count, grad_two, name="grad2",
                 )
-            sent_two = send_grad(grad_two)
-            parts = tied(parts, grad_two, *sent_two[1:3])
+            parts = tied(parts, grad_two)
 
             d_act_one = jnp.concatenate(parts, axis=0).astype(f32)
             sigma_one = jax.nn.sigmoid(pre_one)
@@ -761,31 +785,37 @@
             ).astype(bf16)
             values = list(d_first.reshape(chunks, step, wide))
             norm_grads = jnp.stack([gain_one_grad, shift_one_grad, gain_two_grad, shift_two_grad])
-            norm_grads = gather_small(norm_grads, d, z, c)
             grads_one = gather_chunks(values)
+            sent_two = send_grad(grad_two, {2: grads_one[1][1:3], 3: grads_one[3][1:3]})
             outs = []
             for p in range(chunks):
                 ready = tied(grads_one[p], *outs[-1:], *(grads_one[p + 1][1:3] if p + 1 < chunks else ()))
-                ready = tied(ready, *[(), (norm_grads,), (), ()][p])
                 outs += convolve(ready, wide_one, [(step, wide_in)], back=True, name="back1")
-            near_two = near_grad([after(v, grads_one[-1][3]) for v in sent_two])
-
-            grad_one = None
+            near = [permute(norm_grads, "dp", dp, lambda i, r=r: i ^ r) for r in range(1, dp)]
+            norm_grads = jnp.stack(unswap([norm_grads] + near, d))
+            near_two = near_grad([after(v, grads_one[-1][3], norm_grads) for v in sent_two])
+
+            grad_one, d_in = None, None
             count = shard // 2
             for first in range(0, shard, count):
-                ready = [tied(grads_one[0], outs[-1], *(near_two[0][1:3] if first else ()))] + grads_one[1:]
+                ready = [tied(grads_one[0], outs[-1], *((near_two[0][0], near_two[1][0]) if first else sent_two[1:2]))] + grads_one[1:]
                 grad_one = weight_grad(
                     [(v, 0) for v in maps_in], ready, table, spread, lane_in, True, shard, first, count, grad_one, name="grad1",
                 )
-            d_in = unpack_maps(outs, packing, frames, rows).reshape(shard, rows // shard, wide_in)
+            d_in = unpack_maps(tied(outs, grad_one), packing, frames, rows)
+            d_in = d_in.reshape(shard, rows // shard, wide_in)
             total = lax.psum_scatter(d_in, "shard", scatter_dimension=0)
-            sent_one = send_grad(grad_one, {1: near_two[0][1:3], 4: near_two[1][1:3]})
+            sent_one = send_grad(grad_one)
             conv2_grad = join_grad([h for pair in zip(*near_two) for h in pair], place, dp, shard)
             total = total.reshape(dp, own_rows, wide_in)
             from_dp = [other_dp(pick(total, d ^ r), r) if r else pick(total, d) for r in range(dp)]
-            near_one = near_grad(sent_one)
+            near_one = near_grad([after(v, near_two[0][2], near_two[1][3]) for v in sent_one], *from_dp[1:])
             conv1_grad = join_grad([h for pair in zip(*near_one) for h in pair], place, dp, shard)
 
+            norm_grads = after(norm_grads, sent_one[-1])
+            line = [norm_grads] + [permute(norm_grads, "shard", shard, lambda i, k=k: i - 2 * k) for k in range(1, depth)]
+            line = roll_to(jnp.stack(line), (depth - z) % depth, 0)
+            norm_grads = jnp.stack(core_order(line, other_core(line), c), axis=1)
             norm_grads = norm_grads.reshape(dp * shard, 4, lane)
             norm_grads = jnp.moveaxis(norm_grads, 0, 1).reshape(4, chan_mid)
 

time: 803 us -> 707 us (0.88)
  waiting for transfers between devices: 317 us -> 245 us
  starting transfers between devices: 149 us -> 135 us
    ppermute x129 -> x114, waiting for transfers between devices: 315 us -> 232 us  [permute(): return lax.ppermute(value, axis, [(i, move(i) % size) for i in range(size)])]
    ppermute x129 -> x114, starting transfers between devices: 149 us -> 134 us  [permute(): return lax.ppermute(value, axis, [(i, move(i) % size) for i in range(size)])]
    reduce_scatter x2, waiting for transfers between devices: 2.02 us -> 12.8 us  [after_maps(): parts.append(lax.psum_scatter(out, 'shard', scatter_dimension=0))]
  transfers between devices with their start and end apart: 136 -> 121, of which waited for: 57 -> 49; matrix products, arithmetic and copies ran while one was open for 8% -> 10% of each run, Pallas kernels for 20% -> 22%
where the time goes in v4:
time: 707 us; the launch traced here: 697 us
  waiting for transfers between devices  245 us (35%)
  Pallas kernels  190 us (27%)
  starting transfers between devices  135 us (19%)
  other arithmetic  52.7 us (7%)
  local copies, waits for them, and re-layouts  32.6 us (5%)
  between operations  18.8 us (3%)
  matrix products  13.4 us (2%)
  loops' own time  9.52 us (1%)
    ppermute x114, waiting for transfers between devices, permute(): return lax.ppermute(value, axis, [(i, move(i) % size) for i in range(size)])  232 us
    ppermute x114, starting transfers between devices, permute(): return lax.ppermute(value, axis, [(i, move(i) % size) for i in range(size)])  134 us
    pallas_call x16, Pallas kernels, convolve(): pl.pallas_call(functools.partial(conv_kernel, len(rows_in), back, height...  80.3 us
    pallas_call x6, Pallas kernels, weight_grad(): pl.pallas_call(functools.partial(grad_kernel, len(x_chunks), 1, len(g_chu...  54.6 us
    pallas_call x2, Pallas kernels, join_grad(): pl.pallas_call(functools.partial(join_kernel, dp, shard // 2), grid=(9,),...  20.3 us
  transfers between devices with their start and end apart: 121, of which 49 were waited for; matrix products, arithmetic and copies ran while one was open for 10% of the time, Pallas kernels for 22%

profile of v4, /device:TPU:16, one launch (start us, length us, event | category | flops | bytes accessed | tf_op | source)
XLA Modules:
  0.0 697.2 jit_solution(15783202004557496678)
XLA Ops:
  11.3 4.3 fusion.183
  42.6 29.1 %collective-permute-done.203 = bf16[4,4,640]{2,1,0:T(4,128)(2,1)S(1)} collective-permute-done((bf16[4,4,640]{2,1,0:T(4,128)(2,1)S(1)}, bf16[4,4,640]{2,1,0:T(4,128)(2,1)S(1)}, u32[]{:S(2)}, u32[]{:S(2)}) %collective-permute-start.203) | collective-permute-done | bytes 20512 | tf_op jit(solution)/shard_map/ppermute | solution.py:470
  71.8 8.9 %collective-permute-done.205 = bf16[4,4,640]{2,1,0:T(4,128)(2,1)S(1)} collective-permute-done((bf16[4,4,640]{2,1,0:T(4,128)(2,1)S(1)}, bf16[4,4,640]{2,1,0:T(4,128)(2,1)S(1)}, u32[]{:S(2)}, u32[]{:S(2)}) %collective-permute-start.205) | collective-permute-done | bytes 20512 | tf_op jit(solution)/shard_map/ppermute | solution.py:470
  91.4 4.0 split_weight.3
  98.5 590.6 %conditional.1 = (f32[1152,2048]{1,0:T(8,128)}, f32[2048]{0:T(1024)S(1)}, f32[2048]{0:T(1024)S(1)}, f32[2304,2048]{1,0:T(8,128)}, f32[2048]{0:T(1024)S(1)}, /*in...) conditional(s32[]{:T(128)} %convert_element_type.407, ...), branch_computations={%region_9.27_spmd, %region_27.45_spmd} | conditional | flops 61126852608 | bytes 804677760 | solution.py:852
  109.1 6.7 pack_maps.3
  158.6 4.6 collective-permute-done.111
  171.3 15.0 %collective-permute-done.114.refs_3_ = bf16[2,9,64,256]{3,2,1,0:T(8,128)(2,1)S(1)} collective-permute-done((bf16[2,9,64,256]{3,2,1,0:T(8,128)(2,1)}, bf16[2,9,64,256]{3,2,1,0:T(8,128)(2,1)S(1)}, u32[]{:S(2)}, u32[]{:S(2)}) %collective-permute-start.114) | collective-permute-done | bytes 589856 | tf_op jit(solution)/shard_map/cond/branch_1_fun/ppermute | solution.py:470
  190.5 5.5 expand_weight.4
  203.4 4.7 collective-permute-done.119
  210.4 6.0 conv2.12
  219.9 6.0 conv2.13
  230.2 8.5 %collective-permute-done.128 = bf16[672,128]{1,0:T(8,128)(2,1)S(1)} collective-permute-done((bf16[672,128]{1,0:T(8,128)(2,1)}, bf16[672,128]{1,0:T(8,128)(2,1)S(1)}, u32[]{:S(2)}, u32[]{:S(2)}) %collective-permute-start.128) | collective-permute-done | bytes 172064 | tf_op jit(solution)/shard_map/cond/branch_1_fun/ppermute | solution.py:470
  241.7 6.1 conv2.14
  251.3 6.0 conv2.15
  262.4 4.8 collective-permute-done.134
  278.2 5.1 reduce_sum.297
  305.9 4.0 collective-permute-done.141
  309.9 5.8 collective-permute-done.140
  328.6 4.0 pack_rows.3
  343.6 4.2 collective-permute-start.146
  354.2 6.4 back2.12
  361.3 6.4 back2.13
  373.2 4.3 collective-permute-done.151.refs_1_.refs_17_
  379.3 6.4 back2.14
  386.4 6.4 back2.15
  396.5 8.2 %grad2.12.refs_21_ = bf16[72,64,256]{2,1,0:T(8,128)(2,1)} custom-call(s32[72]{0:T(128)S(1)} %copy-done.186, bf16[8,1344,128]{2,1,0:T(8,128)(2,1)} %bitcast.377, bf16[8,1344,128]{2,1,0:T(8,128)(2,1)} %bitcast.378, bf16[8,1344,128]{2,1,0:T(8,128)(2,1)} %bitcast.387, bf16[8,1344,128]{2,1,0:T(8,128)(2,1)} %bitcast.388, bf16[672,128]{1,0:T(8,128)(2,1)} %copy-done.46, ...), custom_call_target="tpu_custom_call" | custom-call | flops 2113929216 | bytes 4718592 | tf_op jit(solution)/shard_map/cond/branch_1_fun/grad2/pallas_call | solution.py:252
  404.6 8.2 %grad2.13.refs_21_ = bf16[72,64,256]{2,1,0:T(8,128)(2,1)} custom-call(s32[72]{0:T(128)S(1)} %copy-done.186, bf16[8,1344,128]{2,1,0:T(8,128)(2,1)} %bitcast.379, bf16[8,1344,128]{2,1,0:T(8,128)(2,1)} %bitcast.380, bf16[8,1344,128]{2,1,0:T(8,128)(2,1)} %bitcast.389, bf16[8,1344,128]{2,1,0:T(8,128)(2,1)} %bitcast.390, ...), custom_call_target="tpu_custom_call", output_to_operand_aliasing={{}: (22, {})} | custom-call | flops 2113929216 | bytes 4718592 | tf_op jit(solution)/shard_map/cond/branch_1_fun/grad2/pallas_call | solution.py:252
  412.8 8.1 %grad2.14.refs_21_ = bf16[72,64,256]{2,1,0:T(8,128)(2,1)} custom-call(s32[72]{0:T(128)S(1)} %copy-done.186, bf16[8,1344,128]{2,1,0:T(8,128)(2,1)} %bitcast.381, bf16[8,1344,128]{2,1,0:T(8,128)(2,1)} %bitcast.382, bf16[8,1344,128]{2,1,0:T(8,128)(2,1)} %bitcast.391, bf16[8,1344,128]{2,1,0:T(8,128)(2,1)} %bitcast.392, ...), custom_call_target="tpu_custom_call", output_to_operand_aliasing={{}: (22, {})} | custom-call | flops 2113929216 | bytes 4718592 | tf_op jit(solution)/shard_map/cond/branch_1_fun/grad2/pallas_call | solution.py:252
  421.0 8.6 %grad2.15 = bf16[72,64,256]{2,1,0:T(8,128)(2,1)} custom-call(s32[72]{0:T(128)S(1)} %copy-done.186, bf16[8,1344,128]{2,1,0:T(8,128)(2,1)} %bitcast.383, bf16[8,1344,128]{2,1,0:T(8,128)(2,1)} %bitcast.384, bf16[8,1344,128]{2,1,0:T(8,128)(2,1)} %bitcast.393, bf16[8,1344,128]{2,1,0:T(8,128)(2,1)} %bitcast.394, ...), custom_call_target="tpu_custom_call", output_to_operand_aliasing={{}: (22, {})} | custom-call | flops 2113929216 | bytes 4718592 | tf_op jit(solution)/shard_map/cond/branch_1_fun/grad2/pallas_call | solution.py:252
  433.1 12.8 %reduce-scatter.15.cloned.1.call-done = bf16[1,1344,128]{2,1,0:T(8,128)(2,1)} async-done(((bf16[8,1344,128]{2,1,0:T(8,128)(2,1)}), bf16[1,1344,128]{2,1,0:T(8,128)(2,1)}) %reduce-scatter.15.cloned.1.call-update) | async-done | bytes 344080 | tf_op jit(solution)/shard_map/cond/branch_1_fun/reduce_scatter | solution.py:763
  463.2 4.6 collective-permute-done.159.refs_3_.refs_7_
  483.2 3.9 back1.12.refs_0_
  489.8 3.9 back1.13.refs_1_
  493.8 3.9 back1.14.refs_2_
  498.4 3.9 back1.15.refs_3_
  502.4 11.0 %grad1.6.refs_21_ = bf16[72,32,256]{2,1,0:T(8,128)(2,1)} custom-call(s32[72]{0:T(128)S(1)} %copy-done.186, bf16[672,512]{1,0:T(8,128)(2,1)} %get-tuple-element.288.refs_0_, bf16[672,512]{1,0:T(8,128)(2,1)} %get-tuple-element.296.refs_0_.refs_1_, bf16[672,512]{1,0:T(8,128)(2,1)} %get-tuple-element.304.refs_0_.refs_2_, ...), custom_call_target="tpu_custom_call" | custom-call | flops 2113929216 | bytes 4718592 | tf_op jit(solution)/shard_map/cond/branch_1_fun/grad1/pallas_call | solution.py:252
  514.5 10.6 %grad1.7 = bf16[72,32,256]{2,1,0:T(8,128)(2,1)} custom-call(s32[72]{0:T(128)S(1)} %copy-done.186, bf16[672,512]{1,0:T(8,128)(2,1)} %get-tuple-element.288.refs_0_, bf16[672,512]{1,0:T(8,128)(2,1)} %get-tuple-element.296.refs_0_.refs_1_, bf16[672,512]{1,0:T(8,128)(2,1)} %get-tuple-element.304.refs_0_.refs_2_, ...), custom_call_target="tpu_custom_call", output_to_operand_aliasing={{}: (22, {})} | custom-call | flops 2113929216 | bytes 4718592 | tf_op jit(solution)/shard_map/cond/branch_1_fun/grad1/pallas_call | solution.py:252
  525.1 5.8 unpack_maps.3
  536.0 21.4 %collective-permute-done.178.refs_2_ = bf16[2,2,9,64,256]{4,3,2,1,0:T(8,128)(2,1)} collective-permute-done((bf16[2,2,9,64,256]{4,3,2,1,0:T(8,128)(2,1)S(1)}, bf16[2,2,9,64,256]{4,3,2,1,0:T(8,128)(2,1)}, u32[]{:S(2)}, u32[]{:S(2)}) %collective-permute-start.178) | collective-permute-done | bytes 1179680 | tf_op jit(solution)/shard_map/cond/branch_1_fun/ppermute | solution.py:470
  570.6 15.7 %collective-permute-done.186 = bf16[2,9,32,256]{3,2,1,0:T(8,128)(2,1)S(1)} collective-permute-done((bf16[2,9,32,256]{3,2,1,0:T(8,128)(2,1)S(1)}, bf16[2,9,32,256]{3,2,1,0:T(8,128)(2,1)S(1)}, u32[]{:S(2)}, u32[]{:S(2)}) %collective-permute-start.186) | collective-permute-done | bytes 294944 | tf_op jit(solution)/shard_map/cond/branch_1_fun/ppermute | solution.py:470
  586.3 4.4 collective-permute-start.193
  593.0 10.9 %collective-permute-done.193 = f32[4,4,64]{2,1,0:T(4,128)S(1)} collective-permute-done((f32[4,4,64]{2,1,0:T(4,128)S(1)}, f32[4,4,64]{2,1,0:T(4,128)S(1)}, u32[]{:S(2)}, u32[]{:S(2)}) %collective-permute-start.193) | collective-permute-done | bytes 4128 | tf_op jit(solution)/shard_map/cond/branch_1_fun/ppermute | solution.py:470
  609.6 18.8 %collective-permute-done.181.refs_4_ = bf16[2,2,9,64,256]{4,3,2,1,0:T(8,128)(2,1)S(1)} collective-permute-done((bf16[2,2,9,64,256]{4,3,2,1,0:T(8,128)(2,1)S(1)}, bf16[2,2,9,64,256]{4,3,2,1,0:T(8,128)(2,1)S(1)}, u32[]{:S(2)}, u32[]{:S(2)}) %collective-permute-start.181) | collective-permute-done | bytes 1179680 | tf_op jit(solution)/shard_map/cond/branch_1_fun/ppermute | solution.py:470
  633.3 9.9 %collective-permute-done.187.refs_2_ = bf16[2,2,9,32,256]{4,3,2,1,0:T(8,128)(2,1)} collective-permute-done((bf16[2,2,9,32,256]{4,3,2,1,0:T(8,128)(2,1)S(1)}, bf16[2,2,9,32,256]{4,3,2,1,0:T(8,128)(2,1)}, u32[]{:S(2)}, u32[]{:S(2)}) %collective-permute-start.187) | collective-permute-done | bytes 589856 | tf_op jit(solution)/shard_map/cond/branch_1_fun/ppermute | solution.py:470
  645.9 11.7 %join_grad.7 = f32[9,4,64,2048]{3,2,1,0:T(8,128)} custom-call(s32[2]{0:T(128)S(1)} %copy-done.194, bf16[2,2,9,64,256]{4,3,2,1,0:T(8,128)(2,1)} %copy-done.43, bf16[2,2,9,64,256]{4,3,2,1,0:T(8,128)(2,1)} %pad_maximum_fusion.33.refs_1_, bf16[2,2,9,64,256]{4,3,2,1,0:T(8,128)(2,1)} %collective-permute-done.178.refs_2_, ...), custom_call_target="tpu_custom_call" | custom-call | bytes 28311552 | tf_op jit(solution)/shard_map/cond/branch_1_fun/join_grad/pallas_call | solution.py:288
  673.3 5.4 collective-permute-done.192.refs_7_
  680.4 8.6 %join_grad.6 = f32[9,4,32,2048]{3,2,1,0:T(8,128)} custom-call(s32[2]{0:T(128)S(1)} %copy-done.194, bf16[2,2,9,32,256]{4,3,2,1,0:T(8,128)(2,1)} %copy-done.87, bf16[2,2,9,32,256]{4,3,2,1,0:T(8,128)(2,1)} %copy-done.85, bf16[2,2,9,32,256]{4,3,2,1,0:T(8,128)(2,1)} %collective-permute-done.187.refs_2_, ...), custom_call_target="tpu_custom_call" | custom-call | bytes 14155776 | tf_op jit(solution)/shard_map/cond/branch_1_fun/join_grad/pallas_call | solution.py:288
  (732 shorter events, 295.3 us)
Async XLA Ops:
  7.2 90.7 %all-gather.24.cloned.1.call-start = ((), (), s32[]{:S(2)}) async-start(), calls=%async_computation.18 | async-start | bytes 4718592 | tf_op jit(solution)/shard_map/all_gather | solution.py:611
  32.5 56.3 %collective-permute-start.211 = (bf16[2,9,32,256]{3,2,1,0:T(8,128)(2,1)S(1)}, bf16[2,9,32,256]{3,2,1,0:T(8,128)(2,1)S(1)}, u32[]{:S(2)}, u32[]{:S(2)}) collective-permute-start(bf16[2,9,32,256]{3,2,1,0:T(8,128)(2,1)S(1)} %copy-done.246), channel_id=1, source_target_pairs={{0,4},{1,5},{2,6},{3,7},{4,0},{5,1},{6,2},{7,3},{8,12},{9,13},{10,... | collective-permute-start | bytes 884744 | tf_op jit(solution)/shard_map/ppermute | solution.py:470
  34.0 54.8 %collective-permute-start.212 = (bf16[2,9,32,256]{3,2,1,0:T(8,128)(2,1)S(1)}, bf16[2,9,32,256]{3,2,1,0:T(8,128)(2,1)S(1)}, u32[]{:S(2)}, u32[]{:S(2)}) collective-permute-start(bf16[2,9,32,256]{3,2,1,0:T(8,128)(2,1)S(1)} %copy-done.245), channel_id=1, source_target_pairs={{0,2},{1,3},{2,4},{3,5},{4,6},{5,7},{6,0},{7,1},{8,10},{9,11},{10,... | collective-permute-start | bytes 884744 | tf_op jit(solution)/shard_map/ppermute | solution.py:470
  37.7 34.1 %collective-permute-start.204 = (bf16[4,4,640]{2,1,0:T(4,128)(2,1)S(1)}, bf16[4,4,640]{2,1,0:T(4,128)(2,1)S(1)}, u32[]{:S(2)}, u32[]{:S(2)}) collective-permute-start(bf16[4,4,640]{2,1,0:T(4,128)(2,1)S(1)} %pad_maximum_fusion.57), channel_id=1, source_target_pairs={{0,4},{1,5},{2,6},{3,7},{4,0},{5,1},{6,2},{7,3},{8,12},{9,13},{10,... | collective-permute-start | bytes 61448 | tf_op jit(solution)/shard_map/ppermute | solution.py:470
  40.6 31.1 %collective-permute-start.203 = (bf16[4,4,640]{2,1,0:T(4,128)(2,1)S(1)}, bf16[4,4,640]{2,1,0:T(4,128)(2,1)S(1)}, u32[]{:S(2)}, u32[]{:S(2)}) collective-permute-start(bf16[4,4,640]{2,1,0:T(4,128)(2,1)S(1)} %pad_maximum_fusion.57), channel_id=1, source_target_pairs={{0,6},{1,7},{2,0},{3,1},{4,2},{5,3},{6,4},{7,5},{8,14},{9,15},{10,... | collective-permute-start | bytes 61448 | tf_op jit(solution)/shard_map/ppermute | solution.py:470
  40.6 40.1 %collective-permute-start.205 = (bf16[4,4,640]{2,1,0:T(4,128)(2,1)S(1)}, bf16[4,4,640]{2,1,0:T(4,128)(2,1)S(1)}, u32[]{:S(2)}, u32[]{:S(2)}) collective-permute-start(bf16[4,4,640]{2,1,0:T(4,128)(2,1)S(1)} %pad_maximum_fusion.57), channel_id=1, source_target_pairs={{0,2},{1,3},{2,4},{3,5},{4,6},{5,7},{6,0},{7,1},{8,10},{9,11},{10,... | collective-permute-start | bytes 61448 | tf_op jit(solution)/shard_map/ppermute | solution.py:470
  106.0 104.3 %all-gather.20.cloned.1.call-start = ((), (), s32[]{:S(2)}) async-start(), calls=%async_computation.16 | async-start | bytes 3096576 | tf_op jit(solution)/shard_map/cond/branch_1_fun/all_gather | solution.py:670
  106.1 61.4 %collective-permute-start.113 = (bf16[2,9,64,256]{3,2,1,0:T(8,128)(2,1)}, bf16[2,9,64,256]{3,2,1,0:T(8,128)(2,1)}, u32[]{:S(2)}, u32[]{:S(2)}) collective-permute-start(bf16[2,9,64,256]{3,2,1,0:T(8,128)(2,1)} %get-tuple-element.325), channel_id=1, source_target_pairs={{0,4},{1,5},{2,6},{3,7},{4,0},{5,1},{6,2},{7,3},{8,12},{9,13},{10,... | collective-permute-start | bytes 1769480 | tf_op jit(solution)/shard_map/cond/branch_1_fun/ppermute | solution.py:470
  106.2 52.4 %collective-permute-start.103 = (bf16[2,9,64,256]{3,2,1,0:T(8,128)(2,1)}, bf16[2,9,64,256]{3,2,1,0:T(8,128)(2,1)}, u32[]{:S(2)}, u32[]{:S(2)}) collective-permute-start(bf16[2,9,64,256]{3,2,1,0:T(8,128)(2,1)} %get-tuple-element.294), channel_id=1, source_target_pairs={{0,6},{1,7},{2,0},{3,1},{4,2},{5,3},{6,4},{7,5},{8,14},{9,15},{10,... | collective-permute-start | bytes 1769480 | tf_op jit(solution)/shard_map/cond/branch_1_fun/ppermute | solution.py:470
  119.6 16.4 %collective-permute-start.100 = (bf16[672,128]{1,0:T(8,128)(2,1)}, bf16[672,128]{1,0:T(8,128)(2,1)S(1)}, u32[]{:S(2)}, u32[]{:S(2)}) collective-permute-start(bf16[672,128]{1,0:T(8,128)(2,1)} %get-tuple-element.291), channel_id=1, source_target_pairs={{0,8},{8,0},{16,24},{24,16},{1,9},{9,1},{17,25},{25,17},{2,10},{10... | collective-permute-start | bytes 516104 | tf_op jit(solution)/shard_map/cond/branch_1_fun/ppermute | solution.py:470
  121.0 16.4 %collective-permute-start.101 = (bf16[672,128]{1,0:T(8,128)(2,1)}, bf16[672,128]{1,0:T(8,128)(2,1)S(1)}, u32[]{:S(2)}, u32[]{:S(2)}) collective-permute-start(bf16[672,128]{1,0:T(8,128)(2,1)} %get-tuple-element.292), channel_id=1, source_target_pairs={{0,16},{8,24},{16,0},{24,8},{1,17},{9,25},{17,1},{25,9},{2,18},{10... | collective-permute-start | bytes 516104 | tf_op jit(solution)/shard_map/cond/branch_1_fun/ppermute | solution.py:470
  122.2 16.4 %collective-permute-start.102 = (bf16[672,128]{1,0:T(8,128)(2,1)}, bf16[672,128]{1,0:T(8,128)(2,1)S(1)}, u32[]{:S(2)}, u32[]{:S(2)}) collective-permute-start(bf16[672,128]{1,0:T(8,128)(2,1)} %get-tuple-element.293), channel_id=1, source_target_pairs={{0,24},{8,16},{16,8},{24,0},{1,25},{9,17},{17,9},{25,1},{2,26},{10... | collective-permute-start | bytes 516104 | tf_op jit(solution)/shard_map/cond/branch_1_fun/ppermute | solution.py:470
  167.5 74.2 %all-gather.22.cloned.1.call-start = ((), (), s32[]{:S(2)}) async-start(), calls=%async_computation.17 | async-start | bytes 3096576 | tf_op jit(solution)/shard_map/cond/branch_1_fun/all_gather | solution.py:671
  167.5 18.7 %collective-permute-start.114 = (bf16[2,9,64,256]{3,2,1,0:T(8,128)(2,1)}, bf16[2,9,64,256]{3,2,1,0:T(8,128)(2,1)S(1)}, u32[]{:S(2)}, u32[]{:S(2)}) collective-permute-start(bf16[2,9,64,256]{3,2,1,0:T(8,128)(2,1)} %get-tuple-element.329), channel_id=1, source_target_pairs={{0,2},{1,3},{2,4},{3,5},{4,6},{5,7},{6,0},{7,1},{8,10},{9,11},{10,... | collective-permute-start | bytes 1769480 | tf_op jit(solution)/shard_map/cond/branch_1_fun/ppermute | solution.py:470
  196.0 102.3 %all-gather.18.cloned.1.call-start = ((), (), s32[]{:S(2)}) async-start(), calls=%async_computation.12 | async-start | bytes 2359296 | tf_op jit(solution)/shard_map/cond/branch_1_fun/all_gather | solution.py:675
  210.1 223.0 %reduce-scatter.13.cloned.1.call-start = ((), (), s32[]{:S(2)}) async-start(), calls=%async_computation.13 | async-start | bytes 3096576 | tf_op jit(solution)/shard_map/cond/branch_1_fun/reduce_scatter | solution.py:763
  225.9 61.7 %collective-permute-start.124 = (bf16[4,64,640]{2,1,0:T(8,128)(2,1)}, bf16[4,64,640]{2,1,0:T(8,128)(2,1)}, u32[]{:S(2)}, u32[]{:S(2)}) collective-permute-start(bf16[4,64,640]{2,1,0:T(8,128)(2,1)} %constant_dynamic-slice_fusion.9), channel_id=1, source_target_pairs={{0,8},{8,0},{16,24},{24,16},{1,9},{9,1},{17,25},{25,17},{2,10},{10... | collective-permute-start | bytes 983048 | tf_op jit(solution)/shard_map/cond/branch_1_fun/ppermute | solution.py:470
  225.9 61.7 %collective-permute-start.123 = (bf16[4,64,640]{2,1,0:T(8,128)(2,1)}, bf16[4,64,640]{2,1,0:T(8,128)(2,1)}, u32[]{:S(2)}, u32[]{:S(2)}) collective-permute-start(bf16[4,64,640]{2,1,0:T(8,128)(2,1)} %constant_dynamic-slice_fusion.9), channel_id=1, source_target_pairs={{0,16},{8,24},{16,0},{24,8},{1,17},{9,25},{17,1},{25,9},{2,18},{10... | collective-permute-start | bytes 983048 | tf_op jit(solution)/shard_map/cond/branch_1_fun/ppermute | solution.py:470
  267.2 20.4 %collective-permute-start.122 = (bf16[4,64,640]{2,1,0:T(8,128)(2,1)}, bf16[4,64,640]{2,1,0:T(8,128)(2,1)}, u32[]{:S(2)}, u32[]{:S(2)}) collective-permute-start(bf16[4,64,640]{2,1,0:T(8,128)(2,1)} %constant_dynamic-slice_fusion.9), channel_id=1, source_target_pairs={{0,24},{8,16},{16,8},{24,0},{1,25},{9,17},{17,9},{25,1},{2,26},{10... | collective-permute-start | bytes 983048 | tf_op jit(solution)/shard_map/cond/branch_1_fun/ppermute | solution.py:470
  296.9 20.2 %collective-permute-start.125 = (bf16[4,4,64,640]{3,2,1,0:T(8,128)(2,1)}, bf16[4,4,64,640]{3,2,1,0:T(8,128)(2,1)}, u32[]{:S(2)}, u32[]{:S(2)}) collective-permute-start(bf16[4,4,64,640]{3,2,1,0:T(8,128)(2,1)} %pad_maximum_fusion.30), channel_id=1, source_target_pairs={{0,1},{1,0},{2,3},{3,2},{4,5},{5,4},{6,7},{7,6},{8,9},{9,8},{10,11... | collective-permute-start | bytes 3932168 | tf_op jit(solution)/shard_map/cond/branch_1_fun/ppermute | solution.py:470
  302.1 13.7 %collective-permute-start.140 = (bf16[64,2048]{1,0:T(8,128)(2,1)S(1)}, bf16[64,2048]{1,0:T(8,128)(2,1)}, u32[]{:S(2)}, u32[]{:S(2)}) collective-permute-start(bf16[64,2048]{1,0:T(8,128)(2,1)S(1)} %convolution_convert_fusion.1), channel_id=1, source_target_pairs={{0,16},{8,24},{16,0},{24,8},{1,17},{9,25},{17,1},{25,9},{2,18},{10... | collective-permute-start | bytes 786440 | tf_op jit(solution)/shard_map/cond/branch_1_fun/ppermute | solution.py:470
  303.0 12.7 %collective-permute-start.139 = (bf16[64,2048]{1,0:T(8,128)(2,1)S(1)}, bf16[64,2048]{1,0:T(8,128)(2,1)}, u32[]{:S(2)}, u32[]{:S(2)}) collective-permute-start(bf16[64,2048]{1,0:T(8,128)(2,1)S(1)} %convolution_convert_fusion.1), channel_id=1, source_target_pairs={{0,24},{8,16},{16,8},{24,0},{1,25},{9,17},{17,9},{25,1},{2,26},{10... | collective-permute-start | bytes 786440 | tf_op jit(solution)/shard_map/cond/branch_1_fun/ppermute | solution.py:470
  347.8 12.8 %collective-permute-start.148 = (bf16[672,128]{1,0:T(8,128)(2,1)S(1)}, bf16[672,128]{1,0:T(8,128)(2,1)S(1)}, u32[]{:S(2)}, u32[]{:S(2)}) collective-permute-start(bf16[672,128]{1,0:T(8,128)(2,1)S(1)} %get-tuple-element.389.refs_0_.refs_12_), channel_id=1, source_target_pairs={{0,8},{8,0},{16,24},{24,16},{1,9},{9,1},{17,25},{25,17},{2,10},{10... | collective-permute-start | bytes 516104 | tf_op jit(solution)/shard_map/cond/branch_1_fun/ppermute | solution.py:470
  370.8 75.2 %reduce-scatter.15.cloned.1.call-start = ((), (), s32[]{:S(2)}) async-start(), calls=%async_computation.14 | async-start | bytes 3096576 | tf_op jit(solution)/shard_map/cond/branch_1_fun/reduce_scatter | solution.py:763
  395.9 261.7 %reduce-scatter.17.cloned.1.call-start = ((), (), s32[]{:S(2)}) async-start(), calls=%async_computation.15 | async-start | bytes 4718592 | tf_op jit(solution)/shard_map/cond/branch_1_fun/reduce_scatter | solution.py:807
  433.1 19.3 %collective-permute-start.167 = (bf16[4,9,64,256]{3,2,1,0:T(8,128)(2,1)}, bf16[4,9,64,256]{3,2,1,0:T(8,128)(2,1)}, u32[]{:S(2)}, u32[]{:S(2)}) collective-permute-start(bf16[4,9,64,256]{3,2,1,0:T(8,128)(2,1)} %bitcast.115), channel_id=1, source_target_pairs={{0,1},{1,0},{2,3},{3,2},{4,5},{5,4},{6,7},{7,6},{8,9},{9,8},{10,11... | collective-permute-start | bytes 3538952 | tf_op jit(solution)/shard_map/cond/branch_1_fun/ppermute | solution.py:470
  457.3 45.0 %collective-permute-start.171 = (bf16[2,9,64,256]{3,2,1,0:T(8,128)(2,1)S(1)}, bf16[2,9,64,256]{3,2,1,0:T(8,128)(2,1)S(1)}, u32[]{:S(2)}, u32[]{:S(2)}) collective-permute-start(bf16[2,9,64,256]{3,2,1,0:T(8,128)(2,1)S(1)} %get-tuple-element.412), channel_id=1, source_target_pairs={{0,2},{1,3},{2,4},{3,5},{4,6},{5,7},{6,0},{7,1},{8,10},{9,11},{10,... | collective-permute-start | bytes 1769480 | tf_op jit(solution)/shard_map/cond/branch_1_fun/ppermute | solution.py:470
  474.5 12.7 %collective-permute-start.163 = (bf16[672,128]{1,0:T(8,128)(2,1)S(1)}, bf16[672,128]{1,0:T(8,128)(2,1)S(1)}, u32[]{:S(2)}, u32[]{:S(2)}) collective-permute-start(bf16[672,128]{1,0:T(8,128)(2,1)S(1)} %get-tuple-element.409.refs_0_.refs_16_), channel_id=1, source_target_pairs={{0,8},{8,0},{16,24},{24,16},{1,9},{9,1},{17,25},{25,17},{2,10},{10... | collective-permute-start | bytes 516104 | tf_op jit(solution)/shard_map/cond/branch_1_fun/ppermute | solution.py:470
  478.7 34.7 %collective-permute-start.172 = (bf16[2,9,64,256]{3,2,1,0:T(8,128)(2,1)S(1)}, bf16[2,9,64,256]{3,2,1,0:T(8,128)(2,1)S(1)}, u32[]{:S(2)}, u32[]{:S(2)}) collective-permute-start(bf16[2,9,64,256]{3,2,1,0:T(8,128)(2,1)S(1)} %get-tuple-element.415), channel_id=1, source_target_pairs={{0,4},{1,5},{2,6},{3,7},{4,0},{5,1},{6,2},{7,3},{8,12},{9,13},{10,... | collective-permute-start | bytes 1769480 | tf_op jit(solution)/shard_map/cond/branch_1_fun/ppermute | solution.py:470
  488.9 24.5 %collective-permute-start.173 = (bf16[2,9,64,256]{3,2,1,0:T(8,128)(2,1)S(1)}, bf16[2,9,64,256]{3,2,1,0:T(8,128)(2,1)S(1)}, u32[]{:S(2)}, u32[]{:S(2)}) collective-permute-start(bf16[2,9,64,256]{3,2,1,0:T(8,128)(2,1)S(1)} %get-tuple-element.418), channel_id=1, source_target_pairs={{0,6},{1,7},{2,0},{3,1},{4,2},{5,3},{6,4},{7,5},{8,14},{9,15},{10,... | collective-permute-start | bytes 1769480 | tf_op jit(solution)/shard_map/cond/branch_1_fun/ppermute | solution.py:470
  530.9 26.5 %collective-permute-start.178 = (bf16[2,2,9,64,256]{4,3,2,1,0:T(8,128)(2,1)S(1)}, bf16[2,2,9,64,256]{4,3,2,1,0:T(8,128)(2,1)}, u32[]{:S(2)}, u32[]{:S(2)}) collective-permute-start(bf16[2,2,9,64,256]{4,3,2,1,0:T(8,128)(2,1)S(1)} %pad_maximum_fusion.32.refs_0_), channel_id=1, source_target_pairs={{0,8},{8,0},{16,24},{24,16},{1,9},{9,1},{17,25},{25,17},{2,10},{10... | collective-permute-start | bytes 3538952 | tf_op jit(solution)/shard_map/cond/branch_1_fun/ppermute | solution.py:470
  532.0 26.9 %collective-permute-start.179 = (bf16[2,2,9,64,256]{4,3,2,1,0:T(8,128)(2,1)}, bf16[2,2,9,64,256]{4,3,2,1,0:T(8,128)(2,1)}, u32[]{:S(2)}, u32[]{:S(2)}) collective-permute-start(bf16[2,2,9,64,256]{4,3,2,1,0:T(8,128)(2,1)} %pad_maximum_fusion.33.refs_1_), channel_id=1, source_target_pairs={{0,16},{8,24},{16,0},{24,8},{1,17},{9,25},{17,1},{25,9},{2,18},{10... | collective-permute-start | bytes 3538952 | tf_op jit(solution)/shard_map/cond/branch_1_fun/ppermute | solution.py:470
  534.8 27.9 %collective-permute-start.177 = (bf16[4,9,32,256]{3,2,1,0:T(8,128)(2,1)}, bf16[4,9,32,256]{3,2,1,0:T(8,128)(2,1)S(1)}, u32[]{:S(2)}, u32[]{:S(2)}) collective-permute-start(bf16[4,9,32,256]{3,2,1,0:T(8,128)(2,1)} %bitcast.143), channel_id=1, source_target_pairs={{0,1},{1,0},{2,3},{3,2},{4,5},{5,4},{6,7},{7,6},{8,9},{9,8},{10,11... | collective-permute-start | bytes 1769480 | tf_op jit(solution)/shard_map/cond/branch_1_fun/ppermute | solution.py:470
  534.8 25.4 %collective-permute-start.199 = (bf16[64,128]{0,1:T(8,128)(2,1)S(1)}, bf16[64,128]{0,1:T(8,128)(2,1)S(1)}, u32[]{:S(2)}, u32[]{:S(2)}) collective-permute-start(bf16[64,128]{0,1:T(8,128)(2,1)S(1)} %bitcast.485), channel_id=1, source_target_pairs={{0,8},{8,0},{16,24},{24,16},{1,9},{9,1},{17,25},{25,17},{2,10},{10... | collective-permute-start | bytes 49160 | tf_op jit(solution)/shard_map/cond/branch_1_fun/ppermute | solution.py:470
  534.9 26.1 %collective-permute-start.198 = (bf16[64,128]{0,1:T(8,128)(2,1)S(1)}, bf16[64,128]{0,1:T(8,128)(2,1)S(1)}, u32[]{:S(2)}, u32[]{:S(2)}) collective-permute-start(bf16[64,128]{0,1:T(8,128)(2,1)S(1)} %bitcast.486), channel_id=1, source_target_pairs={{0,16},{8,24},{16,0},{24,8},{1,17},{9,25},{17,1},{25,9},{2,18},{10... | collective-permute-start | bytes 49160 | tf_op jit(solution)/shard_map/cond/branch_1_fun/ppermute | solution.py:470
  558.9 31.8 %collective-permute-start.182 = (bf16[2,2,9,64,256]{4,3,2,1,0:T(8,128)(2,1)}, bf16[2,2,9,64,256]{4,3,2,1,0:T(8,128)(2,1)}, u32[]{:S(2)}, u32[]{:S(2)}) collective-permute-start(bf16[2,2,9,64,256]{4,3,2,1,0:T(8,128)(2,1)} %pad_maximum_fusion.33.refs_1_), channel_id=1, source_target_pairs={{0,8},{8,0},{16,24},{24,16},{1,9},{9,1},{17,25},{25,17},{2,10},{10... | collective-permute-start | bytes 3538952 | tf_op jit(solution)/shard_map/cond/branch_1_fun/ppermute | solution.py:470
  560.2 30.5 %collective-permute-start.180 = (bf16[2,2,9,64,256]{4,3,2,1,0:T(8,128)(2,1)}, bf16[2,2,9,64,256]{4,3,2,1,0:T(8,128)(2,1)}, u32[]{:S(2)}, u32[]{:S(2)}) collective-permute-start(bf16[2,2,9,64,256]{4,3,2,1,0:T(8,128)(2,1)} %collective-permute-done.178.refs_2_), channel_id=1, source_target_pairs={{0,16},{8,24},{16,0},{24,8},{1,17},{9,25},{17,1},{25,9},{2,18},{10... | collective-permute-start | bytes 3538952 | tf_op jit(solution)/shard_map/cond/branch_1_fun/ppermute | solution.py:470
  562.8 23.6 %collective-permute-start.186 = (bf16[2,9,32,256]{3,2,1,0:T(8,128)(2,1)S(1)}, bf16[2,9,32,256]{3,2,1,0:T(8,128)(2,1)S(1)}, u32[]{:S(2)}, u32[]{:S(2)}) collective-permute-start(bf16[2,9,32,256]{3,2,1,0:T(8,128)(2,1)S(1)} %get-tuple-element.438), channel_id=1, source_target_pairs={{0,6},{1,7},{2,0},{3,1},{4,2},{5,3},{6,4},{7,5},{8,14},{9,15},{10,... | collective-permute-start | bytes 884744 | tf_op jit(solution)/shard_map/cond/branch_1_fun/ppermute | solution.py:470
  569.1 60.4 %collective-permute-start.184 = (bf16[2,9,32,256]{3,2,1,0:T(8,128)(2,1)S(1)}, bf16[2,9,32,256]{3,2,1,0:T(8,128)(2,1)S(1)}, u32[]{:S(2)}, u32[]{:S(2)}) collective-permute-start(bf16[2,9,32,256]{3,2,1,0:T(8,128)(2,1)S(1)} %get-tuple-element.434), channel_id=1, source_target_pairs={{0,2},{1,3},{2,4},{3,5},{4,6},{5,7},{6,0},{7,1},{8,10},{9,11},{10,... | collective-permute-start | bytes 884744 | tf_op jit(solution)/shard_map/cond/branch_1_fun/ppermute | solution.py:470
  569.1 59.3 %collective-permute-start.185 = (bf16[2,9,32,256]{3,2,1,0:T(8,128)(2,1)S(1)}, bf16[2,9,32,256]{3,2,1,0:T(8,128)(2,1)S(1)}, u32[]{:S(2)}, u32[]{:S(2)}) collective-permute-start(bf16[2,9,32,256]{3,2,1,0:T(8,128)(2,1)S(1)} %get-tuple-element.436), channel_id=1, source_target_pairs={{0,4},{1,5},{2,6},{3,7},{4,0},{5,1},{6,2},{7,3},{8,12},{9,13},{10,... | collective-permute-start | bytes 884744 | tf_op jit(solution)/shard_map/cond/branch_1_fun/ppermute | solution.py:470
  586.3 17.6 %collective-permute-start.193 = (f32[4,4,64]{2,1,0:T(4,128)S(1)}, f32[4,4,64]{2,1,0:T(4,128)S(1)}, u32[]{:S(2)}, u32[]{:S(2)}) collective-permute-start(f32[4,4,64]{2,1,0:T(4,128)S(1)} %pad_maximum_fusion.40), channel_id=1, source_target_pairs={{0,6},{1,7},{2,0},{3,1},{4,2},{5,3},{6,4},{7,5},{8,14},{9,15},{10,... | collective-permute-start | bytes 12296 | tf_op jit(solution)/shard_map/cond/branch_1_fun/ppermute | solution.py:470
  590.7 14.6 %collective-permute-start.194 = (f32[4,4,64]{2,1,0:T(4,128)S(1)}, f32[4,4,64]{2,1,0:T(4,128)S(1)}, u32[]{:S(2)}, u32[]{:S(2)}) collective-permute-start(f32[4,4,64]{2,1,0:T(4,128)S(1)} %pad_maximum_fusion.40), channel_id=1, source_target_pairs={{0,4},{1,5},{2,6},{3,7},{4,0},{5,1},{6,2},{7,3},{8,12},{9,13},{10,... | collective-permute-start | bytes 12296 | tf_op jit(solution)/shard_map/cond/branch_1_fun/ppermute | solution.py:470
  590.7 18.9 %collective-permute-start.183 = (bf16[2,2,9,64,256]{4,3,2,1,0:T(8,128)(2,1)}, bf16[2,2,9,64,256]{4,3,2,1,0:T(8,128)(2,1)S(1)}, u32[]{:S(2)}, u32[]{:S(2)}) collective-permute-start(bf16[2,2,9,64,256]{4,3,2,1,0:T(8,128)(2,1)} %collective-permute-done.179.refs_5_), channel_id=1, source_target_pairs={{0,8},{8,0},{16,24},{24,16},{1,9},{9,1},{17,25},{25,17},{2,10},{10... | collective-permute-start | bytes 3538952 | tf_op jit(solution)/shard_map/cond/branch_1_fun/ppermute | solution.py:470
  603.9 24.5 %collective-permute-start.181 = (bf16[2,2,9,64,256]{4,3,2,1,0:T(8,128)(2,1)S(1)}, bf16[2,2,9,64,256]{4,3,2,1,0:T(8,128)(2,1)S(1)}, u32[]{:S(2)}, u32[]{:S(2)}) collective-permute-start(bf16[2,2,9,64,256]{4,3,2,1,0:T(8,128)(2,1)S(1)} %pad_maximum_fusion.32.refs_0_), channel_id=1, source_target_pairs={{0,16},{8,24},{16,0},{24,8},{1,17},{9,25},{17,1},{25,9},{2,18},{10... | collective-permute-start | bytes 3538952 | tf_op jit(solution)/shard_map/cond/branch_1_fun/ppermute | solution.py:470
  629.7 13.6 %collective-permute-start.187 = (bf16[2,2,9,32,256]{4,3,2,1,0:T(8,128)(2,1)S(1)}, bf16[2,2,9,32,256]{4,3,2,1,0:T(8,128)(2,1)}, u32[]{:S(2)}, u32[]{:S(2)}) collective-permute-start(bf16[2,2,9,32,256]{4,3,2,1,0:T(8,128)(2,1)S(1)} %pad_maximum_fusion.35.refs_0_), channel_id=1, source_target_pairs={{0,8},{8,0},{16,24},{24,16},{1,9},{9,1},{17,25},{25,17},{2,10},{10... | collective-permute-start | bytes 1769480 | tf_op jit(solution)/shard_map/cond/branch_1_fun/ppermute | solution.py:470
  631.0 13.5 %collective-permute-start.189 = (bf16[2,2,9,32,256]{4,3,2,1,0:T(8,128)(2,1)S(1)}, bf16[2,2,9,32,256]{4,3,2,1,0:T(8,128)(2,1)S(1)}, u32[]{:S(2)}, u32[]{:S(2)}) collective-permute-start(bf16[2,2,9,32,256]{4,3,2,1,0:T(8,128)(2,1)S(1)} %pad_maximum_fusion.36.refs_1_), channel_id=1, source_target_pairs={{0,16},{8,24},{16,0},{24,8},{1,17},{9,25},{17,1},{25,9},{2,18},{10... | collective-permute-start | bytes 1769480 | tf_op jit(solution)/shard_map/cond/branch_1_fun/ppermute | solution.py:470
  643.2 25.4 %collective-permute-start.188 = (bf16[2,2,9,32,256]{4,3,2,1,0:T(8,128)(2,1)S(1)}, bf16[2,2,9,32,256]{4,3,2,1,0:T(8,128)(2,1)}, u32[]{:S(2)}, u32[]{:S(2)}) collective-permute-start(bf16[2,2,9,32,256]{4,3,2,1,0:T(8,128)(2,1)S(1)} %pad_maximum_fusion.36.refs_1_), channel_id=1, source_target_pairs={{0,8},{8,0},{16,24},{24,16},{1,9},{9,1},{17,25},{25,17},{2,10},{10... | collective-permute-start | bytes 1769480 | tf_op jit(solution)/shard_map/cond/branch_1_fun/ppermute | solution.py:470
  644.5 18.0 %collective-permute-start.190 = (bf16[2,2,9,32,256]{4,3,2,1,0:T(8,128)(2,1)}, bf16[2,2,9,32,256]{4,3,2,1,0:T(8,128)(2,1)}, u32[]{:S(2)}, u32[]{:S(2)}) collective-permute-start(bf16[2,2,9,32,256]{4,3,2,1,0:T(8,128)(2,1)} %collective-permute-done.187.refs_2_), channel_id=1, source_target_pairs={{0,16},{8,24},{16,0},{24,8},{1,17},{9,25},{17,1},{25,9},{2,18},{10... | collective-permute-start | bytes 1769480 | tf_op jit(solution)/shard_map/cond/branch_1_fun/ppermute | solution.py:470
  (214 other events, 2697.7 us)
Sparse Core Ops, SparseCore 0:
  28.9 57.8 all-gather.23
  167.6 35.1 all-gather.19
  204.4 36.9 all-gather.21
  242.9 28.5 all-gather.17
  370.9 34.4 reduce-scatter.12
  408.2 37.7 reduce-scatter.14
  531.0 73.8 reduce-scatter.16

commit v5 on v4

--- a/solution.py
+++ b/solution.py
@@ -148,8 +148,11 @@
     width = taps.shape[1] if back else taps.shape[2]
     specs = [whole(v.shape) for v in rows_in]
     if chunk is not None:
-        count, _, lanes = rows_in[0].shape
-        specs = [pl.BlockSpec((count, height, lanes), lambda i: (0, chunk, 0))]
+        lanes = rows_in[0].shape[-1]
+        if len(rows_in[0].shape) == 2:
+            specs = [pl.BlockSpec((height, lanes), lambda i: (chunk, 0))]
+        else:
+            specs = [pl.BlockSpec((rows_in[0].shape[0], height, lanes), lambda i: (0, chunk, 0))]
     moved = 2 * (taps.size + sum(math.prod(s) for s in out_shapes)) + 2 * height * taps.shape[2 if back else 1]
     return pl.pallas_call(
         functools.partial(conv_kernel, len(rows_in), back, height // 2),
@@ -250,7 +253,7 @@
     if before is not None:
         inputs, specs = inputs + [before], specs + [HB]
     return pl.pallas_call(
-        functools.partial(grad_kernel, len(x_chunks), 1, len(g_chunks[0]), first, count, by_mel, shard, height),
+        functools.partial(grad_kernel, len(x_chunks), 1, len(g_chunks[0]), first, count, by_mel, shard, height // 2),
         grid=(1,),
         out_shape=jax.ShapeDtypeStruct((9 * shard, part, wide // 2), bf16),
         in_specs=specs,
@@ -375,46 +378,61 @@
     )(*packing[:2], *parts)
 
 
-def unpack_rows_kernel(frames, order, offset, length, value, out, held):
+def pool_rows_kernel(frames, order, offset, length, value, out, held):
     height = value.shape[0]
     held[:height] = value[...]
     held[height:] = jnp.zeros((frames, held.shape[1]), f32)
+    halves = frames // 2
 
     def one(k, carry):
-        target = pl.ds(pl.multiple_of(order[k] * frames, frames), frames)
-        rows = held[pl.ds(pl.multiple_of(offset[k], 8), frames)]
-        out[target] = rows * valid_rows(frames, rows.shape[1], length[k])
+        target = pl.ds(pl.multiple_of(order[k] * halves, halves), halves)
+        rows = held[pl.ds(pl.multiple_of(offset[k], 8), frames)].reshape(halves, 2, held.shape[1])
+        out[target] = jnp.sum(rows, axis=1) * valid_rows(halves, held.shape[1], lax.div(length[k], 2))
         return carry
 
     lax.fori_loop(0, order.shape[0], one, 0)
 
 
-def pack_rows_kernel(frames, order, offset, length, value, out, held):
+def spread_rows_kernel(frames, order, offset, value, out, held):
     held[...] = jnp.zeros_like(held)
+    halves = frames // 2
 
     def one(k, carry):
-        rows = value[pl.ds(pl.multiple_of(order[k] * frames, frames), frames)]
-        target = pl.ds(pl.multiple_of(offset[k], 8), frames)
-        held[target] = rows * valid_rows(frames, rows.shape[1], length[k])
+        rows = value[pl.ds(pl.multiple_of(order[k] * halves, halves), halves)]
+        rows = jnp.broadcast_to(rows[:, None, :], (halves, 2, rows.shape[1])).reshape(frames, rows.shape[1])
+        held[pl.ds(pl.multiple_of(offset[k], 8), frames)] = rows
         return carry
 
     lax.fori_loop(0, order.shape[0], one, 0)
     out[...] = held[: out.shape[0]]
 
 
-def move_rows(value, packing, frames, height, packed):
-    lanes = value.shape[1]
-    held = height if packed else value.shape[0]
+def pool_rows(value, packing, frames, clips):
+    height, lanes = value.shape
     return pl.pallas_call(
-        functools.partial(pack_rows_kernel if packed else unpack_rows_kernel, frames),
-        out_shape=jax.ShapeDtypeStruct((height, lanes), f32),
+        functools.partial(pool_rows_kernel, frames),
+        out_shape=jax.ShapeDtypeStruct((clips * frames // 2, lanes), f32),
         in_specs=[SM] * 3 + [VM],
         out_specs=VM,
-        scratch_shapes=[pltpu.VMEM((held + frames, lanes), f32)],
+        scratch_shapes=[pltpu.VMEM((height + frames, lanes), f32)],
         compiler_params=params(),
         cost_estimate=cost(0, 8 * height * lanes),
-        name="pack_rows" if packed else "unpack_rows",
+        name="pool_rows",
     )(*packing, value)
+
+
+def spread_rows(value, packing, frames, height):
+    lanes = value.shape[1]
+    return pl.pallas_call(
+        functools.partial(spread_rows_kernel, frames),
+        out_shape=jax.ShapeDtypeStruct((height, lanes), f32),
+        in_specs=[SM] * 2 + [VM],
+        out_specs=VM,
+        scratch_shapes=[pltpu.VMEM((height + frames, lanes), f32)],
+        compiler_params=params(),
+        cost_estimate=cost(0, 8 * height * lanes),
+        name="spread_rows",
+    )(*packing[:2], value)
 
 
 under_way_xy, chunks = 3, 4
@@ -485,19 +503,9 @@
     def other_dp(value, r):
         return queued("xy", value, lambda v: permute(v, "dp", dp, lambda i: i ^ r), under_way_xy)
 
-    def gather_dp(value, order):
-        one, two = other_dp(value, 1), other_dp(value, 2)
-        three = other_dp(one, 2) if order == 0 else other_dp(two, 1)
-        return [value, one, two, three]
-
-    def gather_chunks(values):
-        near = [[values[0], other_dp(values[0], 1), other_dp(values[0], 2), other_dp(values[0], 3)]]
-        for p, value in enumerate(values[1:], 1):
-            near.append([value, other_dp(value, 1), other_dp(value, 2)])
-            if p > 1:
-                near[p - 1].append(other_dp(near[p - 1][1 + (p - 1) % 2], 2 - (p - 1) % 2))
-        near[-1].append(other_dp(near[-1][1 + p % 2], 2 - p % 2))
-        return near
+    def gather_dp(value):
+        three = other_dp(value, 3)
+        return [value, other_dp(value, 1), other_dp(value, 2), three]
 
     def tied(values, *earlier):
         return [after(values[0], *earlier)] + list(values[1:])
@@ -528,15 +536,18 @@
         pieces = jnp.stack([pieces[0], other_core(pieces[1])], axis=1)
         return [pieces[0]] + [to_z(pieces[k], k, 3, *done.get(k, ())) for k in range(1, depth)]
 
-    def near_grad(parts, *earlier):
-        def along(value, r, *earlier):
-            return permute(after(value, *earlier), "dp", dp, lambda i: i ^ r)
-
+    def along(value, r, *earlier):
+        return permute(after(value, *earlier), "dp", dp, lambda i: i ^ r)
+
+    def near_start(parts):
         half = depth // 2
         low, high = jnp.stack(parts[:half]), jnp.stack(parts[half:])
-        low_one, high_two = along(low, 1), along(high, 2)
-        low_three, high_one = along(low_one, 2, high_two), along(high, 1, low_one)
-        low_two, high_three = along(low, 2, low_three, *earlier), along(high_two, 1, high_one, *earlier)
+        return low, high, along(low, 1), along(high, 2)
+
+    def near_finish(start, second=(), third=()):
+        low, high, low_one, high_two = start
+        low_three, high_one = along(low_one, 2, high_two, *second), along(high, 1, low_one, *second)
+        low_two, high_three = along(low, 2, low_three, *third), along(high_two, 1, high_one, *third)
         return [[low, low_one, low_two, low_three], [high, high_one, high_two, high_three]]
 
     def on_device(
@@ -642,14 +653,13 @@
                     total = total + other_dp(outs[r], r).astype(f32)
                 return total
 
-            maps_in, valid = pack_maps(all_maps, packing, frames, height, chunks)
+            maps_in, valid = pack_maps(all_maps, packing, frames, height, 2)
             pieces_two, across_two = weight_in(split_two, 3)
             parts = []
             for p in range(chunks):
-                value = after(maps_in[p], *())
-                outs = convolve([value], wide_one, [(step, wide)] * dp, name="conv1")
+                outs = convolve([maps_in[p // 2]], wide_one, [(step, wide)] * dp, chunk=p % 2, name="conv1")
                 parts.append(scatter_dp(outs))
-            parts = tied(parts, *pieces_two[1:2])
+            parts = tied(parts, *pieces_two[1:])
             first_out = jnp.concatenate(parts, axis=0)
 
             wide_two = expand_weight(pieces_two, across_two, table, spread, False)
@@ -667,7 +677,7 @@
             pre_one = normed_one * gain_one + shift_one
             act_one = (jax.nn.silu(pre_one) * valid).astype(bf16)
             acts = [
-                lax.all_gather(after(act_one[:half], *pieces_two[2:3]), "shard"),
+                lax.all_gather(act_one[:half], "shard"),
                 lax.all_gather(after(act_one[half:], wide_two), "shard"),
             ]
             fc_rows = fc1_weight.shape[0]
@@ -699,8 +709,7 @@
             slope_two = (sigma_two + act_two * (1.0 - sigma_two)) * valid
 
             halves = frames // 2
-            act_two = move_rows(act_two, packing, frames, rows, False)
-            pooled = jnp.sum(act_two.reshape(clips, halves, 2, wide), axis=2)
+            pooled = pool_rows(act_two, packing, frames, clips).reshape(clips, halves, wide)
             pooled = (pooled[:, :, :lane] + pooled[:, :, lane:]) / (2.0 * mels)
             half_len = all_lengths // 2
             half_ids = lax.broadcasted_iota(jnp.int32, (clips, halves), 1)
@@ -734,16 +743,15 @@
             d_pooled = d_embed[:, None, :] * (soft + pooled_valid / half_float[:, :, None])
 
             fc1_grad = dot(own_columns, d_hidden)
-            own_columns = lax.dynamic_slice_in_dim(gated, s * fc_rows, fc_rows, axis=1)
-            fc2_grad = dot(own_columns.T, d_logits)
+            own_gated = lax.dynamic_slice_in_dim(gated, s * fc_rows, fc_rows, axis=1)
+            fc2_grad = dot(own_gated.T, d_logits)
             fc1_bias_grad = jnp.sum(d_hidden.astype(f32), axis=0)
             fc2_bias_grad = jnp.sum(d_logits.astype(f32), axis=0)
             own_clips = (s * dp + d) * clip_count
             own_logits = lax.dynamic_slice_in_dim(logits, own_clips, clip_count, axis=0)
 
             d_frames = jnp.concatenate([d_pooled, d_pooled], axis=2) / (2.0 * mels)
-            d_frames = jnp.broadcast_to(d_frames[:, :, None, :], (clips, halves, 2, wide))
-            dz_two = move_rows(d_frames.reshape(rows, wide), packing, frames, height, True) * slope_two
+            dz_two = spread_rows(d_frames.reshape(clips * halves, wide), packing, frames, height) * slope_two
             shift_two_grad, shift_two_lanes = both_mels(jnp.sum(dz_two, axis=0))
             gain_two_grad, gain_two_lanes = both_mels(jnp.sum(dz_two * normed_two, axis=0))
             d_second = (
@@ -753,18 +761,16 @@
                 * valid
             ).astype(bf16)
 
-            grads_two = gather_chunks(list(d_second.reshape(chunks, step, wide)))
+            grads_two = [gather_dp(v) for v in d_second.reshape(2, half, wide)]
             parts, outs = [], []
-            for p in range(chunks):
-                ready = tied(grads_two[p], *outs[-1:], *(grads_two[p + 1][1:3] if p + 1 < chunks else ()))
-                outs += convolve(ready, wide_two, [(shard, step, wide)], back=True, name="back2")
-                if p % 2:
-                    out = jnp.concatenate(outs[-2:], axis=1)
-                    parts.append(lax.psum_scatter(out, "shard", scatter_dimension=0))
+            for p in range(2):
+                ready = tied(grads_two[p], *outs[-1:], *((own_columns,) if p else ()))
+                outs += convolve(ready, wide_two, [(shard, half, wide)], back=True, name="back2")
+                parts.append(lax.psum_scatter(outs[p], "shard", scatter_dimension=0))
 
             grad_two = None
             count = shard // 4
-            act_chunks = [(acts[p // 2], p % 2) for p in range(chunks)]
+            act_chunks = [(v, 0) for v in acts]
             for first in range(0, shard, count):
                 ready = [tied(grads_two[0], outs[-1])] + grads_two[1:]
                 grad_two = weight_grad(
@@ -783,36 +789,36 @@
                 * (dz_one - (shift_one_lanes + normed_one * gain_one_lanes) / pixel_count)
                 * valid
             ).astype(bf16)
-            values = list(d_first.reshape(chunks, step, wide))
             norm_grads = jnp.stack([gain_one_grad, shift_one_grad, gain_two_grad, shift_two_grad])
-            grads_one = gather_chunks(values)
-            sent_two = send_grad(grad_two, {2: grads_one[1][1:3], 3: grads_one[3][1:3]})
+            grads_one = [gather_dp(v) for v in d_first.reshape(2, half, wide)]
+            sent_two = send_grad(grad_two, {2: grads_one[0][1:3], 3: grads_one[1][1:3]})
             outs = []
-            for p in range(chunks):
-                ready = tied(grads_one[p], *outs[-1:], *(grads_one[p + 1][1:3] if p + 1 < chunks else ()))
-                outs += convolve(ready, wide_one, [(step, wide_in)], back=True, name="back1")
+            for p in range(2):
+                ready = tied(grads_one[p], *outs[-1:])
+                outs += convolve(ready, wide_one, [(half, wide_in)], back=True, name="back1")
             near = [permute(norm_grads, "dp", dp, lambda i, r=r: i ^ r) for r in range(1, dp)]
             norm_grads = jnp.stack(unswap([norm_grads] + near, d))
-            near_two = near_grad([after(v, grads_one[-1][3], norm_grads) for v in sent_two])
+            start_two = near_start([after(v, outs[-1], norm_grads) for v in sent_two])
 
             grad_one, d_in = None, None
             count = shard // 2
             for first in range(0, shard, count):
-                ready = [tied(grads_one[0], outs[-1], *((near_two[0][0], near_two[1][0]) if first else sent_two[1:2]))] + grads_one[1:]
+                ready = [tied(grads_one[0], outs[-1], *start_two[:2])] + grads_one[1:]
                 grad_one = weight_grad(
                     [(v, 0) for v in maps_in], ready, table, spread, lane_in, True, shard, first, count, grad_one, name="grad1",
                 )
             d_in = unpack_maps(tied(outs, grad_one), packing, frames, rows)
             d_in = d_in.reshape(shard, rows // shard, wide_in)
-            total = lax.psum_scatter(d_in, "shard", scatter_dimension=0)
             sent_one = send_grad(grad_one)
+            near_two = near_finish(start_two, sent_one[:1], sent_one[1:])
+            total = lax.psum_scatter(after(d_in, near_two[0][3], near_two[1][1], *sent_one[1:]), "shard", scatter_dimension=0)
             conv2_grad = join_grad([h for pair in zip(*near_two) for h in pair], place, dp, shard)
             total = total.reshape(dp, own_rows, wide_in)
             from_dp = [other_dp(pick(total, d ^ r), r) if r else pick(total, d) for r in range(dp)]
-            near_one = near_grad([after(v, near_two[0][2], near_two[1][3]) for v in sent_one], *from_dp[1:])
+            near_one = near_finish(near_start([after(v, near_two[0][2], near_two[1][3]) for v in sent_one]), (), from_dp[1:])
             conv1_grad = join_grad([h for pair in zip(*near_one) for h in pair], place, dp, shard)
 
-            norm_grads = after(norm_grads, sent_one[-1])
+            norm_grads = after(norm_grads, total)
             line = [norm_grads] + [permute(norm_grads, "shard", shard, lambda i, k=k: i - 2 * k) for k in range(1, depth)]
             line = roll_to(jnp.stack(line), (depth - z) % depth, 0)
             norm_grads = jnp.stack(core_order(line, other_core(line), c), axis=1)

time: 707 us -> 687 us (0.972)
  starting transfers between devices: 135 us -> 115 us
    ppermute x114 -> x102, starting transfers between devices: 134 us -> 114 us  [permute(): return lax.ppermute(value, axis, [(i, move(i) % size) for i in range(size)])]
    reduce_scatter x3, waiting for transfers between devices: 12.9 us -> 0.02 us  [the longest x2 0.01 us: after_maps(): parts.append(lax.psum_scatter(outs[p], 'shard', scatter_dimension=0))]
    pallas_call x16 -> x12, Pallas kernels: 80.3 us -> 68.5 us  [convolve(): pl.pallas_call(functools.partial(conv_kernel, len(rows_in), back, height...]
    pallas_call x6, Pallas kernels: 54.6 us -> 63.6 us  [weight_grad(): pl.pallas_call(functools.partial(grad_kernel, len(x_chunks), 1, len(g_chu...]
    ppermute x114 -> x102, waiting for transfers between devices: 232 us -> 240 us  [permute(): return lax.ppermute(value, axis, [(i, move(i) % size) for i in range(size)])]
  transfers between devices with their start and end apart: 121 -> 109, of which waited for: 49 -> 49; matrix products, arithmetic and copies ran while one was open for 10% -> 10% of each run, Pallas kernels for 22% -> 24%
where the time goes in v5:
time: 687 us; the launch traced here: 676 us
  waiting for transfers between devices  244 us (36%)
  Pallas kernels  191 us (28%)
  starting transfers between devices  115 us (17%)
  other arithmetic  47.1 us (7%)
  local copies, waits for them, and re-layouts  36.7 us (5%)
  between operations  18.8 us (3%)
  matrix products  14.2 us (2%)
  loops' own time  9.04 us (1%)
    ppermute x102, waiting for transfers between devices, permute(): return lax.ppermute(value, axis, [(i, move(i) % size) for i in range(size)])  240 us
    ppermute x102, starting transfers between devices, permute(): return lax.ppermute(value, axis, [(i, move(i) % size) for i in range(size)])  114 us
    pallas_call x12, Pallas kernels, convolve(): pl.pallas_call(functools.partial(conv_kernel, len(rows_in), back, height...  68.5 us
    pallas_call x6, Pallas kernels, weight_grad(): pl.pallas_call(functools.partial(grad_kernel, len(x_chunks), 1, len(g_chu...  63.6 us
    pallas_call x2, Pallas kernels, join_grad(): pl.pallas_call(functools.partial(join_kernel, dp, shard // 2), grid=(9,),...  20.2 us
  transfers between devices with their start and end apart: 109, of which 49 were waited for; matrix products, arithmetic and copies ran while one was open for 10% of the time, Pallas kernels for 24%

profile of v5, /device:TPU:16, one launch (start us, length us, event | category | flops | bytes accessed | tf_op | source)
XLA Modules:
  0.0 676.0 jit_solution(11535085308699024123)
XLA Ops:
  11.3 4.3 fusion.165
  42.7 29.1 %collective-permute-done.179 = bf16[4,4,640]{2,1,0:T(4,128)(2,1)S(1)} collective-permute-done((bf16[4,4,640]{2,1,0:T(4,128)(2,1)S(1)}, bf16[4,4,640]{2,1,0:T(4,128)(2,1)S(1)}, u32[]{:S(2)}, u32[]{:S(2)}) %collective-permute-start.179) | collective-permute-done | bytes 20512 | tf_op jit(solution)/shard_map/ppermute | solution.py:488
  71.8 9.0 %collective-permute-done.181 = bf16[4,4,640]{2,1,0:T(4,128)(2,1)S(1)} collective-permute-done((bf16[4,4,640]{2,1,0:T(4,128)(2,1)S(1)}, bf16[4,4,640]{2,1,0:T(4,128)(2,1)S(1)}, u32[]{:S(2)}, u32[]{:S(2)}) %collective-permute-start.181) | collective-permute-done | bytes 20512 | tf_op jit(solution)/shard_map/ppermute | solution.py:488
  91.5 4.0 split_weight.3
  98.6 569.4 %conditional.1 = (f32[1152,2048]{1,0:T(8,128)}, f32[2048]{0:T(1024)S(1)}, f32[2048]{0:T(1024)S(1)}, f32[2304,2048]{1,0:T(8,128)}, f32[2048]{0:T(1024)S(1)}, /*in...) conditional(s32[]{:T(128)} %convert_element_type.407, ...), branch_computations={%region_9.26_spmd, %region_26.43_spmd} | conditional | flops 61109813248 | bytes 752351744 | solution.py:858
  107.5 6.8 %pack_maps.3 = (bf16[1344,512]{1,0:T(8,128)(2,1)}, bf16[1344,512]{1,0:T(8,128)(2,1)}, f32[2688,128]{1,0:T(8,128)}) custom-call(s32[128]{0:T(128)} %get-tuple-element.1103.order, s32[128]{0:T(128)} %get-tuple-element.1102.offset, s32[128]{0:T(128)} %get-tuple-element.1101.length, bf16[4096,512]{1,0:T(8,128)(2,1)} %get-tuple-element.266.maps), custom_call_target="tpu_custom_call" | custom-call | bytes 16777216 | tf_op jit(solution)/shard_map/cond/branch_1_fun/pack_maps/pallas_call | solution.py:330
  134.3 3.9 conv1.14
  143.0 6.7 collective-permute-done.95
  151.1 7.2 %collective-permute-done.98 = bf16[672,128]{1,0:T(8,128)(2,1)S(1)} collective-permute-done((bf16[672,128]{1,0:T(8,128)(2,1)}, bf16[672,128]{1,0:T(8,128)(2,1)S(1)}, u32[]{:S(2)}, u32[]{:S(2)}) %collective-permute-start.98) | collective-permute-done | bytes 172064 | tf_op jit(solution)/shard_map/cond/branch_1_fun/ppermute | solution.py:488
  175.9 5.7 expand_weight.4
  190.9 13.3 %collective-permute-done.107 = bf16[64,640]{1,0:T(8,128)(2,1)S(1)} collective-permute-done((bf16[64,640]{1,0:T(8,128)(2,1)S(1)}, bf16[64,640]{1,0:T(8,128)(2,1)S(1)}, u32[]{:S(2)}, u32[]{:S(2)}) %collective-permute-start.107) | collective-permute-done | bytes 81952 | tf_op jit(solution)/shard_map/cond/branch_1_fun/ppermute | solution.py:488
  207.2 6.0 conv2.12
  216.7 6.2 conv2.13
  229.5 8.9 %collective-permute-done.116 = bf16[672,128]{1,0:T(8,128)(2,1)S(1)} collective-permute-done((bf16[672,128]{1,0:T(8,128)(2,1)}, bf16[672,128]{1,0:T(8,128)(2,1)S(1)}, u32[]{:S(2)}, u32[]{:S(2)}) %collective-permute-start.116) | collective-permute-done | bytes 172064 | tf_op jit(solution)/shard_map/cond/branch_1_fun/ppermute | solution.py:488
  244.5 6.0 conv2.14
  254.0 6.0 conv2.15
  265.5 4.8 collective-permute-done.122
  277.5 6.1 pool_rows.3
  305.9 4.0 collective-permute-done.129
  309.9 5.8 collective-permute-done.128
  327.0 4.8 spread_rows.3
  338.5 7.4 %collective-permute-done.131.refs_1_.refs_3_ = bf16[1344,128]{1,0:T(8,128)(2,1)S(1)} collective-permute-done((bf16[1344,128]{1,0:T(8,128)(2,1)S(1)}, bf16[1344,128]{1,0:T(8,128)(2,1)S(1)}, u32[]{:S(2)}, u32[]{:S(2)}) %collective-permute-start.131) | collective-permute-done | bytes 344096 | tf_op jit(solution)/shard_map/cond/branch_1_fun/ppermute | solution.py:488
  346.3 7.0 %collective-permute-done.133.refs_3_.refs_5_ = bf16[1344,128]{1,0:T(8,128)(2,1)S(1)} collective-permute-done((bf16[1344,128]{1,0:T(8,128)(2,1)S(1)}, bf16[1344,128]{1,0:T(8,128)(2,1)S(1)}, u32[]{:S(2)}, u32[]{:S(2)}) %collective-permute-start.133) | collective-permute-done | bytes 344096 | tf_op jit(solution)/shard_map/cond/branch_1_fun/ppermute | solution.py:488
  354.0 9.1 %back2.6 = bf16[8,1344,128]{2,1,0:T(8,128)(2,1)} custom-call(bf16[1344,128]{1,0:T(8,128)(2,1)} %copy-done.35, bf16[1344,128]{1,0:T(8,128)(2,1)} %copy-done.43, bf16[1344,128]{1,0:T(8,128)(2,1)} %copy-done.44, bf16[1344,128]{1,0:T(8,128)(2,1)} %copy-done.45, bf16[3,1024,512]{2,1,0:T(8,128)(2,1)} %bitcast.405), custom_call_target="tpu_custom_call" | custom-call | flops 4227858432 | bytes 7274496 | tf_op jit(solution)/shard_map/cond/branch_1_fun/back2/pallas_call | solution.py:157
  372.9 6.2 collective-permute-done.137.refs_1_.refs_7_
  379.1 5.8 collective-permute-done.138.refs_2_.refs_8_
  386.5 9.2 %back2.7 = bf16[8,1344,128]{2,1,0:T(8,128)(2,1)} custom-call(bf16[1344,128]{1,0:T(8,128)(2,1)} %copy-done.36, bf16[1344,128]{1,0:T(8,128)(2,1)} %copy-done.46, bf16[1344,128]{1,0:T(8,128)(2,1)} %copy-done.47, bf16[1344,128]{1,0:T(8,128)(2,1)} %copy-done.48, bf16[3,1024,512]{2,1,0:T(8,128)(2,1)} %bitcast.406), custom_call_target="tpu_custom_call" | custom-call | flops 4227858432 | bytes 7274496 | tf_op jit(solution)/shard_map/cond/branch_1_fun/back2/pallas_call | solution.py:157
  396.3 9.7 %grad2.12.refs_11_ = bf16[72,64,256]{2,1,0:T(8,128)(2,1)} custom-call(s32[72]{0:T(128)S(1)} %copy-done.158, bf16[8,1344,128]{2,1,0:T(8,128)(2,1)} %bitcast.371, bf16[8,1344,128]{2,1,0:T(8,128)(2,1)} %bitcast.377, bf16[1344,128]{1,0:T(8,128)(2,1)} %copy-done.35, bf16[1344,128]{1,0:T(8,128)(2,1)} %copy-done.43, bf16[1344,128]{1,0:T(8,128)(2,1)} %copy-done.44, ...), custom_call_target="tpu_custom_call" | custom-call | flops 2113929216 | bytes 4718592 | tf_op jit(solution)/shard_map/cond/branch_1_fun/grad2/pallas_call | solution.py:255
  406.0 9.7 %grad2.13.refs_11_ = bf16[72,64,256]{2,1,0:T(8,128)(2,1)} custom-call(s32[72]{0:T(128)S(1)} %copy-done.158, bf16[8,1344,128]{2,1,0:T(8,128)(2,1)} %bitcast.372, bf16[8,1344,128]{2,1,0:T(8,128)(2,1)} %bitcast.378, bf16[1344,128]{1,0:T(8,128)(2,1)} %copy-done.35, bf16[1344,128]{1,0:T(8,128)(2,1)} %copy-done.43, ...), custom_call_target="tpu_custom_call", output_to_operand_aliasing={{}: (12, {})} | custom-call | flops 2113929216 | bytes 4718592 | tf_op jit(solution)/shard_map/cond/branch_1_fun/grad2/pallas_call | solution.py:255
  415.7 9.8 %grad2.14.refs_11_ = bf16[72,64,256]{2,1,0:T(8,128)(2,1)} custom-call(s32[72]{0:T(128)S(1)} %copy-done.158, bf16[8,1344,128]{2,1,0:T(8,128)(2,1)} %bitcast.373, bf16[8,1344,128]{2,1,0:T(8,128)(2,1)} %bitcast.379, bf16[1344,128]{1,0:T(8,128)(2,1)} %copy-done.35, bf16[1344,128]{1,0:T(8,128)(2,1)} %copy-done.43, ...), custom_call_target="tpu_custom_call", output_to_operand_aliasing={{}: (12, {})} | custom-call | flops 2113929216 | bytes 4718592 | tf_op jit(solution)/shard_map/cond/branch_1_fun/grad2/pallas_call | solution.py:255
  425.5 10.2 %grad2.15 = bf16[72,64,256]{2,1,0:T(8,128)(2,1)} custom-call(s32[72]{0:T(128)S(1)} %copy-done.158, bf16[8,1344,128]{2,1,0:T(8,128)(2,1)} %bitcast.374, bf16[8,1344,128]{2,1,0:T(8,128)(2,1)} %bitcast.380, bf16[1344,128]{1,0:T(8,128)(2,1)} %copy-done.35, bf16[1344,128]{1,0:T(8,128)(2,1)} %copy-done.43, ...), custom_call_target="tpu_custom_call", output_to_operand_aliasing={{}: (12, {})} | custom-call | flops 2113929216 | bytes 4718592 | tf_op jit(solution)/shard_map/cond/branch_1_fun/grad2/pallas_call | solution.py:255
  447.8 4.8 collective-permute-done.140.refs_1_.refs_3_
  459.8 4.6 collective-permute-done.142.refs_3_.refs_5_
  465.9 4.3 collective-permute-start.151
  473.8 5.4 back1.6.refs_0_
  479.9 5.4 back1.7.refs_1_
  485.4 11.8 %collective-permute-done.150 = bf16[2,9,64,256]{3,2,1,0:T(8,128)(2,1)S(1)} collective-permute-done((bf16[2,9,64,256]{3,2,1,0:T(8,128)(2,1)S(1)}, bf16[2,9,64,256]{3,2,1,0:T(8,128)(2,1)S(1)}, u32[]{:S(2)}, u32[]{:S(2)}) %collective-permute-start.150) | collective-permute-done | bytes 589856 | tf_op jit(solution)/shard_map/cond/branch_1_fun/ppermute | solution.py:488
  498.1 10.6 %collective-permute-done.152 = bf16[2,9,64,256]{3,2,1,0:T(8,128)(2,1)S(1)} collective-permute-done((bf16[2,9,64,256]{3,2,1,0:T(8,128)(2,1)S(1)}, bf16[2,9,64,256]{3,2,1,0:T(8,128)(2,1)S(1)}, u32[]{:S(2)}, u32[]{:S(2)}) %collective-permute-start.152) | collective-permute-done | bytes 589856 | tf_op jit(solution)/shard_map/cond/branch_1_fun/ppermute | solution.py:488
  511.6 12.1 %grad1.6.refs_11_ = bf16[72,32,256]{2,1,0:T(8,128)(2,1)} custom-call(s32[72]{0:T(128)S(1)} %copy-done.158, bf16[1344,512]{1,0:T(8,128)(2,1)} %get-tuple-element.267.refs_0_, bf16[1344,512]{1,0:T(8,128)(2,1)} %get-tuple-element.284.refs_0_.refs_1_, bf16[1344,128]{1,0:T(8,128)(2,1)} %copy-done.79, bf16[1344,128]{1,0:T(8,128)(2,1)} %copy-done.122, ...), custom_call_target="tpu_custom_call" | custom-call | flops 2113929216 | bytes 4718592 | tf_op jit(solution)/shard_map/cond/branch_1_fun/grad1/pallas_call | solution.py:255
  523.7 12.1 %grad1.7 = bf16[72,32,256]{2,1,0:T(8,128)(2,1)} custom-call(s32[72]{0:T(128)S(1)} %copy-done.158, bf16[1344,512]{1,0:T(8,128)(2,1)} %get-tuple-element.267.refs_0_, bf16[1344,512]{1,0:T(8,128)(2,1)} %get-tuple-element.284.refs_0_.refs_1_, bf16[1344,128]{1,0:T(8,128)(2,1)} %copy-done.79, ...), custom_call_target="tpu_custom_call", output_to_operand_aliasing={{}: (12, {})} | custom-call | flops 2113929216 | bytes 4718592 | tf_op jit(solution)/shard_map/cond/branch_1_fun/grad1/pallas_call | solution.py:255
  546.3 5.8 unpack_maps.3
  552.1 4.2 collective-permute-done.159
  556.3 11.4 %collective-permute-done.160 = bf16[2,9,32,256]{3,2,1,0:T(8,128)(2,1)} collective-permute-done((bf16[2,9,32,256]{3,2,1,0:T(8,128)(2,1)S(1)}, bf16[2,9,32,256]{3,2,1,0:T(8,128)(2,1)}, u32[]{:S(2)}, u32[]{:S(2)}) %collective-permute-start.160) | collective-permute-done | bytes 294944 | tf_op jit(solution)/shard_map/cond/branch_1_fun/ppermute | solution.py:488
  576.2 25.7 %collective-permute-done.165.refs_7_ = bf16[2,2,9,64,256]{4,3,2,1,0:T(8,128)(2,1)} collective-permute-done((bf16[2,2,9,64,256]{4,3,2,1,0:T(8,128)(2,1)S(1)}, bf16[2,2,9,64,256]{4,3,2,1,0:T(8,128)(2,1)}, u32[]{:S(2)}, u32[]{:S(2)}) %collective-permute-start.165) | collective-permute-done | bytes 1179680 | tf_op jit(solution)/shard_map/cond/branch_1_fun/ppermute | solution.py:488
  613.6 11.7 %join_grad.7 = f32[9,4,64,2048]{3,2,1,0:T(8,128)} custom-call(s32[2]{0:T(128)S(1)} %copy-done.166, bf16[2,2,9,64,256]{4,3,2,1,0:T(8,128)(2,1)} %copy-done.54, bf16[2,2,9,64,256]{4,3,2,1,0:T(8,128)(2,1)} %copy-done.56, bf16[2,2,9,64,256]{4,3,2,1,0:T(8,128)(2,1)} %copy-done.86, bf16[2,2,9,64,256]{4,3,2,1,0:T(8,128)(2,1)} %copy-done.92, ...), custom_call_target="tpu_custom_call" | custom-call | bytes 28311552 | tf_op jit(solution)/shard_map/cond/branch_1_fun/join_grad/pallas_call | solution.py:291
  637.0 5.7 collective-permute-done.169.refs_6_
  650.1 7.5 %collective-permute-done.171.refs_7_ = bf16[2,2,9,32,256]{4,3,2,1,0:T(8,128)(2,1)S(1)} collective-permute-done((bf16[2,2,9,32,256]{4,3,2,1,0:T(8,128)(2,1)}, bf16[2,2,9,32,256]{4,3,2,1,0:T(8,128)(2,1)S(1)}, u32[]{:S(2)}, u32[]{:S(2)}) %collective-permute-start.171) | collective-permute-done | bytes 589856 | tf_op jit(solution)/shard_map/cond/branch_1_fun/ppermute | solution.py:488
  659.2 8.6 %join_grad.6 = f32[9,4,32,2048]{3,2,1,0:T(8,128)} custom-call(s32[2]{0:T(128)S(1)} %copy-done.166, bf16[2,2,9,32,256]{4,3,2,1,0:T(8,128)(2,1)} %copy-done.67, bf16[2,2,9,32,256]{4,3,2,1,0:T(8,128)(2,1)} %pad_maximum_fusion.33.refs_1_, bf16[2,2,9,32,256]{4,3,2,1,0:T(8,128)(2,1)} %collective-permute-done.166.refs_2_, ...), custom_call_target="tpu_custom_call" | custom-call | bytes 14155776 | tf_op jit(solution)/shard_map/cond/branch_1_fun/join_grad/pallas_call | solution.py:291
  (674 shorter events, 263.8 us)
Async XLA Ops:
  7.2 90.8 %all-gather.24.cloned.1.call-start = ((), (), s32[]{:S(2)}) async-start(), calls=%async_computation.18 | async-start | bytes 4718592 | tf_op jit(solution)/shard_map/all_gather | solution.py:622
  32.5 56.3 %collective-permute-start.187 = (bf16[2,9,32,256]{3,2,1,0:T(8,128)(2,1)S(1)}, bf16[2,9,32,256]{3,2,1,0:T(8,128)(2,1)S(1)}, u32[]{:S(2)}, u32[]{:S(2)}) collective-permute-start(bf16[2,9,32,256]{3,2,1,0:T(8,128)(2,1)S(1)} %copy-done.218), channel_id=1, source_target_pairs={{0,4},{1,5},{2,6},{3,7},{4,0},{5,1},{6,2},{7,3},{8,12},{9,13},{10,... | collective-permute-start | bytes 884744 | tf_op jit(solution)/shard_map/ppermute | solution.py:488
  34.0 54.9 %collective-permute-start.188 = (bf16[2,9,32,256]{3,2,1,0:T(8,128)(2,1)S(1)}, bf16[2,9,32,256]{3,2,1,0:T(8,128)(2,1)S(1)}, u32[]{:S(2)}, u32[]{:S(2)}) collective-permute-start(bf16[2,9,32,256]{3,2,1,0:T(8,128)(2,1)S(1)} %copy-done.217), channel_id=1, source_target_pairs={{0,2},{1,3},{2,4},{3,5},{4,6},{5,7},{6,0},{7,1},{8,10},{9,11},{10,... | collective-permute-start | bytes 884744 | tf_op jit(solution)/shard_map/ppermute | solution.py:488
  37.7 34.1 %collective-permute-start.180 = (bf16[4,4,640]{2,1,0:T(4,128)(2,1)S(1)}, bf16[4,4,640]{2,1,0:T(4,128)(2,1)S(1)}, u32[]{:S(2)}, u32[]{:S(2)}) collective-permute-start(bf16[4,4,640]{2,1,0:T(4,128)(2,1)S(1)} %pad_maximum_fusion.55), channel_id=1, source_target_pairs={{0,4},{1,5},{2,6},{3,7},{4,0},{5,1},{6,2},{7,3},{8,12},{9,13},{10,... | collective-permute-start | bytes 61448 | tf_op jit(solution)/shard_map/ppermute | solution.py:488
  40.6 31.1 %collective-permute-start.179 = (bf16[4,4,640]{2,1,0:T(4,128)(2,1)S(1)}, bf16[4,4,640]{2,1,0:T(4,128)(2,1)S(1)}, u32[]{:S(2)}, u32[]{:S(2)}) collective-permute-start(bf16[4,4,640]{2,1,0:T(4,128)(2,1)S(1)} %pad_maximum_fusion.55), channel_id=1, source_target_pairs={{0,6},{1,7},{2,0},{3,1},{4,2},{5,3},{6,4},{7,5},{8,14},{9,15},{10,... | collective-permute-start | bytes 61448 | tf_op jit(solution)/shard_map/ppermute | solution.py:488
  40.6 40.1 %collective-permute-start.181 = (bf16[4,4,640]{2,1,0:T(4,128)(2,1)S(1)}, bf16[4,4,640]{2,1,0:T(4,128)(2,1)S(1)}, u32[]{:S(2)}, u32[]{:S(2)}) collective-permute-start(bf16[4,4,640]{2,1,0:T(4,128)(2,1)S(1)} %pad_maximum_fusion.55), channel_id=1, source_target_pairs={{0,2},{1,3},{2,4},{3,5},{4,6},{5,7},{6,0},{7,1},{8,10},{9,11},{10,... | collective-permute-start | bytes 61448 | tf_op jit(solution)/shard_map/ppermute | solution.py:488
  105.7 101.5 %all-gather.20.cloned.1.call-start = ((), (), s32[]{:S(2)}) async-start(), calls=%async_computation.16 | async-start | bytes 3096576 | tf_op jit(solution)/shard_map/cond/branch_1_fun/all_gather | solution.py:680
  105.8 54.6 %collective-permute-start.93 = (bf16[2,9,64,256]{3,2,1,0:T(8,128)(2,1)}, bf16[2,9,64,256]{3,2,1,0:T(8,128)(2,1)S(1)}, u32[]{:S(2)}, u32[]{:S(2)}) collective-permute-start(bf16[2,9,64,256]{3,2,1,0:T(8,128)(2,1)} %get-tuple-element.275), channel_id=1, source_target_pairs={{0,2},{1,3},{2,4},{3,5},{4,6},{5,7},{6,0},{7,1},{8,10},{9,11},{10,... | collective-permute-start | bytes 1769480 | tf_op jit(solution)/shard_map/cond/branch_1_fun/ppermute | solution.py:488
  106.4 55.6 %collective-permute-start.92 = (bf16[2,9,64,256]{3,2,1,0:T(8,128)(2,1)}, bf16[2,9,64,256]{3,2,1,0:T(8,128)(2,1)}, u32[]{:S(2)}, u32[]{:S(2)}) collective-permute-start(bf16[2,9,64,256]{3,2,1,0:T(8,128)(2,1)} %get-tuple-element.274), channel_id=1, source_target_pairs={{0,4},{1,5},{2,6},{3,7},{4,0},{5,1},{6,2},{7,3},{8,12},{9,13},{10,... | collective-permute-start | bytes 1769480 | tf_op jit(solution)/shard_map/cond/branch_1_fun/ppermute | solution.py:488
  119.5 18.8 %collective-permute-start.89 = (bf16[672,128]{1,0:T(8,128)(2,1)}, bf16[672,128]{1,0:T(8,128)(2,1)S(1)}, u32[]{:S(2)}, u32[]{:S(2)}) collective-permute-start(bf16[672,128]{1,0:T(8,128)(2,1)} %get-tuple-element.271), channel_id=1, source_target_pairs={{0,16},{8,24},{16,0},{24,8},{1,17},{9,25},{17,1},{25,9},{2,18},{10... | collective-permute-start | bytes 516104 | tf_op jit(solution)/shard_map/cond/branch_1_fun/ppermute | solution.py:488
  126.9 14.0 %collective-permute-start.94 = (bf16[672,128]{1,0:T(8,128)(2,1)}, bf16[672,128]{1,0:T(8,128)(2,1)S(1)}, u32[]{:S(2)}, u32[]{:S(2)}) collective-permute-start(bf16[672,128]{1,0:T(8,128)(2,1)} %get-tuple-element.279), channel_id=1, source_target_pairs={{0,8},{8,0},{16,24},{24,16},{1,9},{9,1},{17,25},{25,17},{2,10},{10... | collective-permute-start | bytes 516104 | tf_op jit(solution)/shard_map/cond/branch_1_fun/ppermute | solution.py:488
  138.2 23.8 %collective-permute-start.91 = (bf16[2,9,64,256]{3,2,1,0:T(8,128)(2,1)S(1)}, bf16[2,9,64,256]{3,2,1,0:T(8,128)(2,1)S(1)}, u32[]{:S(2)}, u32[]{:S(2)}) collective-permute-start(bf16[2,9,64,256]{3,2,1,0:T(8,128)(2,1)S(1)} %copy-done.211), channel_id=1, source_target_pairs={{0,6},{1,7},{2,0},{3,1},{4,2},{5,3},{6,4},{7,5},{8,14},{9,15},{10,... | collective-permute-start | bytes 1769480 | tf_op jit(solution)/shard_map/cond/branch_1_fun/ppermute | solution.py:488
  168.7 75.9 %all-gather.22.cloned.1.call-start = ((), (), s32[]{:S(2)}) async-start(), calls=%async_computation.17 | async-start | bytes 3096576 | tf_op jit(solution)/shard_map/cond/branch_1_fun/all_gather | solution.py:681
  181.6 116.7 %all-gather.18.cloned.1.call-start = ((), (), s32[]{:S(2)}) async-start(), calls=%async_computation.12 | async-start | bytes 2359296 | tf_op jit(solution)/shard_map/cond/branch_1_fun/all_gather | solution.py:685
  186.0 18.2 %collective-permute-start.109 = (bf16[64,640]{1,0:T(8,128)(2,1)S(1)}, bf16[64,640]{1,0:T(8,128)(2,1)S(1)}, u32[]{:S(2)}, u32[]{:S(2)}) collective-permute-start(bf16[64,640]{1,0:T(8,128)(2,1)S(1)} %pad_dynamic-slice_fusion.1), channel_id=1, source_target_pairs={{0,2},{1,3},{2,4},{3,5},{4,6},{5,7},{6,0},{7,1},{8,10},{9,11},{10,... | collective-permute-start | bytes 245768 | tf_op jit(solution)/shard_map/cond/branch_1_fun/ppermute | solution.py:488
  186.8 17.4 %collective-permute-start.108 = (bf16[64,640]{1,0:T(8,128)(2,1)S(1)}, bf16[64,640]{1,0:T(8,128)(2,1)S(1)}, u32[]{:S(2)}, u32[]{:S(2)}) collective-permute-start(bf16[64,640]{1,0:T(8,128)(2,1)S(1)} %pad_dynamic-slice_fusion.1), channel_id=1, source_target_pairs={{0,4},{1,5},{2,6},{3,7},{4,0},{5,1},{6,2},{7,3},{8,12},{9,13},{10,... | collective-permute-start | bytes 245768 | tf_op jit(solution)/shard_map/cond/branch_1_fun/ppermute | solution.py:488
  188.3 15.9 %collective-permute-start.107 = (bf16[64,640]{1,0:T(8,128)(2,1)S(1)}, bf16[64,640]{1,0:T(8,128)(2,1)S(1)}, u32[]{:S(2)}, u32[]{:S(2)}) collective-permute-start(bf16[64,640]{1,0:T(8,128)(2,1)S(1)} %pad_dynamic-slice_fusion.1), channel_id=1, source_target_pairs={{0,6},{1,7},{2,0},{3,1},{4,2},{5,3},{6,4},{7,5},{8,14},{9,15},{10,... | collective-permute-start | bytes 245768 | tf_op jit(solution)/shard_map/cond/branch_1_fun/ppermute | solution.py:488
  205.2 234.0 %reduce-scatter.13.cloned.1.call-start = ((), (), s32[]{:S(2)}) async-start(), calls=%async_computation.13 | async-start | bytes 3096576 | tf_op jit(solution)/shard_map/cond/branch_1_fun/reduce_scatter | solution.py:769
  222.9 64.9 %collective-permute-start.112 = (bf16[4,64,640]{2,1,0:T(8,128)(2,1)}, bf16[4,64,640]{2,1,0:T(8,128)(2,1)}, u32[]{:S(2)}, u32[]{:S(2)}) collective-permute-start(bf16[4,64,640]{2,1,0:T(8,128)(2,1)} %constant_dynamic-slice_fusion.9), channel_id=1, source_target_pairs={{0,8},{8,0},{16,24},{24,16},{1,9},{9,1},{17,25},{25,17},{2,10},{10... | collective-permute-start | bytes 983048 | tf_op jit(solution)/shard_map/cond/branch_1_fun/ppermute | solution.py:488
  224.4 63.5 %collective-permute-start.111 = (bf16[4,64,640]{2,1,0:T(8,128)(2,1)}, bf16[4,64,640]{2,1,0:T(8,128)(2,1)}, u32[]{:S(2)}, u32[]{:S(2)}) collective-permute-start(bf16[4,64,640]{2,1,0:T(8,128)(2,1)} %constant_dynamic-slice_fusion.9), channel_id=1, source_target_pairs={{0,16},{8,24},{16,0},{24,8},{1,17},{9,25},{17,1},{25,9},{2,18},{10... | collective-permute-start | bytes 983048 | tf_op jit(solution)/shard_map/cond/branch_1_fun/ppermute | solution.py:488
  226.4 14.2 %collective-permute-start.115 = (bf16[672,128]{1,0:T(8,128)(2,1)}, bf16[672,128]{1,0:T(8,128)(2,1)S(1)}, u32[]{:S(2)}, u32[]{:S(2)}) collective-permute-start(bf16[672,128]{1,0:T(8,128)(2,1)} %get-tuple-element.324), channel_id=1, source_target_pairs={{0,16},{8,24},{16,0},{24,8},{1,17},{9,25},{17,1},{25,9},{2,18},{10... | collective-permute-start | bytes 516104 | tf_op jit(solution)/shard_map/cond/branch_1_fun/ppermute | solution.py:488
  270.3 17.5 %collective-permute-start.110 = (bf16[4,64,640]{2,1,0:T(8,128)(2,1)}, bf16[4,64,640]{2,1,0:T(8,128)(2,1)S(1)}, u32[]{:S(2)}, u32[]{:S(2)}) collective-permute-start(bf16[4,64,640]{2,1,0:T(8,128)(2,1)} %constant_dynamic-slice_fusion.9), channel_id=1, source_target_pairs={{0,24},{8,16},{16,8},{24,0},{1,25},{9,17},{17,9},{25,1},{2,26},{10... | collective-permute-start | bytes 983048 | tf_op jit(solution)/shard_map/cond/branch_1_fun/ppermute | solution.py:488
  296.9 20.2 %collective-permute-start.113 = (bf16[4,4,64,640]{3,2,1,0:T(8,128)(2,1)}, bf16[4,4,64,640]{3,2,1,0:T(8,128)(2,1)}, u32[]{:S(2)}, u32[]{:S(2)}) collective-permute-start(bf16[4,4,64,640]{3,2,1,0:T(8,128)(2,1)} %pad_maximum_fusion.27), channel_id=1, source_target_pairs={{0,1},{1,0},{2,3},{3,2},{4,5},{5,4},{6,7},{7,6},{8,9},{9,8},{10,11... | collective-permute-start | bytes 3932168 | tf_op jit(solution)/shard_map/cond/branch_1_fun/ppermute | solution.py:488
  302.1 13.7 %collective-permute-start.128 = (bf16[64,2048]{1,0:T(8,128)(2,1)S(1)}, bf16[64,2048]{1,0:T(8,128)(2,1)}, u32[]{:S(2)}, u32[]{:S(2)}) collective-permute-start(bf16[64,2048]{1,0:T(8,128)(2,1)S(1)} %convolution_convert_fusion.1), channel_id=1, source_target_pairs={{0,16},{8,24},{16,0},{24,8},{1,17},{9,25},{17,1},{25,9},{2,18},{10... | collective-permute-start | bytes 786440 | tf_op jit(solution)/shard_map/cond/branch_1_fun/ppermute | solution.py:488
  337.0 16.3 %collective-permute-start.133 = (bf16[1344,128]{1,0:T(8,128)(2,1)S(1)}, bf16[1344,128]{1,0:T(8,128)(2,1)S(1)}, u32[]{:S(2)}, u32[]{:S(2)}) collective-permute-start(bf16[1344,128]{1,0:T(8,128)(2,1)S(1)} %get-tuple-element.361.refs_0_.refs_2_), channel_id=1, source_target_pairs={{0,24},{8,16},{16,8},{24,0},{1,25},{9,17},{17,9},{25,1},{2,26},{10... | collective-permute-start | bytes 1032200 | tf_op jit(solution)/shard_map/cond/branch_1_fun/ppermute | solution.py:488
  363.2 75.9 %reduce-scatter.15.cloned.1.call-start = ((), (), s32[]{:S(2)}) async-start(), calls=%async_computation.14 | async-start | bytes 3096576 | tf_op jit(solution)/shard_map/cond/branch_1_fun/reduce_scatter | solution.py:769
  369.4 15.5 %collective-permute-start.138 = (bf16[1344,128]{1,0:T(8,128)(2,1)S(1)}, bf16[1344,128]{1,0:T(8,128)(2,1)S(1)}, u32[]{:S(2)}, u32[]{:S(2)}) collective-permute-start(bf16[1344,128]{1,0:T(8,128)(2,1)S(1)} %get-tuple-element.360.refs_0_.refs_6_), channel_id=1, source_target_pairs={{0,16},{8,24},{16,0},{24,8},{1,17},{9,25},{17,1},{25,9},{2,18},{10... | collective-permute-start | bytes 1032200 | tf_op jit(solution)/shard_map/cond/branch_1_fun/ppermute | solution.py:488
  370.4 14.5 %collective-permute-start.139 = (bf16[1344,128]{1,0:T(8,128)(2,1)S(1)}, bf16[1344,128]{1,0:T(8,128)(2,1)S(1)}, u32[]{:S(2)}, u32[]{:S(2)}) collective-permute-start(bf16[1344,128]{1,0:T(8,128)(2,1)S(1)} %get-tuple-element.360.refs_0_.refs_6_), channel_id=1, source_target_pairs={{0,24},{8,16},{16,8},{24,0},{1,25},{9,17},{17,9},{25,1},{2,26},{10... | collective-permute-start | bytes 1032200 | tf_op jit(solution)/shard_map/cond/branch_1_fun/ppermute | solution.py:488
  395.7 232.0 %reduce-scatter.17.cloned.1.call-start = ((), (), s32[]{:S(2)}) async-start(), calls=%async_computation.15 | async-start | bytes 4718592 | tf_op jit(solution)/shard_map/cond/branch_1_fun/reduce_scatter | solution.py:814
  455.6 41.6 %collective-permute-start.150 = (bf16[2,9,64,256]{3,2,1,0:T(8,128)(2,1)S(1)}, bf16[2,9,64,256]{3,2,1,0:T(8,128)(2,1)S(1)}, u32[]{:S(2)}, u32[]{:S(2)}) collective-permute-start(bf16[2,9,64,256]{3,2,1,0:T(8,128)(2,1)S(1)} %get-tuple-element.371), channel_id=1, source_target_pairs={{0,2},{1,3},{2,4},{3,5},{4,6},{5,7},{6,0},{7,1},{8,10},{9,11},{10,... | collective-permute-start | bytes 1769480 | tf_op jit(solution)/shard_map/cond/branch_1_fun/ppermute | solution.py:488
  456.9 14.3 %collective-permute-start.143 = (bf16[1344,128]{1,0:T(8,128)(2,1)S(1)}, bf16[1344,128]{1,0:T(8,128)(2,1)S(1)}, u32[]{:S(2)}, u32[]{:S(2)}) collective-permute-start(bf16[1344,128]{1,0:T(8,128)(2,1)S(1)} %get-tuple-element.369.refs_0_.refs_6_), channel_id=1, source_target_pairs={{0,8},{8,0},{16,24},{24,16},{1,9},{9,1},{17,25},{25,17},{2,10},{10... | collective-permute-start | bytes 1032200 | tf_op jit(solution)/shard_map/cond/branch_1_fun/ppermute | solution.py:488
  457.7 14.1 %collective-permute-start.144 = (bf16[1344,128]{1,0:T(8,128)(2,1)S(1)}, bf16[1344,128]{1,0:T(8,128)(2,1)S(1)}, u32[]{:S(2)}, u32[]{:S(2)}) collective-permute-start(bf16[1344,128]{1,0:T(8,128)(2,1)S(1)} %get-tuple-element.369.refs_0_.refs_6_), channel_id=1, source_target_pairs={{0,16},{8,24},{16,0},{24,8},{1,17},{9,25},{17,1},{25,9},{2,18},{10... | collective-permute-start | bytes 1032200 | tf_op jit(solution)/shard_map/cond/branch_1_fun/ppermute | solution.py:488
  464.4 14.8 %collective-permute-start.145 = (bf16[1344,128]{1,0:T(8,128)(2,1)S(1)}, bf16[1344,128]{1,0:T(8,128)(2,1)S(1)}, u32[]{:S(2)}, u32[]{:S(2)}) collective-permute-start(bf16[1344,128]{1,0:T(8,128)(2,1)S(1)} %get-tuple-element.369.refs_0_.refs_6_), channel_id=1, source_target_pairs={{0,24},{8,16},{16,8},{24,0},{1,25},{9,17},{17,9},{25,1},{2,26},{10... | collective-permute-start | bytes 1032200 | tf_op jit(solution)/shard_map/cond/branch_1_fun/ppermute | solution.py:488
  465.9 32.2 %collective-permute-start.151 = (bf16[2,9,64,256]{3,2,1,0:T(8,128)(2,1)S(1)}, bf16[2,9,64,256]{3,2,1,0:T(8,128)(2,1)S(1)}, u32[]{:S(2)}, u32[]{:S(2)}) collective-permute-start(bf16[2,9,64,256]{3,2,1,0:T(8,128)(2,1)S(1)} %get-tuple-element.374), channel_id=1, source_target_pairs={{0,4},{1,5},{2,6},{3,7},{4,0},{5,1},{6,2},{7,3},{8,12},{9,13},{10,... | collective-permute-start | bytes 1769480 | tf_op jit(solution)/shard_map/cond/branch_1_fun/ppermute | solution.py:488
  472.5 36.2 %collective-permute-start.152 = (bf16[2,9,64,256]{3,2,1,0:T(8,128)(2,1)S(1)}, bf16[2,9,64,256]{3,2,1,0:T(8,128)(2,1)S(1)}, u32[]{:S(2)}, u32[]{:S(2)}) collective-permute-start(bf16[2,9,64,256]{3,2,1,0:T(8,128)(2,1)S(1)} %get-tuple-element.377), channel_id=1, source_target_pairs={{0,6},{1,7},{2,0},{3,1},{4,2},{5,3},{6,4},{7,5},{8,14},{9,15},{10,... | collective-permute-start | bytes 1769480 | tf_op jit(solution)/shard_map/cond/branch_1_fun/ppermute | solution.py:488
  497.3 42.8 %collective-permute-start.153 = (bf16[2,2,9,64,256]{4,3,2,1,0:T(8,128)(2,1)S(1)}, bf16[2,2,9,64,256]{4,3,2,1,0:T(8,128)(2,1)S(1)}, u32[]{:S(2)}, u32[]{:S(2)}) collective-permute-start(bf16[2,2,9,64,256]{4,3,2,1,0:T(8,128)(2,1)S(1)} %pad_maximum_fusion.29.refs_0_), channel_id=1, source_target_pairs={{0,8},{8,0},{16,24},{24,16},{1,9},{9,1},{17,25},{25,17},{2,10},{10... | collective-permute-start | bytes 3538952 | tf_op jit(solution)/shard_map/cond/branch_1_fun/ppermute | solution.py:488
  510.7 30.4 %collective-permute-start.154 = (bf16[2,2,9,64,256]{4,3,2,1,0:T(8,128)(2,1)S(1)}, bf16[2,2,9,64,256]{4,3,2,1,0:T(8,128)(2,1)S(1)}, u32[]{:S(2)}, u32[]{:S(2)}) collective-permute-start(bf16[2,2,9,64,256]{4,3,2,1,0:T(8,128)(2,1)S(1)} %pad_maximum_fusion.30.refs_1_), channel_id=1, source_target_pairs={{0,16},{8,24},{16,0},{24,8},{1,17},{9,25},{17,1},{25,9},{2,18},{10... | collective-permute-start | bytes 3538952 | tf_op jit(solution)/shard_map/cond/branch_1_fun/ppermute | solution.py:488
  540.1 30.7 %collective-permute-start.157 = (bf16[2,2,9,64,256]{4,3,2,1,0:T(8,128)(2,1)S(1)}, bf16[2,2,9,64,256]{4,3,2,1,0:T(8,128)(2,1)S(1)}, u32[]{:S(2)}, u32[]{:S(2)}) collective-permute-start(bf16[2,2,9,64,256]{4,3,2,1,0:T(8,128)(2,1)S(1)} %pad_maximum_fusion.30.refs_1_), channel_id=1, source_target_pairs={{0,8},{8,0},{16,24},{24,16},{1,9},{9,1},{17,25},{25,17},{2,10},{10... | collective-permute-start | bytes 3538952 | tf_op jit(solution)/shard_map/cond/branch_1_fun/ppermute | solution.py:488
  541.1 29.6 %collective-permute-start.156 = (bf16[2,2,9,64,256]{4,3,2,1,0:T(8,128)(2,1)S(1)}, bf16[2,2,9,64,256]{4,3,2,1,0:T(8,128)(2,1)S(1)}, u32[]{:S(2)}, u32[]{:S(2)}) collective-permute-start(bf16[2,2,9,64,256]{4,3,2,1,0:T(8,128)(2,1)S(1)} %collective-permute-done.153.refs_2_), channel_id=1, source_target_pairs={{0,16},{8,24},{16,0},{24,8},{1,17},{9,25},{17,1},{25,9},{2,18},{10... | collective-permute-start | bytes 3538952 | tf_op jit(solution)/shard_map/cond/branch_1_fun/ppermute | solution.py:488
  542.2 14.1 %collective-permute-start.159 = (bf16[2,9,32,256]{3,2,1,0:T(8,128)(2,1)}, bf16[2,9,32,256]{3,2,1,0:T(8,128)(2,1)}, u32[]{:S(2)}, u32[]{:S(2)}) collective-permute-start(bf16[2,9,32,256]{3,2,1,0:T(8,128)(2,1)} %get-tuple-element.384), channel_id=1, source_target_pairs={{0,4},{1,5},{2,6},{3,7},{4,0},{5,1},{6,2},{7,3},{8,12},{9,13},{10,... | collective-permute-start | bytes 884744 | tf_op jit(solution)/shard_map/cond/branch_1_fun/ppermute | solution.py:488
  542.2 25.5 %collective-permute-start.160 = (bf16[2,9,32,256]{3,2,1,0:T(8,128)(2,1)S(1)}, bf16[2,9,32,256]{3,2,1,0:T(8,128)(2,1)}, u32[]{:S(2)}, u32[]{:S(2)}) collective-permute-start(bf16[2,9,32,256]{3,2,1,0:T(8,128)(2,1)S(1)} %get-tuple-element.385), channel_id=1, source_target_pairs={{0,6},{1,7},{2,0},{3,1},{4,2},{5,3},{6,4},{7,5},{8,14},{9,15},{10,... | collective-permute-start | bytes 884744 | tf_op jit(solution)/shard_map/cond/branch_1_fun/ppermute | solution.py:488
  544.7 26.1 %collective-permute-start.158 = (bf16[2,9,32,256]{3,2,1,0:T(8,128)(2,1)S(1)}, bf16[2,9,32,256]{3,2,1,0:T(8,128)(2,1)}, u32[]{:S(2)}, u32[]{:S(2)}) collective-permute-start(bf16[2,9,32,256]{3,2,1,0:T(8,128)(2,1)S(1)} %get-tuple-element.383), channel_id=1, source_target_pairs={{0,2},{1,3},{2,4},{3,5},{4,6},{5,7},{6,0},{7,1},{8,10},{9,11},{10,... | collective-permute-start | bytes 884744 | tf_op jit(solution)/shard_map/cond/branch_1_fun/ppermute | solution.py:488
  574.1 27.8 %collective-permute-start.165 = (bf16[2,2,9,64,256]{4,3,2,1,0:T(8,128)(2,1)S(1)}, bf16[2,2,9,64,256]{4,3,2,1,0:T(8,128)(2,1)}, u32[]{:S(2)}, u32[]{:S(2)}) collective-permute-start(bf16[2,2,9,64,256]{4,3,2,1,0:T(8,128)(2,1)S(1)} %copy-done.90), channel_id=1, source_target_pairs={{0,8},{8,0},{16,24},{24,16},{1,9},{9,1},{17,25},{25,17},{2,10},{10... | collective-permute-start | bytes 3538952 | tf_op jit(solution)/shard_map/cond/branch_1_fun/ppermute | solution.py:488
  575.3 27.6 %collective-permute-start.164 = (bf16[2,2,9,64,256]{4,3,2,1,0:T(8,128)(2,1)S(1)}, bf16[2,2,9,64,256]{4,3,2,1,0:T(8,128)(2,1)}, u32[]{:S(2)}, u32[]{:S(2)}) collective-permute-start(bf16[2,2,9,64,256]{4,3,2,1,0:T(8,128)(2,1)S(1)} %pad_maximum_fusion.29.refs_0_), channel_id=1, source_target_pairs={{0,16},{8,24},{16,0},{24,8},{1,17},{9,25},{17,1},{25,9},{2,18},{10... | collective-permute-start | bytes 3538952 | tf_op jit(solution)/shard_map/cond/branch_1_fun/ppermute | solution.py:488
  606.0 19.3 %collective-permute-start.168 = (bf16[2,2,9,32,256]{4,3,2,1,0:T(8,128)(2,1)}, bf16[2,2,9,32,256]{4,3,2,1,0:T(8,128)(2,1)}, u32[]{:S(2)}, u32[]{:S(2)}) collective-permute-start(bf16[2,2,9,32,256]{4,3,2,1,0:T(8,128)(2,1)} %pad_maximum_fusion.33.refs_1_), channel_id=1, source_target_pairs={{0,16},{8,24},{16,0},{24,8},{1,17},{9,25},{17,1},{25,9},{2,18},{10... | collective-permute-start | bytes 1769480 | tf_op jit(solution)/shard_map/cond/branch_1_fun/ppermute | solution.py:488
  606.8 18.5 %collective-permute-start.166 = (bf16[2,2,9,32,256]{4,3,2,1,0:T(8,128)(2,1)S(1)}, bf16[2,2,9,32,256]{4,3,2,1,0:T(8,128)(2,1)}, u32[]{:S(2)}, u32[]{:S(2)}) collective-permute-start(bf16[2,2,9,32,256]{4,3,2,1,0:T(8,128)(2,1)S(1)} %pad_maximum_fusion.32.refs_0_), channel_id=1, source_target_pairs={{0,8},{8,0},{16,24},{24,16},{1,9},{9,1},{17,25},{25,17},{2,10},{10... | collective-permute-start | bytes 1769480 | tf_op jit(solution)/shard_map/cond/branch_1_fun/ppermute | solution.py:488
  625.3 20.1 %collective-permute-start.167 = (bf16[2,2,9,32,256]{4,3,2,1,0:T(8,128)(2,1)}, bf16[2,2,9,32,256]{4,3,2,1,0:T(8,128)(2,1)}, u32[]{:S(2)}, u32[]{:S(2)}) collective-permute-start(bf16[2,2,9,32,256]{4,3,2,1,0:T(8,128)(2,1)} %pad_maximum_fusion.33.refs_1_), channel_id=1, source_target_pairs={{0,8},{8,0},{16,24},{24,16},{1,9},{9,1},{17,25},{25,17},{2,10},{10... | collective-permute-start | bytes 1769480 | tf_op jit(solution)/shard_map/cond/branch_1_fun/ppermute | solution.py:488
  626.4 16.3 %collective-permute-start.169 = (bf16[2,2,9,32,256]{4,3,2,1,0:T(8,128)(2,1)}, bf16[2,2,9,32,256]{4,3,2,1,0:T(8,128)(2,1)}, u32[]{:S(2)}, u32[]{:S(2)}) collective-permute-start(bf16[2,2,9,32,256]{4,3,2,1,0:T(8,128)(2,1)} %collective-permute-done.166.refs_2_), channel_id=1, source_target_pairs={{0,16},{8,24},{16,0},{24,8},{1,17},{9,25},{17,1},{25,9},{2,18},{10... | collective-permute-start | bytes 1769480 | tf_op jit(solution)/shard_map/cond/branch_1_fun/ppermute | solution.py:488
  (189 other events, 2124.4 us)
Sparse Core Ops, SparseCore 0:
  28.9 57.8 all-gather.23
  168.8 38.3 all-gather.19
  208.9 35.6 all-gather.21
  246.0 28.5 all-gather.17
  363.3 34.4 reduce-scatter.12
  400.6 37.4 reduce-scatter.14
  572.9 46.5 reduce-scatter.16
